TPU v7x, 32 devices: a whole 2x2x4 slice. The times are simulated.
32 devices in a mesh: dp: 8 (over y, x, core), tensor: 4 (over z).
Axes of the slice: x: 2, y: 2, z: 4, core: 2. Of those that a mesh axis runs over, the one named last changes fastest.
Arguments:
- hidden_in: bfloat16 [8192, 2048], P(('dp', 'tensor')), may hold values from -6 to 6
- segments: int32 [8192], P('dp'), may hold values from 0 to 3, as said below
- norm_gain: bfloat16 [2048], P('dp'), may hold values from 0.25 to 1.75
- mamba_in: bfloat16 [2048, 2, 3072], P('dp', None, 'tensor'), may hold values from -0.125 to 0.125
- step_weight: bfloat16 [2048, 48], P('dp', 'tensor'), may hold values from -0.125 to 0.125
- state_weight: bfloat16 [2048, 2, 256], P('dp'), may hold values from -0.03125 to 0.03125
- decay_log: float32 [48], P('tensor'), may hold values from -5.8 to -1.2
- step_bias: float32 [48], P('tensor'), may hold values from -4 to -2
- skip_gain: float32 [48], P('tensor'), may hold values from 0.5 to 2
- gated_gain: bfloat16 [3072], P('tensor'), may hold values from 0.25 to 1.75
- query_weight: bfloat16 [2048, 1024], P('dp', 'tensor'), may hold values from -0.125 to 0.125
- keyval_weight: bfloat16 [2048, 2, 256], P('dp'), may hold values from -0.125 to 0.125
- mamba_out: bfloat16 [3072, 2048], P('tensor', 'dp'), may hold values from -0.109375 to 0.109375
- attn_out: bfloat16 [1024, 2048], P('tensor', 'dp'), may hold values from -0.75 to 0.75
- ffn_gain: bfloat16 [2048], P('dp'), may hold values from 0.25 to 1.75
- gate_up: bfloat16 [2048, 2, 4096], P('dp', None, 'tensor'), may hold values from -0.125 to 0.125
- down_weight: bfloat16 [4096, 2048], P('tensor', 'dp'), may hold values from -0.09375 to 0.09375
- cotangent: bfloat16 [8192, 2048], P(('dp', 'tensor')), may hold values from -6 to 6
Outputs:
- hidden_out: bfloat16 [8192, 2048], P(('dp', 'tensor'))
- hidden_grad: float32 [8192, 2048], P(('dp', 'tensor'))
- norm_gain_grad: float32 [2048], P('dp')
- mamba_in_grad: float32 [2048, 2, 3072], P('dp', None, 'tensor')
- step_weight_grad: float32 [2048, 48], P('dp', 'tensor')
- state_weight_grad: float32 [2048, 2, 256], P('dp')
- decay_log_grad: float32 [48], P('tensor')
- step_bias_grad: float32 [48], P('tensor')
- skip_gain_grad: float32 [48], P('tensor')
- gated_gain_grad: float32 [3072], P('tensor')
- query_weight_grad: float32 [2048, 1024], P('dp', 'tensor')
- keyval_weight_grad: float32 [2048, 2, 256], P('dp')
- mamba_out_grad: float32 [3072, 2048], P('tensor', 'dp')
- attn_out_grad: float32 [1024, 2048], P('tensor', 'dp')
- ffn_gain_grad: float32 [2048], P('dp')
- gate_up_grad: float32 [2048, 2, 4096], P('dp', None, 'tensor')
- down_weight_grad: float32 [4096, 2048], P('tensor', 'dp')
Inputs may be any that keep to these rules, and one draw needn't show every extreme that they name: `segments`: within each sequence of 1024 tokens the numbers start at 0 and rise by one at each document start; every document holds one eighth of 1024 tokens or more; some sequence is a single document and some holds four.
All inputs are finite; a program needn't handle non-finite values.
Results may differ from a plain program's by a relative error of at most 0.018.
Values may be sent and summed in bfloat16 or wider, within the bound.
A program may use at most 256 MiB of HBM per device.

v0:
```python
import math

import jax
import jax.numpy as jnp
from jax import lax
from jax.sharding import PartitionSpec as P

MAMBA_HEADS = 48
HEAD_DIM = 64
ATT_HEADS = 8
KV_HEADS = 2
ATT_DIM = 128
STRETCH = 128
ATT_BLOCK = 512


EPSILON = 1e-05
PRECISE = lax.Precision.HIGHEST
ROPE_BASE = 10000.0


def rotate(values):
    half_width = values.shape[-1] // 2
    positions = jnp.arange(values.shape[0], dtype=jnp.float32)
    frequency = ROPE_BASE ** (-jnp.arange(half_width, dtype=jnp.float32) / half_width)
    angles = positions[:, None] * frequency[None, :]
    cosine = jnp.cos(angles)[:, None, :]
    sine_vals = jnp.sin(angles)[:, None, :]
    front_half = values[..., :half_width]
    back_half = values[..., half_width:]
    return jnp.concatenate(
        [front_half * cosine - back_half * sine_vals, back_half * cosine + front_half * sine_vals],
        -1,
    )


def attend(queries, keys_full, values_full, segment_ids):
    length = queries.shape[0]
    query_heads = queries.shape[1]
    head_size = queries.shape[2]
    repeat_count = query_heads // keys_full.shape[1]
    keys_full = rotate(jnp.repeat(keys_full, repeat_count, axis=1))
    values_full = jnp.repeat(values_full, repeat_count, axis=1)
    queries = rotate(queries)
    positions = jnp.arange(length, dtype=jnp.int32)

    def score_block(block_index):
        first_row = block_index * ATT_BLOCK
        query_block = lax.dynamic_slice_in_dim(queries, first_row, ATT_BLOCK, 0)
        segment_block = lax.dynamic_slice_in_dim(segment_ids, first_row, ATT_BLOCK, 0)
        place_block = first_row + jnp.arange(ATT_BLOCK, dtype=jnp.int32)
        scores = jnp.einsum("qhe,khe->hqk", query_block, keys_full, precision=PRECISE) / math.sqrt(
            head_size
        )
        allowed = (place_block[:, None] >= positions[None, :]) & (
            segment_block[:, None] == segment_ids[None, :]
        )
        scores = jnp.where(allowed[None], scores, -1e30)
        highest = jnp.max(scores, -1, keepdims=True)
        weights = jnp.exp(scores - highest)
        weights = weights / jnp.sum(weights, -1, keepdims=True)
        return jnp.einsum("hqk,khe->qhe", weights, values_full, precision=PRECISE)

    blocks = length // ATT_BLOCK
    attended = lax.map(jax.checkpoint(score_block), jnp.arange(blocks, dtype=jnp.int32))
    return attended.reshape(length, query_heads * head_size)


def stretch_step(carried, pieces):
    drive_part, keep_part, input_part, output_part, segment_part, before_id = pieces
    span = segment_part.shape[0]
    running = jnp.cumsum(keep_part, 0)
    places = jnp.arange(span, dtype=jnp.int32)
    causal = (places[:, None] >= places[None, :]) & (segment_part[:, None] == segment_part[None, :])
    spread_log = running[:, None, :] - running[None, :, :]
    decays = jnp.exp(jnp.where(causal[:, :, None], spread_log, -jnp.inf))
    scores = jnp.dot(output_part, input_part.T, precision=PRECISE)
    within = jnp.einsum("tsh,shp->thp", decays * scores[:, :, None], drive_part, precision=PRECISE)
    carry_live = (segment_part == before_id).astype(running.dtype)
    across = jnp.einsum("tn,hpn->thp", output_part, carried, precision=PRECISE)
    across = across * (jnp.exp(running) * carry_live[:, None])[:, :, None]
    final_log = running[-1]
    tail_live = (segment_part == segment_part[-1]).astype(running.dtype)
    weights = jnp.exp(final_log[None, :] - running) * tail_live[:, None]
    keep_old = jnp.exp(final_log) * (segment_part[-1] == before_id).astype(running.dtype)
    updated = carried * keep_old[:, None, None] + jnp.einsum(
        "sh,shp,sn->hpn", weights, drive_part, input_part, precision=PRECISE
    )
    return (updated, within + across)


def mixer_scan(
    drive_vals, raw_vals, input_map, output_map, decay_rates, biases, skip_vals, segment_ids
):
    length, head_count, head_width = drive_vals.shape
    stretch_count = length // STRETCH
    step_size = jax.nn.softplus(raw_vals + biases[None, :])
    log_keep = -jnp.exp(decay_rates)[None, :] * step_size
    driven = drive_vals * step_size[:, :, None]
    before = jnp.concatenate(
        [jnp.full((1,), -1, jnp.int32), segment_ids[STRETCH - 1 : length - 1 : STRETCH]]
    )
    pieces = (
        driven.reshape(stretch_count, STRETCH, head_count, head_width),
        log_keep.reshape(stretch_count, STRETCH, head_count),
        input_map.reshape(stretch_count, STRETCH, -1),
        output_map.reshape(stretch_count, STRETCH, -1),
        segment_ids.reshape(stretch_count, STRETCH),
        before,
    )
    initial = jnp.zeros((head_count, head_width, input_map.shape[1]), jnp.float32)
    last_state, stretch_outs = lax.scan(jax.checkpoint(stretch_step), initial, pieces)
    return (
        stretch_outs.reshape(length, head_count, head_width) + skip_vals[None, :, None] * drive_vals
    )


def gather_rows(pieces):
    return lax.all_gather(pieces, "tensor", axis=0, tiled=True)


def sum_rows(pieces):
    return lax.psum_scatter(pieces, "tensor", scatter_dimension=0, tiled=True)


def norm_forward(values, gain_vals):
    inverse = lax.rsqrt(jnp.mean(values * values, -1, keepdims=True) + EPSILON)
    plain = values * inverse
    return (plain, inverse, plain * gain_vals)


def norm_backward(grad_above, plain, inverse, gain_vals):
    grad_plain = grad_above * gain_vals
    grad_below = inverse * (grad_plain - plain * jnp.mean(grad_plain * plain, -1, keepdims=True))
    return (grad_below, jnp.sum(grad_above * plain, 0))


def silu_parts(gate_input):
    sigmoid_vals = jax.nn.sigmoid(gate_input)
    return (gate_input * sigmoid_vals, sigmoid_vals * (1.0 + gate_input * (1.0 - sigmoid_vals)))


def split_high(values):
    high_part = values.astype(jnp.bfloat16)
    rest_part = (values - high_part.astype(jnp.float32)).astype(jnp.bfloat16)
    return (high_part, rest_part)


def twin_product(form, plain_arg, exact_arg, first_exact):
    high_part, rest_part = split_high(exact_arg)
    if first_exact:
        return jnp.einsum(
            form, high_part, plain_arg, preferred_element_type=jnp.float32
        ) + jnp.einsum(form, rest_part, plain_arg, preferred_element_type=jnp.float32)
    return jnp.einsum(form, plain_arg, high_part, preferred_element_type=jnp.float32) + jnp.einsum(
        form, plain_arg, rest_part, preferred_element_type=jnp.float32
    )


def body(
    hidden_in,
    segments,
    norm_gain,
    mamba_in,
    step_weight,
    state_weight,
    decay_log,
    step_bias,
    skip_gain,
    gated_gain,
    query_weight,
    keyval_weight,
    mamba_out,
    attn_out,
    ffn_gain,
    gate_up,
    down_weight,
    cotangent,
):
    half_type = jnp.bfloat16
    full_type = jnp.float32
    tensor_index = lax.axis_index("tensor")
    heads_local = decay_log.shape[0]
    width_local = mamba_in.shape[2]
    qheads_local = query_weight.shape[1] // ATT_DIM
    group_size = ATT_HEADS // KV_HEADS
    kv_head = tensor_index * qheads_local // group_size
    fetched = (
        lax.all_gather(norm_gain, "dp", axis=0, tiled=True),
        lax.all_gather(mamba_in, "dp", axis=0, tiled=True),
        lax.all_gather(step_weight, "dp", axis=0, tiled=True),
        lax.all_gather(state_weight, "dp", axis=0, tiled=True),
        lax.all_gather(query_weight, "dp", axis=0, tiled=True),
        lax.all_gather(keyval_weight, "dp", axis=0, tiled=True),
        lax.all_gather(mamba_out, "dp", axis=1, tiled=True),
        lax.all_gather(attn_out, "dp", axis=1, tiled=True),
    )
    (
        gain_first,
        inner_full,
        steps_full,
        states_full,
        query_full,
        keyval_full,
        project_ssm,
        project_att,
    ) = fetched
    gain_one = gain_first.astype(full_type)
    hidden = hidden_in.astype(full_type)
    plain_one, inverse_one, scaled_one = norm_forward(hidden, gain_one)
    sequence = gather_rows(scaled_one.astype(half_type))
    length = sequence.shape[0]
    inner_vals = jnp.einsum("sd,dkc->skc", sequence, inner_full, preferred_element_type=full_type)
    raw_step = jnp.dot(sequence, steps_full, preferred_element_type=full_type)
    states_in = jnp.einsum("sd,dkn->skn", sequence, states_full, preferred_element_type=full_type)
    queries = jnp.dot(sequence, query_full, preferred_element_type=full_type)
    own_keyval = lax.dynamic_slice_in_dim(keyval_full, kv_head * ATT_DIM, ATT_DIM, 2)
    keyvals = jnp.einsum("sd,dke->ske", sequence, own_keyval, preferred_element_type=full_type)

    def mamba_local(
        gate_in, drive_vals, raw_vals, input_map, output_map, decay_rates, biases, skip_vals
    ):
        result = mixer_scan(
            drive_vals.reshape(length, heads_local, HEAD_DIM),
            raw_vals,
            input_map,
            output_map,
            decay_rates,
            biases,
            skip_vals,
            segments,
        )
        return result.reshape(length, width_local) * jax.nn.silu(gate_in)

    gated_vals, mamba_pull = jax.vjp(
        mamba_local,
        inner_vals[:, 0],
        inner_vals[:, 1],
        raw_step,
        states_in[:, 0],
        states_in[:, 1],
        decay_log,
        step_bias,
        skip_gain,
    )
    square_sum = lax.psum(jnp.sum(gated_vals * gated_vals, -1), "tensor")
    gated_inverse = lax.rsqrt(square_sum / (MAMBA_HEADS * HEAD_DIM) + EPSILON)[:, None]
    gated_plain = gated_vals * gated_inverse
    gated_scale = gated_gain.astype(full_type)
    mamba_normed = (gated_plain * gated_scale).astype(half_type)

    def attend_local(query_in, keys_in, values_in):
        return attend(
            query_in.reshape(length, qheads_local, ATT_DIM),
            keys_in[:, None, :],
            values_in[:, None, :],
            segments,
        )

    attended, attend_pull = jax.vjp(attend_local, queries, keyvals[:, 0], keyvals[:, 1])
    attended_low = attended.astype(half_type)
    partial_mix = jnp.dot(mamba_normed, project_ssm, preferred_element_type=full_type) + jnp.dot(
        attended_low, project_att, preferred_element_type=full_type
    )
    mixed_vals = sum_rows(partial_mix)
    middle = hidden + mixed_vals
    gain_second, gate_full, down_full = (
        lax.all_gather(ffn_gain, "dp", axis=0, tiled=True),
        lax.all_gather(gate_up, "dp", axis=0, tiled=True),
        lax.all_gather(down_weight, "dp", axis=1, tiled=True),
    )
    gain_two = gain_second.astype(full_type)
    plain_two, inverse_two, scaled_two = norm_forward(middle, gain_two)
    ffn_rows = gather_rows(scaled_two.astype(half_type))
    gate_vals = jnp.einsum("sd,dkf->skf", ffn_rows, gate_full, preferred_element_type=full_type)
    silu_gate, silu_slope = silu_parts(gate_vals[:, 0])
    activated = (silu_gate * gate_vals[:, 1]).astype(half_type)
    ffn_out = sum_rows(jnp.dot(activated, down_full, preferred_element_type=full_type))
    hidden_out = (middle + ffn_out).astype(half_type)
    grad_out = cotangent.astype(full_type)
    grad_rows = gather_rows(cotangent)
    grad_act = jnp.einsum("sd,fd->sf", grad_rows, down_full, preferred_element_type=full_type)
    down_grad = jnp.einsum("sf,sd->fd", activated, grad_rows, preferred_element_type=full_type)
    grad_gate = jnp.stack(
        [grad_act * gate_vals[:, 1] * silu_slope, grad_act * silu_gate], 1
    ).astype(half_type)
    gate_grad = jnp.einsum("sd,skf->dkf", ffn_rows, grad_gate, preferred_element_type=full_type)
    grad_ffn_in = sum_rows(
        jnp.einsum("skf,dkf->sd", grad_gate, gate_full, preferred_element_type=full_type)
    )
    grad_middle_norm, ffn_gain_part = norm_backward(grad_ffn_in, plain_two, inverse_two, gain_two)
    grad_middle = grad_out + grad_middle_norm
    grad_mixed = gather_rows(grad_middle.astype(half_type))
    grad_mamba = jnp.einsum("sd,cd->sc", grad_mixed, project_ssm, preferred_element_type=full_type)
    grad_attend = jnp.einsum("sd,cd->sc", grad_mixed, project_att, preferred_element_type=full_type)
    ssm_out_grad = jnp.einsum(
        "sc,sd->cd", mamba_normed, grad_mixed, preferred_element_type=full_type
    )
    att_out_grad = jnp.einsum(
        "sc,sd->cd", attended_low, grad_mixed, preferred_element_type=full_type
    )
    grad_plain = grad_mamba * gated_scale
    product_sum = lax.psum(jnp.sum(grad_plain * gated_plain, -1), "tensor")
    grad_gated = gated_inverse * (
        grad_plain - gated_plain * (product_sum / (MAMBA_HEADS * HEAD_DIM))[:, None]
    )
    gated_gain_part = jnp.sum(grad_mamba * gated_plain, 0)
    (
        grad_gating,
        grad_drive,
        grad_rawstep,
        grad_inmap,
        grad_outmap,
        grad_rates,
        grad_biases,
        grad_skips,
    ) = mamba_pull(grad_gated)
    grad_query, grad_keys, grad_values = attend_pull(grad_attend)
    grad_inner = jnp.stack([grad_gating, grad_drive], 1).astype(half_type)
    grad_raw_low = grad_rawstep.astype(half_type)
    grad_query_low = grad_query.astype(half_type)
    grad_states = jnp.stack([grad_inmap, grad_outmap], 1)
    grad_keyval = jnp.stack([grad_keys, grad_values], 1)
    inner_grad = jnp.einsum("sd,skc->dkc", sequence, grad_inner, preferred_element_type=full_type)
    step_grad = jnp.einsum("sd,sh->dh", sequence, grad_raw_low, preferred_element_type=full_type)
    query_grad = jnp.einsum("sd,se->de", sequence, grad_query_low, preferred_element_type=full_type)
    state_grad = twin_product("sd,skn->dkn", sequence, grad_states, False)
    keyval_part = twin_product("sd,ske->dke", sequence, grad_keyval, False)
    grad_normed = jnp.einsum(
        "skc,dkc->sd", grad_inner, inner_full, preferred_element_type=full_type
    )
    grad_normed = grad_normed + jnp.einsum(
        "sh,dh->sd", grad_raw_low, steps_full, preferred_element_type=full_type
    )
    grad_normed = grad_normed + jnp.einsum(
        "se,de->sd", grad_query_low, query_full, preferred_element_type=full_type
    )
    grad_normed = grad_normed + twin_product("skn,dkn->sd", states_full, grad_states, True)
    grad_normed = grad_normed + twin_product("ske,dke->sd", own_keyval, grad_keyval, True)
    grad_first = sum_rows(grad_normed)
    grad_hidden_norm, norm_gain_part = norm_backward(grad_first, plain_one, inverse_one, gain_one)
    hidden_grad = grad_middle + grad_hidden_norm
    inner_share, step_share, query_share, ssm_share, att_share, gate_share, down_share = (
        lax.psum_scatter(
            inner_grad.astype(jnp.bfloat16), "dp", scatter_dimension=0, tiled=True
        ).astype(jnp.float32),
        lax.psum_scatter(
            step_grad.astype(jnp.bfloat16), "dp", scatter_dimension=0, tiled=True
        ).astype(jnp.float32),
        lax.psum_scatter(
            query_grad.astype(jnp.bfloat16), "dp", scatter_dimension=0, tiled=True
        ).astype(jnp.float32),
        lax.psum_scatter(
            ssm_out_grad.astype(jnp.bfloat16), "dp", scatter_dimension=1, tiled=True
        ).astype(jnp.float32),
        lax.psum_scatter(
            att_out_grad.astype(jnp.bfloat16), "dp", scatter_dimension=1, tiled=True
        ).astype(jnp.float32),
        lax.psum_scatter(
            gate_grad.astype(jnp.bfloat16), "dp", scatter_dimension=0, tiled=True
        ).astype(jnp.float32),
        lax.psum_scatter(
            down_grad.astype(jnp.bfloat16), "dp", scatter_dimension=1, tiled=True
        ).astype(jnp.float32),
    )
    keyval_grad = lax.dynamic_update_slice_in_dim(
        jnp.zeros(keyval_full.shape, full_type), keyval_part, kv_head * ATT_DIM, 2
    )
    row_shares = (
        lax.psum_scatter(
            norm_gain_part.astype(jnp.bfloat16), "dp", scatter_dimension=0, tiled=True
        ).astype(jnp.float32),
        lax.psum_scatter(
            ffn_gain_part.astype(jnp.bfloat16), "dp", scatter_dimension=0, tiled=True
        ).astype(jnp.float32),
        lax.psum_scatter(
            state_grad.astype(jnp.bfloat16), "dp", scatter_dimension=0, tiled=True
        ).astype(jnp.float32),
        lax.psum_scatter(
            keyval_grad.astype(jnp.bfloat16), "dp", scatter_dimension=0, tiled=True
        ).astype(jnp.float32),
    )
    norm_gain_grad, ffn_gain_grad, state_weight_grad, keyval_weight_grad = (
        lax.psum(row_shares[0].astype(jnp.bfloat16), "tensor").astype(jnp.float32),
        lax.psum(row_shares[1].astype(jnp.bfloat16), "tensor").astype(jnp.float32),
        lax.psum(row_shares[2].astype(jnp.bfloat16), "tensor").astype(jnp.float32),
        lax.psum(row_shares[3].astype(jnp.bfloat16), "tensor").astype(jnp.float32),
    )
    decay_log_grad, step_bias_grad, skip_gain_grad, gated_gain_grad = lax.psum(
        (grad_rates, grad_biases, grad_skips, gated_gain_part), "dp"
    )
    return (
        hidden_out,
        hidden_grad,
        norm_gain_grad,
        inner_share,
        step_share,
        state_weight_grad,
        decay_log_grad,
        step_bias_grad,
        skip_gain_grad,
        gated_gain_grad,
        query_share,
        keyval_weight_grad,
        ssm_share,
        att_share,
        ffn_gain_grad,
        gate_share,
        down_share,
    )


def solution(mesh):
    return jax.shard_map(
        body,
        mesh=mesh,
        in_specs=(
            P(("dp", "tensor"), None),
            P("dp"),
            P("dp"),
            P("dp", None, "tensor"),
            P("dp", "tensor"),
            P("dp", None, None),
            P("tensor"),
            P("tensor"),
            P("tensor"),
            P("tensor"),
            P("dp", "tensor"),
            P("dp", None, None),
            P("tensor", "dp"),
            P("tensor", "dp"),
            P("dp"),
            P("dp", None, "tensor"),
            P("tensor", "dp"),
            P(("dp", "tensor"), None),
        ),
        out_specs=(
            P(("dp", "tensor"), None),
            P(("dp", "tensor"), None),
            P("dp"),
            P("dp", None, "tensor"),
            P("dp", "tensor"),
            P("dp", None, None),
            P("tensor"),
            P("tensor"),
            P("tensor"),
            P("tensor"),
            P("dp", "tensor"),
            P("dp", None, None),
            P("tensor", "dp"),
            P("tensor", "dp"),
            P("dp"),
            P("dp", None, "tensor"),
            P("tensor", "dp"),
        ),
        check_vma=False,
    )
```

profile of v0, /device:TPU:0, one launch (start us, length us, event | category | flops | bytes accessed | tf_op | source)
XLA Modules:
  0.0 2373.5 jit_solution(4669924213050585910)
XLA Ops:
  9.9 10.3 all-gather
  29.4 9.4 all_gather.47
  42.8 81.7 %all-gather.15.cloned.1.call-done = bf16[1024,2048]{1,0:T(8,128)(2,1)} async-done(((bf16[256,2048]{1,0:T(8,128)(2,1)}), bf16[1024,2048]{1,0:T(8,128)(2,1)}) %all-gather.15.cloned.1.call-update) | async-done | bytes 4194320 | tf_op jit(solution)/shard_map/all_gather | solution.py:119
  130.1 18.4 all-gather.23.cloned.1.call-done
  155.1 25.8 %while.70 = (s32[]{:T(128)}, bf16[2,512,2,128]{3,1,2,0:T(8,128)(2,1)}, s32[2]{0:T(128)S(1)}, s32[1024]{0:T(1024)S(1)}, s32[1,1024]{1,0:T(1,128)S(1)}, /*index=5*...) while((s32[]{:T(128)}, ...), condition=%wide.region_9.10_spmd.clone, body=%wide.region_6.9_spmd.clone.sunk | while | flops 3234331136 | bytes 17337020 | solution.py:65
  196.5 31.2 %all-gather.17.cloned.1.call-done = bf16[2048,2,768]{0,2,1:T(8,128)(2,1)} async-done(((bf16[256,2,768]{0,2,1:T(8,128)(2,1)}), bf16[2048,2,768]{0,2,1:T(8,128)(2,1)}) %all-gather.17.cloned.1.call-update) | async-done | bytes 6291472 | tf_op jit(solution)/shard_map/all_gather | solution.py:190
  227.8 10.1 fusion.157
  247.1 124.8 %while.71 = (s32[]{:T(128)}, f32[12,64,256]{2,1,0:T(8,128)S(1)}, f32[8,128,12,64]{1,3,2,0:T(8,128)}, f32[8,12,64,256]{3,2,1,0:T(8,128)}, f32[8,128,12]{2,1,0:T(8...) while((s32[]{:T(128)}, f32[12,64,256]{2,1,0:T(8,128)S(1)}, ...), condition=%wide.region_3.4_spmd.clone, body=%wide.region_1.3_spmd.clone.sunk | while | flops 807423488 | bytes 6703587 | solution.py:112
  379.4 11.7 psum.70
  396.5 9.8 fusion.218
  426.0 130.5 %reduce-scatter.13.cloned.1.call-done = f32[256,2048]{1,0:T(8,128)} async-done(((f32[1024,2048]{1,0:T(8,128)}), f32[256,2048]{1,0:T(8,128)}) %reduce-scatter.13.cloned.1.call-update) | async-done | bytes 2097168 | tf_op jit(solution)/shard_map/reduce_scatter | solution.py:123
  561.3 52.8 %all-gather.31.cloned.1.call-done = bf16[2048,2,1024]{2,0,1:T(8,128)(2,1)} async-done(((bf16[256,2,1024]{2,0,1:T(8,128)(2,1)}), bf16[2048,2,1024]{2,0,1:T(8,128)(2,1)}) %all-gather.31.cloned.1.call-update) | async-done | bytes 8388624 | tf_op jit(solution)/shard_map/all_gather | solution.py:269
  614.1 82.8 %all-gather.29.cloned.1.call-done = bf16[1024,2048]{1,0:T(8,128)(2,1)} async-done(((bf16[256,2048]{1,0:T(8,128)(2,1)}), bf16[1024,2048]{1,0:T(8,128)(2,1)}) %all-gather.29.cloned.1.call-update) | async-done | bytes 4194320 | tf_op jit(solution)/shard_map/all_gather | solution.py:119
  696.9 14.6 fusion.144
  711.5 66.3 %all-gather.35.cloned.1.call-done = bf16[1024,2048]{1,0:T(8,128)(2,1)} async-done(((bf16[256,2048]{1,0:T(8,128)(2,1)}), bf16[1024,2048]{1,0:T(8,128)(2,1)}) %all-gather.35.cloned.1.call-update) | async-done | bytes 4194320 | tf_op jit(solution)/shard_map/all_gather | solution.py:119
  777.8 37.7 %all-gather.33.cloned.1.call-done = bf16[1024,2048]{1,0:T(8,128)(2,1)} async-done(((bf16[1024,256]{1,0:T(8,128)(2,1)}), bf16[1024,2048]{1,0:T(8,128)(2,1)}) %all-gather.33.cloned.1.call-update) | async-done | bytes 4194320 | tf_op jit(solution)/shard_map/all_gather | solution.py:270
  815.5 13.1 fusion.186
  830.6 13.3 convolution_bitcast_fusion.5
  844.0 144.6 %reduce-scatter.17.cloned.1.call-done = f32[256,2048]{1,0:T(8,128)} async-done(((f32[1024,2048]{1,0:T(8,128)}), f32[256,2048]{1,0:T(8,128)}) %reduce-scatter.17.cloned.1.call-update) | async-done | bytes 2097168 | tf_op jit(solution)/shard_map/reduce_scatter | solution.py:123
  993.5 81.3 %all-gather.37.cloned.1.call-done = bf16[1024,2048]{1,0:T(8,128)(2,1)} async-done(((bf16[256,2048]{1,0:T(8,128)(2,1)}), bf16[1024,2048]{1,0:T(8,128)(2,1)}) %all-gather.37.cloned.1.call-update) | async-done | bytes 4194320 | tf_op jit(solution)/shard_map/all_gather | solution.py:119
  1074.8 9.8 multiply_reduce_fusion.4
  1108.7 300.0 %while.72 = (s32[]{:T(128)}, f32[12,64,256]{2,1,0:T(8,128)S(1)}, f32[8,128,12,64]{1,0,3,2:T(8,128)}, f32[8,128,12]{2,1,0:T(8,128)}, f32[8,128,256]{2,1,0:T(8,128...) while((s32[]{:T(128)}, f32[12,64,256]{2,1,0:T(8,128)S(1)}, ...), condition=%wide.region_26.27_spmd.clone, body=%wide.region_17.26_spmd.clone.sunk | while | flops 1967670272 | bytes 19261676 | solution.py:112
  1133.0 11.0 dynamic_update_slice.93
  1170.5 11.0 dynamic_update_slice.93
  1207.9 11.0 dynamic_update_slice.93
  1245.4 11.0 dynamic_update_slice.93
  1282.8 11.0 dynamic_update_slice.93
  1320.3 11.0 dynamic_update_slice.93
  1357.7 11.0 dynamic_update_slice.93
  1395.1 11.0 dynamic_update_slice.93
  1417.4 121.2 %while.73 = (s32[]{:T(128)}, f32[1024,2,128]{0,2,1:T(8,128)}, f32[1024,2,128]{2,0,1:T(8,128)}, f32[1024,2,128]{0,2,1:T(8,128)}, s32[2]{0:T(128)S(1)}, /*index=5*...) while((s32[]{:T(128)}, f32[1024,2,128]{0,2,1:T(8,128)}, ...), condition=%wide.region_34.35_spmd.clone, body=%wide.region_28.34_spmd.clone.sunk | while | flops 8092516864 | bytes 143243824 | solution.py:65
  1551.1 9.5 copy_dynamic-update-slice_fusion
  1581.2 13.8 convolution_convert_fusion
  1624.4 41.7 %reduce-scatter.25.cloned.1.call-done = bf16[256,2,256]{2,0,1:T(8,128)(2,1)} async-done(((bf16[2048,2,256]{2,0,1:T(8,128)(2,1)}), bf16[256,2,256]{2,0,1:T(8,128)(2,1)}) %reduce-scatter.25.cloned.1.call-update) | async-done | bytes 262160 | tf_op jit(solution)/shard_map/reduce_scatter | solution.py:376
  1715.3 9.3 fusion.187
  1724.6 23.9 %fusion.140 = f32[1024,2048]{1,0:T(8,128)} fusion(f32[1024,2048,1]{1,0,2:T(8,128)} %fusion.202, f32[1024,2048,1]{1,0,2:T(8,128)} %fusion.219, f32[1024,2048,1]{1,0,2:T(8,128)} %fusion.197, f32[1024,2048]{1,0:T(8,128)} %fusion.233, f32[1024,2048]{1,0:T(8,128)} %fusion.208, f32[1024,2048,1]{1,0,2:T(8,128)} %fusion.187, ...), kind=kOutput, calls=%fused_computation.192 | convolution fusion | flops 1087635456 | bytes 60817408 | tf_op jit(solution)/shard_map/ske,dke->sd/dot_general | solution.py:154
  1761.7 33.9 %reduce-scatter.33.cloned.1.call-done = bf16[256,2,1024]{2,0,1:T(8,128)(2,1)} async-done(((bf16[2048,2,1024]{2,0,1:T(8,128)(2,1)}), bf16[256,2,1024]{2,0,1:T(8,128)(2,1)}) %reduce-scatter.33.cloned.1.call-update) | async-done | bytes 1048592 | tf_op jit(solution)/shard_map/reduce_scatter | solution.py:359
  1799.5 13.7 all-reduce.8
  1813.2 17.8 reduce-scatter.23.cloned.1.call-done
  1832.3 37.8 %reduce-scatter.31.cloned.1.call-done = bf16[256,256]{1,0:T(8,128)(2,1)} async-done(((bf16[256,2048]{1,0:T(8,128)(2,1)}), bf16[256,256]{1,0:T(8,128)(2,1)}) %reduce-scatter.31.cloned.1.call-update) | async-done | bytes 131088 | tf_op jit(solution)/shard_map/reduce_scatter | solution.py:356
  1871.7 38.2 %reduce-scatter.27.cloned.1.call-done = bf16[256,256]{1,0:T(8,128)(2,1)} async-done(((bf16[2048,256]{1,0:T(8,128)(2,1)}), bf16[256,256]{1,0:T(8,128)(2,1)}) %reduce-scatter.27.cloned.1.call-update) | async-done | bytes 131088 | tf_op jit(solution)/shard_map/reduce_scatter | solution.py:350
  1911.5 39.9 %all-reduce.17.cloned.1.call-done = (bf16[256,2,256]{2,0,1:T(8,128)(2,1)}, bf16[256,2,256]{2,1,0:T(2,128)(2,1)}) async-done(((bf16[256,2,256]{2,0,1:T(8,128)(2,1)}, bf16[256,2,256]{2,1,0:T(2,128)(2,1)}), (bf16[256,2,256]{2,0,1:T(8,128)(2,1)}, bf16[256,2,256]{2,1,0:T(2,128)(2,1)})) %all-reduce.17.cloned.1.call-update) | async-done | bytes 524304 | tf_op jit(solution)/shard_map/psum | solution.py:386
  1955.3 45.6 %reduce-scatter.29.cloned.1.call-done = bf16[768,256]{1,0:T(8,128)(2,1)} async-done(((bf16[768,2048]{1,0:T(8,128)(2,1)}), bf16[768,256]{1,0:T(8,128)(2,1)}) %reduce-scatter.29.cloned.1.call-update) | async-done | bytes 393232 | tf_op jit(solution)/shard_map/reduce_scatter | solution.py:353
  2002.8 63.4 %reduce-scatter.21.cloned.1.call-done = bf16[256,2,768]{2,0,1:T(8,128)(2,1)} async-done(((bf16[2048,2,768]{2,0,1:T(8,128)(2,1)}), bf16[256,2,768]{2,0,1:T(8,128)(2,1)}) %reduce-scatter.21.cloned.1.call-update) | async-done | bytes 786448 | tf_op jit(solution)/shard_map/reduce_scatter | solution.py:344
  2069.4 143.8 %reduce-scatter.19.cloned.1.call-done = f32[256,2048]{1,0:T(8,128)} async-done(((f32[1024,2048]{1,0:T(8,128)}), f32[256,2048]{1,0:T(8,128)}) %reduce-scatter.19.cloned.1.call-update) | async-done | bytes 2097168 | tf_op jit(solution)/shard_map/reduce_scatter | solution.py:123
  2215.4 13.7 all-reduce.9
  2229.3 11.8 all-reduce.10
  2242.3 118.5 %reduce-scatter.15.cloned.1.call-done = f32[256,2048]{1,0:T(8,128)} async-done(((f32[1024,2048]{1,0:T(8,128)}), f32[256,2048]{1,0:T(8,128)}) %reduce-scatter.15.cloned.1.call-update) | async-done | bytes 2097168 | tf_op jit(solution)/shard_map/reduce_scatter | solution.py:123
  (978 shorter events, 711.9 us)
Async XLA Ops:
  7.2 34.3 %all-gather.25.cloned.1.call-start = ((), (), s32[]{:S(2)}) async-start(), calls=%async_computation.17 | async-start | bytes 2359296 | tf_op jit(solution)/shard_map/all_gather | solution.py:194
  9.2 115.4 %all-gather.15.cloned.1.call-start = ((), (), s32[]{:S(2)}) async-start(), calls=%async_computation.12 | async-start | bytes 5242880 | tf_op jit(solution)/shard_map/all_gather | solution.py:119
  24.4 124.1 %all-gather.23.cloned.1.call-start = ((), (), s32[]{:S(2)}) async-start(), calls=%async_computation.16 | async-start | bytes 1179648 | tf_op jit(solution)/shard_map/all_gather | solution.py:193
  25.1 164.6 %all-gather.19.cloned.1.call-start = ((), (), s32[]{:S(2)}) async-start(), calls=%async_computation.14 | async-start | bytes 2359296 | tf_op jit(solution)/shard_map/all_gather | solution.py:192
  25.9 201.8 %all-gather.17.cloned.1.call-start = ((), (), s32[]{:S(2)}) async-start(), calls=%async_computation.13 | async-start | bytes 7077888 | tf_op jit(solution)/shard_map/all_gather | solution.py:190
  28.0 368.5 %all-gather.21.cloned.1.call-start = ((), (), s32[]{:S(2)}) async-start(), calls=%async_computation.15 | async-start | bytes 3538944 | tf_op jit(solution)/shard_map/all_gather | solution.py:195
  28.5 377.7 %all-gather.27.cloned.1.call-start = ((), (), s32[]{:S(2)}) async-start(), calls=%async_computation.18 | async-start | bytes 1179648 | tf_op jit(solution)/shard_map/all_gather | solution.py:196
  29.3 527.2 %reduce-scatter.13.cloned.1.call-start = ((), (), s32[]{:S(2)}) async-start(), calls=%async_computation.19 | async-start | bytes 10485760 | tf_op jit(solution)/shard_map/reduce_scatter | solution.py:123
  38.8 144.9 %copy-start.65 = (bf16[2048,12]{0,1:T(8,128)(2,1)}, bf16[2048,12]{0,1:T(8,128)(2,1)S(1)}, u32[]{:S(2)}) copy-start(bf16[2048,12]{0,1:T(8,128)(2,1)S(1)} %all_gather.47) | copy-start | bytes 147460
  39.6 1054.0 %copy-start.74 = (f32[768]{0:T(1024)}, f32[768]{0:T(1024)S(1)}, u32[]{:S(2)}) copy-start(f32[768]{0:T(1024)S(1)} %mul.927) | copy-start | bytes 9220
  42.8 85.2 %copy-start.34 = (bf16[2048,2,128]{0,2,1:T(8,128)(2,1)}, bf16[2048,2,128]{0,2,1:T(8,128)(2,1)S(1)}, u32[]{:S(2)}) copy-start(bf16[2048,2,128]{0,2,1:T(8,128)(2,1)S(1)} %constant_dynamic-slice_fusion.6) | copy-start | bytes 3145732
  414.6 141.9 %copy-start.21 = (bf16[256,2048]{1,0:T(8,128)(2,1)S(1)}, bf16[256,2048]{1,0:T(8,128)(2,1)}, u32[]{:S(2)}) copy-start(bf16[256,2048]{1,0:T(8,128)(2,1)} %param.26) | copy-start | bytes 3145732
  414.6 199.5 %all-gather.31.cloned.1.call-start = ((), (), s32[]{:S(2)}) async-start(), calls=%async_computation.21 | async-start | bytes 9437184 | tf_op jit(solution)/shard_map/all_gather | solution.py:269
  417.1 279.8 %all-gather.29.cloned.1.call-start = ((), (), s32[]{:S(2)}) async-start(), calls=%async_computation.20 | async-start | bytes 5242880 | tf_op jit(solution)/shard_map/all_gather | solution.py:119
  426.0 565.5 %copy-start.69 = (f32[8,1,256]{2,1,0:T(1,128)}, f32[8,1,256]{2,1,0:T(1,128)S(1)}, u32[]{:S(2)}) copy-start(f32[8,1,256]{2,1,0:T(1,128)S(1)} %convert_element_type.252) | copy-start | bytes 24580
  558.4 433.1 %copy-start.6 = (f32[256,2048]{1,0:T(8,128)}, f32[256,2048]{1,0:T(8,128)S(1)}, u32[]{:S(2)}) copy-start(f32[256,2048]{1,0:T(8,128)S(1)} %get-tuple-element.1227) | copy-start | bytes 6291460
  558.4 433.0 %copy-start.77 = (f32[256]{0:T(256)}, f32[256]{0:T(256)S(1)}, u32[]{:S(2)}) copy-start(f32[256]{0:T(256)S(1)} %add_rsqrt_fusion.1) | copy-start | bytes 3076
  559.9 217.9 %all-gather.35.cloned.1.call-start = ((), (), s32[]{:S(2)}) async-start(), calls=%async_computation.24 | async-start | bytes 5242880 | tf_op jit(solution)/shard_map/all_gather | solution.py:119
  560.6 254.9 %all-gather.33.cloned.1.call-start = ((), (), s32[]{:S(2)}) async-start(), calls=%async_computation.22 | async-start | bytes 4718592 | tf_op jit(solution)/shard_map/all_gather | solution.py:270
  561.2 427.4 %reduce-scatter.17.cloned.1.call-start = ((), (), s32[]{:S(2)}) async-start(), calls=%async_computation.25 | async-start | bytes 10485760 | tf_op jit(solution)/shard_map/reduce_scatter | solution.py:123
  844.0 147.5 %copy-start.33 = (bf16[256,2048]{1,0:T(8,128)(2,1)S(1)}, bf16[256,2048]{1,0:T(8,128)(2,1)}, u32[]{:S(2)}) copy-start(bf16[256,2048]{1,0:T(8,128)(2,1)} %param.43) | copy-start | bytes 3145732
  844.0 230.8 %all-gather.37.cloned.1.call-start = ((), (), s32[]{:S(2)}) async-start(), calls=%async_computation.26 | async-start | bytes 5242880 | tf_op jit(solution)/shard_map/all_gather | solution.py:119
  993.2 629.4 %all-reduce.15.cloned.1.call-start = ((), (), s32[]{:S(2)}) async-start(), calls=%async_computation.36 | async-start | bytes 4194304
  993.5 100.1 %copy-start.13 = (f32[8,128,12,64]{1,0,3,2:T(8,128)S(1)}, f32[8,128,12,64]{1,0,3,2:T(8,128)}, u32[]{:S(2)}) copy-start(f32[8,128,12,64]{1,0,3,2:T(8,128)} %copy-done.12) | copy-start | bytes 9437188
  1417.4 122.7 %copy-start.43 = (f32[1024,64]{0,1:T(8,128)S(1)}, f32[1024,64]{0,1:T(8,128)}, u32[]{:S(2)}) copy-start(f32[1024,64]{0,1:T(8,128)} %copy-done.42) | copy-start | bytes 786436
  1561.9 104.2 %reduce-scatter.25.cloned.1.call-start = ((), (), s32[]{:S(2)}) async-start(), calls=%async_computation.30 | async-start | bytes 2359296 | tf_op jit(solution)/shard_map/reduce_scatter | solution.py:376
  1571.1 188.6 %reduce-scatter.35.cloned.1.call-start = ((), (), s32[]{:S(2)}) async-start(), calls=%async_computation.35 | async-start | bytes 4718592 | tf_op jit(solution)/shard_map/reduce_scatter | solution.py:362
  1579.6 216.1 %reduce-scatter.33.cloned.1.call-start = ((), (), s32[]{:S(2)}) async-start(), calls=%async_computation.34 | async-start | bytes 9437184 | tf_op jit(solution)/shard_map/reduce_scatter | solution.py:359
  1595.0 236.0 %reduce-scatter.23.cloned.1.call-start = ((), (), s32[]{:S(2)}) async-start(), calls=%async_computation.29 | async-start | bytes 73728 | tf_op jit(solution)/shard_map/reduce_scatter | solution.py:347
  1605.9 264.2 %reduce-scatter.31.cloned.1.call-start = ((), (), s32[]{:S(2)}) async-start(), calls=%async_computation.33 | async-start | bytes 1179648 | tf_op jit(solution)/shard_map/reduce_scatter | solution.py:356
  1610.4 299.4 %reduce-scatter.27.cloned.1.call-start = ((), (), s32[]{:S(2)}) async-start(), calls=%async_computation.31 | async-start | bytes 1179648 | tf_op jit(solution)/shard_map/reduce_scatter | solution.py:350
  1610.5 55.7 %copy-start.31 = (f32[1024,768]{0,1:T(8,128)S(1)}, f32[1024,768]{0,1:T(8,128)}, u32[]{:S(2)}) copy-start(f32[1024,768]{0,1:T(8,128)} %multiply_multiply_fusion.1) | copy-start | bytes 9437188
  1610.5 55.7 %copy-start.83 = (f32[768]{0:T(1024)S(1)}, f32[768]{0:T(1024)}, u32[]{:S(2)}) copy-start(f32[768]{0:T(1024)} %convert_element_type.210) | copy-start | bytes 9220
  1615.5 335.9 %all-reduce.17.cloned.1.call-start = ((), (), s32[]{:S(2)}) async-start(), calls=%async_computation.37 | async-start | bytes 1048576 | tf_op jit(solution)/shard_map/psum | solution.py:386
  1666.1 334.8 %reduce-scatter.29.cloned.1.call-start = ((), (), s32[]{:S(2)}) async-start(), calls=%async_computation.32 | async-start | bytes 3538944 | tf_op jit(solution)/shard_map/reduce_scatter | solution.py:353
  1673.4 392.9 %reduce-scatter.21.cloned.1.call-start = ((), (), s32[]{:S(2)}) async-start(), calls=%async_computation.28 | async-start | bytes 7077888 | tf_op jit(solution)/shard_map/reduce_scatter | solution.py:344
  1689.4 523.8 %reduce-scatter.19.cloned.1.call-start = ((), (), s32[]{:S(2)}) async-start(), calls=%async_computation.27 | async-start | bytes 10485760 | tf_op jit(solution)/shard_map/reduce_scatter | solution.py:123
  1748.6 612.2 %reduce-scatter.15.cloned.1.call-start = ((), (), s32[]{:S(2)}) async-start(), calls=%async_computation.23 | async-start | bytes 10485760 | tf_op jit(solution)/shard_map/reduce_scatter | solution.py:123
  1759.6 39.9 %copy-start.96 = (f32[12]{0:T(128)S(1)}, f32[12]{0:T(128)}, u32[]{:S(2)}) copy-start(f32[12]{0:T(128)} %param.32) | copy-start | bytes 148
  1759.6 39.9 %copy-start.89 = (f32[768]{0:T(1024)S(1)}, f32[768]{0:T(1024)}, u32[]{:S(2)}) copy-start(f32[768]{0:T(1024)} %get-tuple-element.1116) | copy-start | bytes 9220
  1799.3 413.8 %copy-start.22 = (bf16[256,2048]{1,0:T(8,128)(2,1)S(1)}, bf16[256,2048]{1,0:T(8,128)(2,1)}, u32[]{:S(2)}) copy-start(bf16[256,2048]{1,0:T(8,128)(2,1)} %param.26) | copy-start | bytes 3145732
  1799.3 413.8 %copy-start.72 = (f32[8,1,256]{2,1,0:T(1,128)S(1)}, f32[8,1,256]{2,1,0:T(1,128)}, u32[]{:S(2)}) copy-start(f32[8,1,256]{2,1,0:T(1,128)} %copy-done.71) | copy-start | bytes 24580
  1799.3 413.8 %copy-start.80 = (f32[256]{0:T(256)S(1)}, f32[256]{0:T(256)}, u32[]{:S(2)}) copy-start(f32[256]{0:T(256)} %copy-done.79) | copy-start | bytes 3076
  1955.3 260.1 %copy-start.84 = (bf16[2048]{0:T(1024)(128)(2,1)S(1)}, bf16[2048]{0:T(1024)(128)(2,1)}, u32[]{:S(2)}) copy-start(bf16[2048]{0:T(1024)(128)(2,1)} %get-tuple-element.1118) | copy-start | bytes 12292
  1955.3 405.5 %copy-start.7 = (f32[256,2048]{1,0:T(8,128)S(1)}, f32[256,2048]{1,0:T(8,128)}, u32[]{:S(2)}) copy-start(f32[256,2048]{1,0:T(8,128)} %copy-done.6) | copy-start | bytes 6291460
  1955.3 405.5 %copy-start.70 = (f32[8,1,256]{2,1,0:T(1,128)S(1)}, f32[8,1,256]{2,1,0:T(1,128)}, u32[]{:S(2)}) copy-start(f32[8,1,256]{2,1,0:T(1,128)} %copy-done.69) | copy-start | bytes 24580
  1955.3 405.5 %copy-start.78 = (f32[256]{0:T(256)S(1)}, f32[256]{0:T(256)}, u32[]{:S(2)}) copy-start(f32[256]{0:T(256)} %copy-done.77) | copy-start | bytes 3076
  1955.3 405.5 %copy-start.86 = (f32[256]{0:T(256)S(1)}, f32[256]{0:T(256)}, u32[]{:S(2)}) copy-start(f32[256]{0:T(256)} %copy-done.85) | copy-start | bytes 3076
  (122 other events, 715.6 us)
Sparse Core Ops, SparseCore 0:
  10.5 30.9 all-gather.24
  43.7 80.8 all-gather.14
  126.4 22.0 all-gather.22
  150.8 27.9 all-gather.18
  181.1 46.6 all-gather.16
  229.5 32.8 all-gather.20
  264.2 23.5 all-gather.26
  414.7 141.7 reduce-scatter.12
  559.0 55.1 all-gather.30
  616.1 80.7 all-gather.28
  698.5 79.2 all-gather.34
  779.5 35.9 all-gather.32
  844.1 144.4 reduce-scatter.16
  993.3 81.4 all-gather.36
  1562.1 60.4 all-reduce.14
  1625.7 40.3 reduce-scatter.24
  1669.7 51.3 reduce-scatter.34
  1724.4 71.2 reduce-scatter.32
  1799.5 31.4 reduce-scatter.22
  1834.0 36.0 reduce-scatter.30
  1873.8 35.9 reduce-scatter.26
  1912.8 38.4 all-reduce.16
  1954.7 46.1 reduce-scatter.28
  2004.5 61.7 reduce-scatter.20
  2068.6 144.4 reduce-scatter.18
  2215.4 145.4 reduce-scatter.14
where the time goes:
time: 2390 us; the launch traced here: 2370 us
  waiting for transfers between devices  1320 us (55%)
  matrix products  458 us (19%)
  local copies, waits for them, and re-layouts  302 us (13%)
  other arithmetic  137 us (6%)
  blocking collectives  88.5 us (4%)
  loops' own time  51.8 us (2%)
    reduce_scatter x4, waiting for transfers between devices, sum_rows(): return lax.psum_scatter(pieces, 'tensor', scatter_dimension=0, tiled=True)  537 us
    all_gather x4, waiting for transfers between devices, gather_rows(): return lax.all_gather(pieces, 'tensor', axis=0, tiled=True)  312 us
    dynamic_update_slice x16, local copies, waits for them, and re-layouts, mixer_scan(): lax.scan(jax.checkpoint(stretch_step), initial, pieces)  92.8 us
    reduce_scatter x1, waiting for transfers between devices, body(): lax.psum_scatter(inner_grad.astype(jnp.bfloat16), 'dp', scatter_dimension...  63.4 us
    all_gather x1, waiting for transfers between devices, body(): lax.all_gather(gate_up, 'dp', axis=0, tiled=True)  52.8 us
    dot_general x24, matrix products, stretch_step(): jnp.einsum('tsh,shp->thp', decays * scores[:, :, None], drive_part, preci...  49.6 us
    dot_general x8, matrix products, score_block(): jnp.einsum('qhe,khe->hqk', query_block, keys_full, precision=PRECISE)  49.3 us
  transfers between devices with their start and end apart: 26, of which 22 were waited for; matrix products, arithmetic and copies ran while one was open for 17% of the time, Pallas kernels for 0%

commit v1 on v0

v1 whole, which is shorter than its diff:
```python
import functools
import math
import jax
import jax.numpy as jnp
from jax import lax
from jax.experimental import pallas as pl
from jax.experimental.pallas import tpu as pltpu
from jax.sharding import PartitionSpec as P

MAMBA_HEADS = 48
HEAD_DIM = 64
ATT_HEADS = 8
KV_HEADS = 2
ATT_DIM = 128
STRETCH = 128
ATT_BLOCK = 256
EPSILON = 1e-05
PRECISE = lax.Precision.HIGHEST
ROPE_BASE = 10000.0
LANES = 128
MASKED = -1e30
HALF = jnp.bfloat16
FULL = jnp.float32


def mm(a, b):
    return jnp.dot(a, b, preferred_element_type=FULL)


def mm_nt(a, b):
    return lax.dot_general(a, b, (((1,), (1,)), ((), ())), preferred_element_type=FULL)


def mm_tn(a, b):
    return lax.dot_general(a, b, (((0,), (0,)), ((), ())), preferred_element_type=FULL)


def softplus(v):
    return jnp.maximum(v, 0.0) + jnp.log1p(jnp.exp(-jnp.abs(v)))


def sigmoid(v):
    return 1.0 / (1.0 + jnp.exp(-v))


def iota(shape, dim):
    return lax.broadcasted_iota(jnp.int32, shape, dim)


def halves(left, right, size):
    return jnp.where(iota((size, LANES), 1) < HEAD_DIM, left, right)


def stacked_pair(pair):
    low = iota(pair.shape, 1) < HEAD_DIM
    zero = jnp.zeros_like(pair)
    return jnp.concatenate([jnp.where(low, pair, zero), jnp.where(low, zero, pair)], 0)


class Columns:
    def __init__(self, query, width, state):
        self.query = (0, query)
        self.key = (query, query + ATT_DIM)
        self.value = (query + ATT_DIM, query + 2 * ATT_DIM)
        start = query + 2 * ATT_DIM
        self.attention = start
        self.gate = (start, start + width)
        self.drive = (start + width, start + 2 * width)
        start += 2 * width
        self.inmap = (start, start + state)
        self.outmap = (start + state, start + 2 * state)
        start += 2 * state
        self.step = (start, start + LANES)
        self.total = start + LANES


def stretch_common(col, packed, segc_ref, segr_ref, head_ref, before):
    span = STRETCH
    raw = packed[:, col.step[0] : col.step[1]] + head_ref[1:2, :]
    step = softplus(raw)
    keep = -jnp.exp(head_ref[0:1, :]) * step
    row, column = iota((span, span), 0), iota((span, span), 1)
    running = jnp.dot(
        (row >= column).astype(FULL), keep, precision=PRECISE, preferred_element_type=FULL
    )
    segc, segr = segc_ref[...], segr_ref[0]
    causal = (row >= column) & (segc == segr)
    blocked = jnp.where(causal, 0.0, MASKED)
    live = (segc == before).astype(FULL)
    last = segc[span - 1 : span, :]
    tail = (segc == last).astype(FULL)
    old = (last == before).astype(FULL)
    return raw, step, keep, running, running.T, blocked, live, tail, old


def pair_decay(pair, running, running_t, blocked, live, tail, old):
    span = STRETCH
    a, b = 2 * pair, 2 * pair + 1
    col_a = jnp.broadcast_to(running[:, a : a + 1], (span, LANES))
    col_b = jnp.broadcast_to(running[:, b : b + 1], (span, LANES))
    decay_a = jnp.exp(col_a - running_t[a : a + 1, :] + blocked)
    decay_b = jnp.exp(col_b - running_t[b : b + 1, :] + blocked)
    both = halves(col_a, col_b, span)
    last = both[span - 1 : span, :]
    into = jnp.exp(both) * live
    weight = jnp.exp(last - both) * tail
    keep_old = jnp.exp(last) * old
    return decay_a, decay_b, into, weight, keep_old


def scan_forward_kernel(col, heads, p_ref, segc_ref, segr_ref, head_ref, y_ref, states_ref, gated_ref, square_ref, state, before):
    index = pl.program_id(0)
    span = STRETCH

    @pl.when(index == 0)
    def _():
        state[...] = jnp.zeros_like(state)
        before[...] = jnp.full_like(before, -1)

    raw, step, keep, running, running_t, blocked, live, tail, old = stretch_common(
        col, p_ref, segc_ref, segr_ref, head_ref, before[...]
    )
    inmap = p_ref[:, col.inmap[0] : col.inmap[1]].astype(HALF)
    outmap = p_ref[:, col.outmap[0] : col.outmap[1]].astype(HALF)
    inmap_t = inmap.T
    scores = mm_nt(outmap, inmap)
    square = jnp.zeros((span, 1), FULL)
    for pair in range(heads // 2):
        at = pair * LANES
        lanes = slice(at, at + LANES)
        decay_a, decay_b, into, weight, keep_old = pair_decay(
            pair, running, running_t, blocked, live, tail, old
        )
        drive = p_ref[:, col.drive[0] + at : col.drive[0] + at + LANES]
        gate = p_ref[:, col.gate[0] + at : col.gate[0] + at + LANES]
        driven = drive * halves(step[:, 2 * pair : 2 * pair + 1], step[:, 2 * pair + 1 : 2 * pair + 2], span)
        driven_low = driven.astype(HALF)
        mix = jnp.concatenate([(decay_a * scores).astype(HALF), (decay_b * scores).astype(HALF)], 1)
        held = state[:, lanes]
        held_low = held.astype(HALF)
        states_ref[0, :, lanes] = held_low
        result = mm(mix, stacked_pair(driven_low)) + mm(outmap, held_low) * into
        state[:, lanes] = held * keep_old + mm(inmap_t, (driven_low.astype(FULL) * weight).astype(HALF))
        y_ref[:, lanes] = result
        skip = halves(head_ref[2:3, 2 * pair : 2 * pair + 1], head_ref[2:3, 2 * pair + 1 : 2 * pair + 2], 1)
        gated = (result + skip * drive) * (gate * sigmoid(gate))
        gated_ref[:, lanes] = gated
        square = square + jnp.sum(gated * gated, 1, keepdims=True)
    square_ref[...] = jnp.broadcast_to(square, square_ref.shape)
    before[...] = segc_ref[span - 1 : span, :]


def scan_forward(col, heads, state_size, packed, segments, head_params):
    length = packed.shape[0]
    width = heads * HEAD_DIM
    count = length // STRETCH
    return pl.pallas_call(
        functools.partial(scan_forward_kernel, col, heads),
        grid=(count,),
        in_specs=[
            pl.BlockSpec((STRETCH, col.total), lambda i: (i, 0)),
            pl.BlockSpec((STRETCH, 1), lambda i: (i, 0)),
            pl.BlockSpec((1, 1, STRETCH), lambda i: (i, 0, 0)),
            pl.BlockSpec((8, LANES), lambda i: (0, 0)),
        ],
        out_specs=[
            pl.BlockSpec((STRETCH, width), lambda i: (i, 0)),
            pl.BlockSpec((1, state_size, width), lambda i: (i, 0, 0)),
            pl.BlockSpec((STRETCH, width), lambda i: (i, 0)),
            pl.BlockSpec((STRETCH, LANES), lambda i: (i, 0)),
        ],
        out_shape=[
            jax.ShapeDtypeStruct((length, width), FULL),
            jax.ShapeDtypeStruct((count, state_size, width), HALF),
            jax.ShapeDtypeStruct((length, width), FULL),
            jax.ShapeDtypeStruct((length, LANES), FULL),
        ],
        scratch_shapes=[pltpu.VMEM((state_size, width), FULL), pltpu.VMEM((1, 1), jnp.int32)],
        cost_estimate=pl.CostEstimate(flops=6_000_000_000, bytes_accessed=30_000_000, transcendentals=0),
        compiler_params=pltpu.CompilerParams(vmem_limit_bytes=48 * 2**20),
    )(packed, segments[:, None], segments.reshape(count, 1, STRETCH), head_params)


def scan_backward_kernel(
    col, heads, total_width, p_ref, y_ref, states_ref, gm_ref, inv_ref, prod_ref, gain_ref,
    segc_ref, segr_ref, segb_ref, head_ref, g_ref, gain_grad_ref, skip_grad_ref, head_grad_ref, future,
):
    step_index = pl.program_id(0)
    count = pl.num_programs(0)
    span = STRETCH

    @pl.when(step_index == 0)
    def _():
        future[...] = jnp.zeros_like(future)
        gain_grad_ref[...] = jnp.zeros_like(gain_grad_ref)
        skip_grad_ref[...] = jnp.zeros_like(skip_grad_ref)
        head_grad_ref[...] = jnp.zeros_like(head_grad_ref)

    before = jnp.where(step_index == count - 1, -1, segb_ref[span - 1 : span, :])
    raw, step, keep, running, running_t, blocked, live, tail, old = stretch_common(
        col, p_ref, segc_ref, segr_ref, head_ref, before
    )
    inmap = p_ref[:, col.inmap[0] : col.inmap[1]].astype(HALF)
    outmap = p_ref[:, col.outmap[0] : col.outmap[1]].astype(HALF)
    outmap_t = outmap.T
    scores = mm_nt(outmap, inmap)
    lane = iota((span, LANES), 1)
    head_lane = iota((1, LANES), 1)
    paired = jnp.zeros((span, span), FULL)
    grad_in = jnp.zeros(inmap.shape, FULL)
    grad_out = jnp.zeros(outmap.shape, FULL)
    grad_running = jnp.zeros((span, LANES), FULL)
    grad_step = jnp.zeros((span, LANES), FULL)
    grad_last = jnp.zeros((1, LANES), FULL)
    inverse, product = inv_ref[:, 0:1], prod_ref[:, 0:1] * (1.0 / total_width)
    for pair in range(heads // 2):
        at = pair * LANES
        lanes = slice(at, at + LANES)
        a, b = 2 * pair, 2 * pair + 1
        decay_a, decay_b, into, weight, keep_old = pair_decay(
            pair, running, running_t, blocked, live, tail, old
        )
        drive = p_ref[:, col.drive[0] + at : col.drive[0] + at + LANES]
        gate = p_ref[:, col.gate[0] + at : col.gate[0] + at + LANES]
        result = y_ref[:, lanes]
        skip = halves(head_ref[2:3, a : a + 1], head_ref[2:3, b : b + 1], 1)
        sig = sigmoid(gate)
        silu = gate * sig
        ssm = result + skip * drive
        plain = ssm * silu * inverse
        grad_above = gm_ref[:, lanes].astype(FULL)
        gain_grad_ref[:, lanes] += jnp.sum(grad_above * plain, 0, keepdims=True)
        grad_gated = inverse * (grad_above * gain_ref[:, lanes] - plain * product)
        g_ref[:, col.gate[0] + at : col.gate[0] + at + LANES] = (
            grad_gated * ssm * (sig * (1.0 + gate * (1.0 - sig)))
        ).astype(HALF)
        grad_y = grad_gated * silu
        grad_y_low = grad_y.astype(HALF)
        grad_y = grad_y_low.astype(FULL)
        step_pair = halves(step[:, a : a + 1], step[:, b : b + 1], span)
        driven_low = (drive * step_pair).astype(HALF)
        driven = driven_low.astype(FULL)
        grad_rows = stacked_pair(grad_y_low)
        inner = mm_nt(grad_rows, driven_low)
        paired = paired + decay_a * inner[:span] + decay_b * inner[span:]
        mix = jnp.concatenate([(decay_a * scores).astype(HALF), (decay_b * scores).astype(HALF)], 0)
        later = future[:, lanes]
        later_low = later.astype(HALF)
        held_low = states_ref[0, :, lanes]
        reach = mm(inmap, later_low) * weight
        grad_driven = mm_tn(mix, grad_rows) + reach
        weighted = (driven * weight).astype(HALF)
        spread = (grad_y * into).astype(HALF)
        grad_in = grad_in + mm_nt(weighted, later_low)
        grad_out = grad_out + mm_nt(spread, held_low)
        future[:, lanes] = later * keep_old + mm(outmap_t, spread)
        g_ref[:, col.drive[0] + at : col.drive[0] + at + LANES] = (
            step_pair * grad_driven + skip * grad_y
        ).astype(HALF)
        skip_grad_ref[:, lanes] += jnp.sum(grad_y * drive, 0, keepdims=True)
        turn = grad_y * result - driven * grad_driven
        left = lane < HEAD_DIM
        from_drive = drive * grad_driven
        ends = jnp.sum(driven * reach, 0, keepdims=True) + keep_old * jnp.sum(
            later * held_low.astype(FULL), 0, keepdims=True
        )
        for head, mask in ((a, left), (b, ~left)):
            grad_running = grad_running + jnp.where(
                lane == head, jnp.sum(jnp.where(mask, turn, 0.0), 1, keepdims=True), 0.0
            )
            grad_step = grad_step + jnp.where(
                lane == head, jnp.sum(jnp.where(mask, from_drive, 0.0), 1, keepdims=True), 0.0
            )
            grad_last = grad_last + jnp.where(
                head_lane == head, jnp.sum(jnp.where(mask[0:1], ends, 0.0), 1, keepdims=True), 0.0
            )
    paired = paired.astype(HALF)
    grad_out = grad_out + mm(paired, inmap)
    grad_in = grad_in + mm_tn(paired, outmap)
    g_ref[:, col.inmap[0] : col.inmap[1]] = grad_in.astype(HALF)
    g_ref[:, col.outmap[0] : col.outmap[1]] = grad_out.astype(HALF)
    row, column = iota((span, span), 0), iota((span, span), 1)
    grad_keep = (
        jnp.dot((row <= column).astype(FULL), grad_running, precision=PRECISE, preferred_element_type=FULL)
        + grad_last
    )
    grad_raw = (grad_step - grad_keep * jnp.exp(head_ref[0:1, :])) * sigmoid(raw)
    grad_raw = jnp.where(lane < heads, grad_raw, 0.0)
    g_ref[:, col.step[0] : col.step[1]] = grad_raw.astype(HALF)
    g_ref[:, 0 : col.attention] = jnp.zeros((span, col.attention), HALF)
    head_grad_ref[0:1, :] += jnp.sum(keep * grad_keep, 0, keepdims=True)
    head_grad_ref[1:2, :] += jnp.sum(grad_raw, 0, keepdims=True)


def scan_backward(col, heads, state_size, packed, y, states, grad_mamba, inverse, product, gain, segments, head_params):
    length = packed.shape[0]
    width = heads * HEAD_DIM
    count = length // STRETCH
    back = lambda i: (count - 1 - i, 0)
    return pl.pallas_call(
        functools.partial(scan_backward_kernel, col, heads, MAMBA_HEADS * HEAD_DIM),
        grid=(count,),
        in_specs=[
            pl.BlockSpec((STRETCH, col.total), back),
            pl.BlockSpec((STRETCH, width), back),
            pl.BlockSpec((1, state_size, width), lambda i: (count - 1 - i, 0, 0)),
            pl.BlockSpec((STRETCH, width), back),
            pl.BlockSpec((STRETCH, 1), back),
            pl.BlockSpec((STRETCH, 1), back),
            pl.BlockSpec((1, width), lambda i: (0, 0)),
            pl.BlockSpec((STRETCH, 1), back),
            pl.BlockSpec((1, 1, STRETCH), lambda i: (count - 1 - i, 0, 0)),
            pl.BlockSpec((STRETCH, 1), lambda i: (jnp.maximum(count - 2 - i, 0), 0)),
            pl.BlockSpec((8, LANES), lambda i: (0, 0)),
        ],
        out_specs=[
            pl.BlockSpec((STRETCH, col.total), back),
            pl.BlockSpec((1, width), lambda i: (0, 0)),
            pl.BlockSpec((1, width), lambda i: (0, 0)),
            pl.BlockSpec((8, LANES), lambda i: (0, 0)),
        ],
        out_shape=[
            jax.ShapeDtypeStruct((length, col.total), HALF),
            jax.ShapeDtypeStruct((1, width), FULL),
            jax.ShapeDtypeStruct((1, width), FULL),
            jax.ShapeDtypeStruct((8, LANES), FULL),
        ],
        scratch_shapes=[pltpu.VMEM((state_size, width), FULL)],
        cost_estimate=pl.CostEstimate(flops=20_000_000_000, bytes_accessed=40_000_000, transcendentals=0),
        compiler_params=pltpu.CompilerParams(vmem_limit_bytes=48 * 2**20),
    )(
        packed, y, states, grad_mamba, inverse, product, gain, segments[:, None],
        segments.reshape(count, 1, STRETCH), segments[:, None], head_params,
    )


def turned(values, cosine, sine):
    return values * cosine + pltpu.roll(values, ATT_DIM // 2, 1) * sine


def attend_forward_kernel(col, heads, p_ref, cos_ref, sin_ref, segc_ref, segr_ref, out_ref, lse_ref):
    length = p_ref.shape[0]
    scale = 1.0 / math.sqrt(ATT_DIM)
    keys = turned(p_ref[:, col.key[0] : col.key[1]], cos_ref[...], sin_ref[...]).astype(HALF)
    values = p_ref[:, col.value[0] : col.value[1]].astype(HALF)
    for block in range(length // ATT_BLOCK):
        rows = slice(block * ATT_BLOCK, (block + 1) * ATT_BLOCK)
        end = (block + 1) * ATT_BLOCK
        place = iota((ATT_BLOCK, end), 0) + block * ATT_BLOCK
        allowed = (place >= iota((ATT_BLOCK, end), 1)) & (segc_ref[rows, :] == segr_ref[:, :end])
        blocked = jnp.where(allowed, 0.0, MASKED)
        for head in range(heads):
            lanes = slice(head * ATT_DIM, (head + 1) * ATT_DIM)
            query = (turned(p_ref[rows, lanes], cos_ref[rows, :], sin_ref[rows, :]) * scale).astype(HALF)
            scores = mm_nt(query, keys[:end]) + blocked
            highest = jnp.max(scores, 1, keepdims=True)
            weights = jnp.exp(scores - highest)
            total = jnp.sum(weights, 1, keepdims=True)
            out_ref[rows, lanes] = (mm(weights.astype(HALF), values[:end]) / total).astype(HALF)
            lse_ref[rows, lanes] = jnp.broadcast_to(highest + jnp.log(total), (ATT_BLOCK, ATT_DIM))


def attend_forward(col, heads, packed, tables, segments):
    length = packed.shape[0]
    whole = lambda i: (0, 0)
    return pl.pallas_call(
        functools.partial(attend_forward_kernel, col, heads),
        grid=(1,),
        in_specs=[
            pl.BlockSpec((length, col.attention), whole),
            pl.BlockSpec((length, ATT_DIM), whole),
            pl.BlockSpec((length, ATT_DIM), whole),
            pl.BlockSpec((length, 1), whole),
            pl.BlockSpec((1, length), whole),
        ],
        out_specs=[
            pl.BlockSpec((length, heads * ATT_DIM), whole),
            pl.BlockSpec((length, heads * ATT_DIM), whole),
        ],
        out_shape=[
            jax.ShapeDtypeStruct((length, heads * ATT_DIM), HALF),
            jax.ShapeDtypeStruct((length, heads * ATT_DIM), FULL),
        ],
        cost_estimate=pl.CostEstimate(flops=2_000_000_000, bytes_accessed=5_000_000, transcendentals=2_000_000),
        compiler_params=pltpu.CompilerParams(vmem_limit_bytes=48 * 2**20),
    )(packed, tables[0], tables[1], segments[:, None], segments[None, :])


def attend_backward_kernel(
    col, heads, p_ref, out_ref, lse_ref, go_ref, cos_ref, sin_ref, segc_ref, segr_ref, g_in_ref, g_ref,
    key_grad, value_grad,
):
    length = p_ref.shape[0]
    scale = 1.0 / math.sqrt(ATT_DIM)
    keys = turned(p_ref[:, col.key[0] : col.key[1]], cos_ref[...], sin_ref[...]).astype(HALF)
    values = p_ref[:, col.value[0] : col.value[1]].astype(HALF)
    key_grad[...] = jnp.zeros_like(key_grad)
    value_grad[...] = jnp.zeros_like(value_grad)
    for block in range(length // ATT_BLOCK):
        rows = slice(block * ATT_BLOCK, (block + 1) * ATT_BLOCK)
        end = (block + 1) * ATT_BLOCK
        place = iota((ATT_BLOCK, end), 0) + block * ATT_BLOCK
        allowed = (place >= iota((ATT_BLOCK, end), 1)) & (segc_ref[rows, :] == segr_ref[:, :end])
        blocked = jnp.where(allowed, 0.0, MASKED)
        cosine, sine = cos_ref[rows, :], sin_ref[rows, :]
        for head in range(heads):
            lanes = slice(head * ATT_DIM, (head + 1) * ATT_DIM)
            query = (turned(p_ref[rows, lanes], cosine, sine) * scale).astype(HALF)
            weights = jnp.exp(mm_nt(query, keys[:end]) + blocked - lse_ref[rows, lanes][:, 0:1])
            grad_low = go_ref[rows, lanes].astype(HALF)
            delta = jnp.sum(grad_low.astype(FULL) * out_ref[rows, lanes].astype(FULL), 1, keepdims=True)
            grad_scores = (weights * (mm_nt(grad_low, values[:end]) - delta)).astype(HALF)
            value_grad[:end, :] += mm_tn(weights.astype(HALF), grad_low)
            key_grad[:end, :] += mm_tn(grad_scores, query)
            grad_query = mm(grad_scores, keys[:end]) * scale
            g_ref[rows, lanes] = turned(grad_query, cosine, -sine).astype(HALF)
    g_ref[:, col.key[0] : col.key[1]] = turned(key_grad[...], cos_ref[...], -sin_ref[...]).astype(HALF)
    g_ref[:, col.value[0] : col.value[1]] = value_grad[...].astype(HALF)


def attend_backward(col, heads, packed, attended, lse, grad_attended, tables, segments, grads):
    length = packed.shape[0]
    width = heads * ATT_DIM
    whole = lambda i: (0, 0)
    return pl.pallas_call(
        functools.partial(attend_backward_kernel, col, heads),
        grid=(1,),
        in_specs=[
            pl.BlockSpec((length, col.attention), whole),
            pl.BlockSpec((length, width), whole),
            pl.BlockSpec((length, width), whole),
            pl.BlockSpec((length, width), whole),
            pl.BlockSpec((length, ATT_DIM), whole),
            pl.BlockSpec((length, ATT_DIM), whole),
            pl.BlockSpec((length, 1), whole),
            pl.BlockSpec((1, length), whole),
            pl.BlockSpec(memory_space=pl.ANY),
        ],
        out_specs=pl.BlockSpec((length, col.attention), whole),
        out_shape=jax.ShapeDtypeStruct(grads.shape, grads.dtype),
        scratch_shapes=[pltpu.VMEM((length, ATT_DIM), FULL), pltpu.VMEM((length, ATT_DIM), FULL)],
        input_output_aliases={8: 0},
        cost_estimate=pl.CostEstimate(flops=5_000_000_000, bytes_accessed=10_000_000, transcendentals=2_000_000),
        compiler_params=pltpu.CompilerParams(vmem_limit_bytes=48 * 2**20),
    )(
        packed, attended, lse, grad_attended, tables[0], tables[1], segments[:, None], segments[None, :], grads
    )


def rope_tables(length):
    half = ATT_DIM // 2
    positions = jnp.arange(length, dtype=FULL)
    frequency = ROPE_BASE ** (-jnp.arange(half, dtype=FULL) / half)
    angles = positions[:, None] * frequency[None, :]
    cosine, sine = jnp.cos(angles), jnp.sin(angles)
    return jnp.concatenate([cosine, cosine], 1), jnp.concatenate([-sine, sine], 1)


def gather_rows(pieces):
    return lax.all_gather(pieces, "tensor", axis=0, tiled=True)


def sum_rows(pieces):
    return lax.psum_scatter(pieces, "tensor", scatter_dimension=0, tiled=True).astype(FULL)


def norm_forward(values, gain_vals):
    inverse = lax.rsqrt(jnp.mean(values * values, -1, keepdims=True) + EPSILON)
    plain = values * inverse
    return plain, inverse, plain * gain_vals


def norm_backward(grad_above, plain, inverse, gain_vals):
    grad_plain = grad_above * gain_vals
    grad_below = inverse * (grad_plain - plain * jnp.mean(grad_plain * plain, -1, keepdims=True))
    return grad_below, jnp.sum(grad_above * plain, 0)


def silu_parts(gate_input):
    sigmoid_vals = jax.nn.sigmoid(gate_input)
    return gate_input * sigmoid_vals, sigmoid_vals * (1.0 + gate_input * (1.0 - sigmoid_vals))


def dot_tn(a, b):
    return jnp.einsum("sa,sb->ab", a, b, preferred_element_type=FULL)


def dot_nt(a, b):
    return jnp.einsum("sb,ab->sa", a, b, preferred_element_type=FULL)


def body(
    hidden_in,
    segments,
    norm_gain,
    mamba_in,
    step_weight,
    state_weight,
    decay_log,
    step_bias,
    skip_gain,
    gated_gain,
    query_weight,
    keyval_weight,
    mamba_out,
    attn_out,
    ffn_gain,
    gate_up,
    down_weight,
    cotangent,
):
    tensor_index = lax.axis_index("tensor")
    heads = decay_log.shape[0]
    width = mamba_in.shape[2]
    state_size = state_weight.shape[2]
    query_width = query_weight.shape[1]
    qheads = query_width // ATT_DIM
    units = gate_up.shape[2]
    rows_local = hidden_in.shape[0]
    block = norm_gain.shape[0]
    group_size = ATT_HEADS // KV_HEADS
    kv_head = tensor_index * qheads // group_size
    col = Columns(query_width, width, state_size)

    own_keyval = lax.dynamic_slice_in_dim(keyval_weight, kv_head * ATT_DIM, ATT_DIM, 2)
    spare = LANES - heads - 2
    packed_in = jnp.concatenate(
        [
            query_weight,
            own_keyval[:, 0],
            own_keyval[:, 1],
            mamba_in[:, 0],
            mamba_in[:, 1],
            state_weight[:, 0],
            state_weight[:, 1],
            step_weight,
            jnp.zeros((block, spare), HALF),
            norm_gain[:, None],
            ffn_gain[:, None],
        ],
        1,
    )
    weight_in = lax.all_gather(packed_in, "dp", axis=0, tiled=True)
    hidden_rows = gather_rows(hidden_in)
    weight_out = lax.all_gather(jnp.concatenate([mamba_out, attn_out], 0), "dp", axis=1, tiled=True)
    weight_up = lax.all_gather(gate_up.reshape(block, 2 * units), "dp", axis=0, tiled=True)
    weight_down = lax.all_gather(down_weight, "dp", axis=1, tiled=True)
    grad_rows = gather_rows(cotangent)

    gain_one = weight_in[:, col.total - 2].astype(FULL)
    gain_two = weight_in[:, col.total - 1].astype(FULL)
    sequence = norm_forward(hidden_rows.astype(FULL), gain_one)[2].astype(HALF)
    length = sequence.shape[0]
    packed = jnp.dot(sequence, weight_in, preferred_element_type=FULL)
    head_params = jnp.pad(
        jnp.stack([decay_log, step_bias, skip_gain]), ((0, 5), (0, LANES - heads))
    )
    tables = rope_tables(length)

    scan_y, states, gated_vals, squares = scan_forward(
        col, heads, state_size, packed, segments, head_params
    )
    square_sum = lax.psum(squares[:, 0], "tensor")
    gated_inverse = lax.rsqrt(square_sum / (MAMBA_HEADS * HEAD_DIM) + EPSILON)[:, None]
    attended, lse = attend_forward(col, qheads, packed, tables, segments)
    gated_scale = gated_gain.astype(FULL)
    gated_plain = gated_vals * gated_inverse
    branches = jnp.concatenate([(gated_plain * gated_scale).astype(HALF), attended], 1)
    middle = hidden_in.astype(FULL) + sum_rows(jnp.dot(branches, weight_out))
    plain_two, inverse_two, scaled_two = norm_forward(middle, gain_two)
    ffn_rows = gather_rows(scaled_two.astype(HALF))
    gate_vals = jnp.dot(ffn_rows, weight_up, preferred_element_type=FULL)
    gate_part, up_part = gate_vals[:, :units], gate_vals[:, units:]
    silu_gate, silu_slope = silu_parts(gate_part)
    activated = (silu_gate * up_part).astype(HALF)
    grad_act = dot_nt(grad_rows, weight_down)
    grad_gate = jnp.concatenate(
        [grad_act * up_part * silu_slope, grad_act * silu_gate], 1
    ).astype(HALF)
    grad_ffn_in = sum_rows(dot_nt(grad_gate, weight_up).astype(HALF))
    grad_middle_norm, ffn_gain_part = norm_backward(grad_ffn_in, plain_two, inverse_two, gain_two)
    grad_middle = cotangent.astype(FULL) + grad_middle_norm
    grad_mixed = gather_rows(grad_middle.astype(HALF))

    ffn_out = sum_rows(jnp.dot(activated, weight_down))
    hidden_out = (middle + ffn_out).astype(HALF)
    up_grad = dot_tn(ffn_rows, grad_gate).astype(HALF)
    down_grad = dot_tn(activated, grad_rows).astype(HALF)
    gate_share = lax.psum_scatter(up_grad, "dp", scatter_dimension=0, tiled=True)
    down_share = lax.psum_scatter(down_grad, "dp", scatter_dimension=1, tiled=True)

    grad_branches = dot_nt(grad_mixed, weight_out)
    out_grad = dot_tn(branches, grad_mixed).astype(HALF)
    out_share = lax.psum_scatter(out_grad, "dp", scatter_dimension=1, tiled=True)
    grad_mamba = grad_branches[:, :width]
    product_sum = lax.psum(jnp.sum(grad_mamba * gated_scale * gated_plain, -1), "tensor")[:, None]
    grads, gain_part, skip_part, head_part = scan_backward(
        col,
        heads,
        state_size,
        packed,
        scan_y,
        states,
        grad_mamba,
        gated_inverse,
        product_sum,
        gated_scale[None, :],
        segments,
        head_params,
    )
    grads = attend_backward(
        col, qheads, packed, attended, lse, grad_branches[:, width:], tables, segments, grads
    )
    grad_first = sum_rows(dot_nt(grads, weight_in).astype(HALF))
    in_grad = dot_tn(sequence, grads)
    in_share = lax.psum_scatter(in_grad.astype(HALF), "dp", scatter_dimension=0, tiled=True)
    plain_one, inverse_one, _ = norm_forward(hidden_in.astype(FULL), gain_one)
    grad_hidden_norm, norm_gain_part = norm_backward(grad_first, plain_one, inverse_one, gain_one)
    hidden_grad = grad_middle + grad_hidden_norm

    keyval_part = jnp.stack(
        [in_share[:, slice(*col.key)], in_share[:, slice(*col.value)]], 1
    )
    keyval_grad = lax.dynamic_update_slice_in_dim(
        jnp.zeros(keyval_weight.shape, HALF), keyval_part, kv_head * ATT_DIM, 2
    ).reshape(block, -1)
    shared = lax.psum(
        jnp.concatenate([in_share[:, col.inmap[0] : col.outmap[1]], keyval_grad], 1), "tensor"
    ).astype(FULL)
    state_weight_grad = shared[:, : 2 * state_size].reshape(state_weight.shape)
    keyval_weight_grad = shared[:, 2 * state_size :].reshape(keyval_weight.shape)

    gains = lax.psum(jnp.stack([norm_gain_part, ffn_gain_part]), ("dp", "tensor"))
    dp_index = lax.axis_index("dp")
    gains = lax.dynamic_slice_in_dim(gains, dp_index * block, block, 1)
    head_sums = lax.psum(
        jnp.concatenate(
            [
                head_part[0, :heads],
                head_part[1, :heads],
                skip_part.reshape(heads, HEAD_DIM).sum(1),
                gain_part[0],
            ]
        ),
        "dp",
    )
    inner_grad = jnp.stack([in_share[:, slice(*col.gate)], in_share[:, slice(*col.drive)]], 1)
    return (
        hidden_out,
        hidden_grad,
        gains[0],
        inner_grad.astype(FULL),
        in_share[:, col.step[0] : col.step[0] + heads].astype(FULL),
        state_weight_grad,
        head_sums[:heads],
        head_sums[heads : 2 * heads],
        head_sums[2 * heads : 3 * heads],
        head_sums[3 * heads :],
        in_share[:, slice(*col.query)].astype(FULL),
        keyval_weight_grad,
        out_share[:width].astype(FULL),
        out_share[width:].astype(FULL),
        gains[1],
        gate_share.reshape(gate_up.shape).astype(FULL),
        down_share.astype(FULL),
    )


def solution(mesh):
    rows = P(("dp", "tensor"), None)
    weights_in = P("dp", None, "tensor")
    return jax.shard_map(
        body,
        mesh=mesh,
        in_specs=(
            rows,
            P("dp"),
            P("dp"),
            weights_in,
            P("dp", "tensor"),
            P("dp", None, None),
            P("tensor"),
            P("tensor"),
            P("tensor"),
            P("tensor"),
            P("dp", "tensor"),
            P("dp", None, None),
            P("tensor", "dp"),
            P("tensor", "dp"),
            P("dp"),
            weights_in,
            P("tensor", "dp"),
            rows,
        ),
        out_specs=(
            rows,
            rows,
            P("dp"),
            weights_in,
            P("dp", "tensor"),
            P("dp", None, None),
            P("tensor"),
            P("tensor"),
            P("tensor"),
            P("tensor"),
            P("dp", "tensor"),
            P("dp", None, None),
            P("tensor", "dp"),
            P("tensor", "dp"),
            P("dp"),
            weights_in,
            P("tensor", "dp"),
        ),
        check_vma=False,
    )
```

time: 2390 us -> 1240 us (0.52)
  waiting for transfers between devices: 1320 us -> 835 us
  matrix products: 458 us -> 155 us
  local copies, waits for them, and re-layouts: 302 us -> 39.7 us
  other arithmetic: 137 us -> 37.9 us
  Pallas kernels: 0 us -> 53.6 us
  loops' own time: 51.8 us -> 0 us
    reduce_scatter x12 -> x8, waiting for transfers between devices: 816 us -> 368 us  [the longest x4 255 us: sum_rows(): lax.psum_scatter(pieces, 'tensor', scatter_dimension=0, tiled=True)]
    dot_general x156 -> x12, matrix products: 455 us -> 155 us  [the longest x4 52.2 us: dot_nt(): return jnp.einsum('sb,ab->sa', a, b, preferred_element_type=FULL)]
    dynamic_update_slice x17 -> x1, local copies, waits for them, and re-layouts: 102 us -> 0.23 us  [body(): lax.dynamic_update_slice_in_dim(jnp.zeros(keyval_weight.shape, HALF), key...]
    pallas_call x0 -> x4, Pallas kernels: none -> 53.6 us  [the longest x1 24.4 us: scan_backward(): pl.pallas_call(functools.partial(scan_backward_kernel, col, heads, MAMBA_...]
    psum x4, blocking collectives: 46.2 us -> 98.6 us  [the longest x1 46.3 us: body(): lax.psum(jnp.stack([norm_gain_part, ffn_gain_part]), ('dp', 'tensor'))]
    another operation x4 -> x0, loops' own time: 51.8 us -> none  [the longest x2 28.5 us: attend(): lax.map(jax.checkpoint(score_block), jnp.arange(blocks, dtype=jnp.int32))]
    dynamic_slice x37 -> x0, local copies, waits for them, and re-layouts: 45.9 us -> none  [the longest x24 37.8 us: mixer_scan(): lax.scan(jax.checkpoint(stretch_step), initial, pieces)]
    squeeze x64 -> x4, local copies, waits for them, and re-layouts: 39.6 us -> 0.18 us  [the longest x1 0.11 us: body(): mamba_in[:, 1]]
  transfers between devices with their start and end apart: 26 -> 17, of which waited for: 22 -> 14; matrix products, arithmetic and copies ran while one was open for 17% -> 14% of each run, Pallas kernels for 0% -> 4%
where the time goes in v1:
time: 1240 us
  waiting for transfers between devices  835 us (67%)
  matrix products  155 us (12%)
  blocking collectives  98.6 us (8%)
  Pallas kernels  53.6 us (4%)
  local copies, waits for them, and re-layouts  39.7 us (3%)
  other arithmetic  37.9 us (3%)
  between operations  14.8 us (1%)
    all_gather x4, waiting for transfers between devices, gather_rows(): return lax.all_gather(pieces, 'tensor', axis=0, tiled=True)  278 us
    reduce_scatter x4, waiting for transfers between devices, sum_rows(): lax.psum_scatter(pieces, 'tensor', scatter_dimension=0, tiled=True)  255 us
    reduce_scatter x1, waiting for transfers between devices, body(): lax.psum_scatter(in_grad.astype(HALF), 'dp', scatter_dimension=0, tiled=T...  83.1 us
    all_gather x1, waiting for transfers between devices, body(): weight_in = lax.all_gather(packed_in, 'dp', axis=0, tiled=True)  63.4 us
    dot_general x4, matrix products, dot_nt(): return jnp.einsum('sb,ab->sa', a, b, preferred_element_type=FULL)  52.2 us
    dot_general x4, matrix products, dot_tn(): return jnp.einsum('sa,sb->ab', a, b, preferred_element_type=FULL)  51.5 us
    all_gather x1, waiting for transfers between devices, body(): lax.all_gather(gate_up.reshape(block, 2 * units), 'dp', axis=0, tiled=True)  51.1 us
    psum x1, blocking collectives, body(): lax.psum(jnp.stack([norm_gain_part, ffn_gain_part]), ('dp', 'tensor'))  46.3 us
  transfers between devices with their start and end apart: 17, of which 14 were waited for; matrix products, arithmetic and copies ran while one was open for 14% of the time, Pallas kernels for 4%

profile of v1, /device:TPU:0, one launch (start us, length us, event | category | flops | bytes accessed | tf_op | source)
XLA Modules:
  0.0 1236.2 jit_solution(598363031592299887)
XLA Ops:
  14.6 2.4 concatenate.25
  18.5 2.0 fusion.26
  20.8 72.3 %all-gather.9.cloned.1.call-done = bf16[1024,2048]{1,0:T(8,128)(2,1)} async-done(((bf16[256,2048]{1,0:T(8,128)(2,1)}), bf16[1024,2048]{1,0:T(8,128)(2,1)}) %all-gather.9.cloned.1.call-update) | async-done | bytes 4194320 | tf_op jit(solution)/shard_map/all_gather | solution.py:460
  93.1 3.1 fusion
  96.2 63.4 %all-gather.11.cloned.1.call-done = bf16[2048,2688]{1,0:T(8,128)(2,1)} async-done(((bf16[256,2688]{1,0:T(8,128)(2,1)}), bf16[2048,2688]{1,0:T(8,128)(2,1)}) %all-gather.11.cloned.1.call-update) | async-done | bytes 11010064 | tf_op jit(solution)/shard_map/all_gather | solution.py:543
  159.6 2.0 convert_reduce_fusion
  161.6 18.9 %fusion.22.p_ref = f32[1024,2688]{1,0:T(8,128)} fusion(bf16[2048,2688]{1,0:T(8,128)(2,1)} %all-gather.11.cloned.1.call-done, bf16[1024,2048]{1,0:T(8,128)(2,1)} %all-gather.9.cloned.1.call-done, f32[2048]{0:T(1024)S(1)} %get-tuple-element.72, f32[1024]{0:T(1024)S(1)} %add_rsqrt_fusion.1), kind=kOutput, calls=%fused_computation.46 | convolution fusion | flops 11282677760 | bytes 26226688 | tf_op jit(solution)/shard_map/dot_general | solution.py:554
  180.5 16.0 %shard_map.305 = (f32[1024,768]{1,0:T(8,128)S(1)}, bf16[8,256,768]{2,1,0:T(8,128)(2,1)}, f32[1024,768]{1,0:T(8,128)}, f32[1024,128]{1,0:T(8,128)S(1)}) custom-call(f32[1024,2688]{1,0:T(8,128)} %fusion.22.p_ref, s32[1024,1]{1,0:T(8,128)S(1)} %copy.53.segc_ref.segb_ref, s32[8,1,128]{2,1,0:T(1,128)S(1)} %bitcast.59, f32[8,128]{1,0:T(8,128)S(1)} %select_maximum_fusion.head_ref), custom_call_target="tpu_custom_call" | custom-call | flops 6000000000 | bytes 30000000 | tf_op jit(solution)/shard_map/pallas_call | solution.py:157
  198.4 11.9 psum.35
  210.3 5.5 shard_map.306
  218.2 9.1 fusion.20
  227.4 2.5 copy.76
  230.1 71.5 %reduce-scatter.9.cloned.1.call-done = bf16[256,2048]{1,0:T(8,128)(2,1)} async-done(((bf16[1024,2048]{1,0:T(8,128)(2,1)}), bf16[256,2048]{1,0:T(8,128)(2,1)}) %reduce-scatter.9.cloned.1.call-update) | async-done | bytes 1048592 | tf_op jit(solution)/shard_map/reduce_scatter | solution.py:464
  303.2 2.6 multiply_convert_fusion.4
  307.8 51.1 %all-gather.17.cloned.1.call-done = bf16[2048,2048]{1,0:T(8,128)(2,1)} async-done(((bf16[256,2048]{1,0:T(8,128)(2,1)}), bf16[2048,2048]{1,0:T(8,128)(2,1)}) %all-gather.17.cloned.1.call-update) | async-done | bytes 8388624 | tf_op jit(solution)/shard_map/all_gather | solution.py:546
  358.9 82.9 %all-gather.15.cloned.1.call-done = bf16[1024,2048]{1,0:T(8,128)(2,1)} async-done(((bf16[256,2048]{1,0:T(8,128)(2,1)}), bf16[1024,2048]{1,0:T(8,128)(2,1)}) %all-gather.15.cloned.1.call-update) | async-done | bytes 4194320 | tf_op jit(solution)/shard_map/all_gather | solution.py:460
  441.8 14.6 %fusion.37 = f32[1024,2048]{1,0:T(8,128)} fusion(bf16[1024,2048]{1,0:T(8,128)(2,1)} %all-gather.15.cloned.1.call-done, bf16[2048,2048]{1,0:T(8,128)(2,1)} %all-gather.17.cloned.1.call-done), kind=kOutput, calls=%fused_computation.103 | convolution fusion | flops 8589934592 | bytes 20971520 | tf_op jit(solution)/shard_map/dot_general | solution.py:572
  456.4 66.4 %all-gather.21.cloned.1.call-done = bf16[1024,2048]{1,0:T(8,128)(2,1)} async-done(((bf16[256,2048]{1,0:T(8,128)(2,1)}), bf16[1024,2048]{1,0:T(8,128)(2,1)}) %all-gather.21.cloned.1.call-update) | async-done | bytes 4194320 | tf_op jit(solution)/shard_map/all_gather | solution.py:460
  522.8 38.0 %all-gather.19.cloned.1.call-done = bf16[1024,2048]{1,0:T(8,128)(2,1)} async-done(((bf16[1024,256]{1,0:T(8,128)(2,1)}), bf16[1024,2048]{1,0:T(8,128)(2,1)}) %all-gather.19.cloned.1.call-update) | async-done | bytes 4194320 | tf_op jit(solution)/shard_map/all_gather | solution.py:547
  560.8 13.1 %multiply_convert_fusion.1 = (bf16[1024,1024]{1,0:T(8,128)(2,1)S(1)}, bf16[1024,1024]{1,0:T(8,128)(2,1)S(1)}, bf16[1024,1024]{1,0:T(8,128)(2,1)}) fusion(f32[1024,2048]{1,0:T(8,128)} %fusion.37, bf16[1024,2048]{1,0:T(8,128)(2,1)} %all-gather.21.cloned.1.call-done, bf16[1024,2048]{1,0:T(8,128)(2,1)} %all-gather.19.cloned.1.call-done), kind=kOutput, calls=%fused_computation.9 | convolution fusion | flops 4310695936 | bytes 23068672 | tf_op jit(solution)/shard_map/sb,ab->sa/dot_general | solution.py:489
  575.9 12.6 %convolution_convert_fusion.3 = bf16[1024,2048]{1,0:T(8,128)(2,1)} fusion(bf16[2048,2048]{1,0:T(8,128)(2,1)} %all-gather.17.cloned.1.call-done, bf16[1024,1024]{1,0:T(8,128)(2,1)S(1)} %get-tuple-element.79, bf16[1024,1024]{1,0:T(8,128)(2,1)S(1)} %get-tuple-element.78), kind=kOutput, calls=%fused_computation.14 | convolution fusion | flops 8600420352 | bytes 16777216 | tf_op jit(solution)/shard_map/sb,ab->sa/dot_general | solution.py:489
  588.7 76.7 %reduce-scatter.13.cloned.1.call-done = bf16[256,2048]{1,0:T(8,128)(2,1)} async-done(((bf16[1024,2048]{1,0:T(8,128)(2,1)}), bf16[256,2048]{1,0:T(8,128)(2,1)}) %reduce-scatter.13.cloned.1.call-update) | async-done | bytes 1048592 | tf_op jit(solution)/shard_map/reduce_scatter | solution.py:464
  665.4 2.7 fusion.15
  668.1 3.8 fusion.31
  672.0 9.4 convolution_convert_fusion.4
  681.4 14.5 %convolution_convert_fusion.1 = bf16[2048,2048]{1,0:T(8,128)(2,1)} fusion(bf16[1024,2048]{1,0:T(8,128)(2,1)} %all-gather.15.cloned.1.call-done, bf16[1024,1024]{1,0:T(8,128)(2,1)} %copy-done.28, bf16[1024,1024]{1,0:T(8,128)(2,1)} %copy-done.27), kind=kOutput, calls=%fused_computation.6 | convolution fusion | flops 8602517504 | bytes 16777216 | tf_op jit(solution)/shard_map/sa,sb->ab/dot_general | solution.py:485
  697.2 56.2 %all-gather.23.cloned.1.call-done = bf16[1024,2048]{1,0:T(8,128)(2,1)} async-done(((bf16[256,2048]{1,0:T(8,128)(2,1)}), bf16[1024,2048]{1,0:T(8,128)(2,1)}) %all-gather.23.cloned.1.call-update) | async-done | bytes 4194320 | tf_op jit(solution)/shard_map/all_gather | solution.py:460
  753.4 9.2 convolution_convert_fusion.5
  762.7 8.4 fusion.39
  771.2 2.3 multiply_reduce_fusion
  774.5 28.7 %psum.36.prod_ref = f32[1024,1]{1,0:T(8,128)} all-reduce(f32[1024,1]{1,0:T(8,128)} %copy.59), channel_id=1, replica_groups=mesh['dp'=8,'tensor'=4] {'tensor'}, use_global_device_ids=true, to_apply=%region_9.10 | all-reduce | flops 1024 | bytes 8192 | tf_op jit(solution)/shard_map/psum | solution.py:596
  807.2 24.4 %shard_map.307 = (bf16[1024,2688]{1,0:T(8,128)(2,1)}, f32[1,768]{1,0:T(1,128)S(1)}, f32[1,768]{1,0:T(1,128)S(1)}, f32[8,128]{1,0:T(8,128)S(1)}) custom-call(f32[1024,2688]{1,0:T(8,128)} %fusion.22.p_ref, f32[1024,768]{1,0:T(8,128)S(1)} %copy-done.6, bf16[8,256,768]{2,1,0:T(8,128)(2,1)} %get-tuple-element.32.states_ref, ...), custom_call_target="tpu_custom_call" | custom-call | flops 20000000000 | bytes 40000000 | tf_op jit(solution)/shard_map/pallas_call | solution.py:300
  831.6 7.7 shard_map.308
  839.3 18.1 %convolution_convert_fusion.2 = bf16[1024,2048]{1,0:T(8,128)(2,1)} fusion(bf16[1024,2688]{1,0:T(8,128)(2,1)} %shard_map.308, bf16[2048,2688]{1,0:T(8,128)(2,1)} %all-gather.11.cloned.1.call-done), kind=kOutput, calls=%fused_computation.13 | convolution fusion | flops 11276386304 | bytes 20709376 | tf_op jit(solution)/shard_map/sb,ab->sa/dot_general | solution.py:489
  859.0 8.3 fusion.38
  868.0 18.5 %convolution_convert_fusion = bf16[2048,2688]{1,0:T(8,128)(2,1)} fusion(bf16[1024,2688]{1,0:T(8,128)(2,1)} %shard_map.308, bf16[1024,2048]{1,0:T(8,128)(2,1)} %all-gather.9.cloned.1.call-done, f32[2048]{0:T(1024)S(1)} %copy-done.19, f32[1024]{0:T(1024)S(1)} %copy-done.22), kind=kOutput, calls=%fused_computation | convolution fusion | flops 11288182784 | bytes 20721664 | tf_op jit(solution)/shard_map/sa,sb->ab/dot_general | solution.py:485
  886.6 2.2 convert_element_type.143
  888.9 4.1 reshape.118
  893.3 11.8 psum.39
  906.4 30.0 %reduce-scatter.19.cloned.1.call-done = bf16[1024,256]{1,0:T(8,128)(2,1)} async-done(((bf16[1024,2048]{1,0:T(8,128)(2,1)}), bf16[1024,256]{1,0:T(8,128)(2,1)}) %reduce-scatter.19.cloned.1.call-update) | async-done | bytes 524304 | tf_op jit(solution)/shard_map/reduce_scatter | solution.py:594
  939.9 75.5 %reduce-scatter.15.cloned.1.call-done = bf16[256,2048]{1,0:T(8,128)(2,1)} async-done(((bf16[1024,2048]{1,0:T(8,128)(2,1)}), bf16[256,2048]{1,0:T(8,128)(2,1)}) %reduce-scatter.15.cloned.1.call-update) | async-done | bytes 1048592 | tf_op jit(solution)/shard_map/reduce_scatter | solution.py:464
  1015.4 2.1 fusion.17
  1017.5 46.3 %psum.37 = f32[2,2048]{1,0:T(2,128)S(1)} all-reduce(f32[2,2048]{1,0:T(2,128)S(1)} %pad_maximum_fusion.11), channel_id=1, replica_groups=mesh['dp'=8,'tensor'=4] {'dp','tensor'}, use_global_device_ids=true, to_apply=%region_14.15 | all-reduce | flops 4096 | bytes 32768 | tf_op jit(solution)/shard_map/psum | solution.py:633
  1064.5 31.4 %reduce-scatter.11.cloned.1.call-done = bf16[256,2048]{1,0:T(8,128)(2,1)} async-done(((bf16[1024,2048]{1,0:T(8,128)(2,1)}), bf16[256,2048]{1,0:T(8,128)(2,1)}) %reduce-scatter.11.cloned.1.call-update) | async-done | bytes 1048592 | tf_op jit(solution)/shard_map/reduce_scatter | solution.py:464
  1095.9 5.3 fusion.11
  1101.2 83.1 %reduce-scatter.17.cloned.1.call-done = bf16[256,2688]{1,0:T(8,128)(2,1)} async-done(((bf16[2048,2688]{1,0:T(8,128)(2,1)}), bf16[256,2688]{1,0:T(8,128)(2,1)}) %reduce-scatter.17.cloned.1.call-update) | async-done | bytes 1376272 | tf_op jit(solution)/shard_map/reduce_scatter | solution.py:616
  1187.8 2.4 copy.65
  1191.6 34.5 %all-reduce.3.cloned.1.call-done = bf16[256,1024]{1,0:T(8,128)(2,1)} async-done(((bf16[256,1024]{1,0:T(8,128)(2,1)}), bf16[256,1024]{1,0:T(8,128)(2,1)}) %all-reduce.3.cloned.1.call-update) | async-done | bytes 524304 | tf_op jit(solution)/shard_map/psum | solution.py:627
  (151 shorter events, 42.3 us)
Async XLA Ops:
  7.2 6.1 copy-start.13
  7.2 85.9 %all-gather.9.cloned.1.call-start = ((), (), s32[]{:S(2)}) async-start(), calls=%async_computation.8 | async-start | bytes 5242880 | tf_op jit(solution)/shard_map/all_gather | solution.py:460
  7.9 151.7 %all-gather.11.cloned.1.call-start = ((), (), s32[]{:S(2)}) async-start(), calls=%async_computation.9 | async-start | bytes 12386304 | tf_op jit(solution)/shard_map/all_gather | solution.py:543
  9.6 5.0 copy-start.16
  13.3 3.9 copy-start.15
  13.3 3.9 copy-start.17
  14.4 3.8 copy-start.4
  14.4 4.0 copy-start.20
  14.4 4.1 copy-start.23
  14.4 4.1 copy-start.24
  14.4 4.1 copy-start.25
  17.1 201.2 %all-gather.13.cloned.1.call-start = ((), (), s32[]{:S(2)}) async-start(), calls=%async_computation.10 | async-start | bytes 4718592 | tf_op jit(solution)/shard_map/all_gather | solution.py:545
  18.0 283.6 %reduce-scatter.9.cloned.1.call-start = ((), (), s32[]{:S(2)}) async-start(), calls=%async_computation.11 | async-start | bytes 5242880 | tf_op jit(solution)/shard_map/reduce_scatter | solution.py:464
  96.2 84.3 %copy-start.21 = (f32[1024]{0:T(1024)}, f32[1024]{0:T(1024)S(1)}, u32[]{:S(2)}) copy-start(f32[1024]{0:T(1024)S(1)} %add_rsqrt_fusion.1) | copy-start | bytes 12292
  161.6 18.9 %copy-start.18 = (f32[2048]{0:T(1024)}, f32[2048]{0:T(1024)S(1)}, u32[]{:S(2)}) copy-start(f32[2048]{0:T(1024)S(1)} %get-tuple-element.72) | copy-start | bytes 24580
  196.5 1.7 copy-start.5
  210.3 6.5 copy-start.10
  215.8 1.0 copy-start
  227.4 74.2 %copy-start.7 = (bf16[256,2048]{1,0:T(8,128)(2,1)S(1)}, bf16[256,2048]{1,0:T(8,128)(2,1)}, u32[]{:S(2)}) copy-start(bf16[256,2048]{1,0:T(8,128)(2,1)} %param.18) | copy-start | bytes 3145732
  227.4 131.6 %all-gather.17.cloned.1.call-start = ((), (), s32[]{:S(2)}) async-start(), calls=%async_computation.13 | async-start | bytes 9437184 | tf_op jit(solution)/shard_map/all_gather | solution.py:546
  230.0 211.8 %all-gather.15.cloned.1.call-start = ((), (), s32[]{:S(2)}) async-start(), calls=%async_computation.12 | async-start | bytes 5242880 | tf_op jit(solution)/shard_map/all_gather | solution.py:460
  305.9 216.9 %all-gather.21.cloned.1.call-start = ((), (), s32[]{:S(2)}) async-start(), calls=%async_computation.16 | async-start | bytes 5242880 | tf_op jit(solution)/shard_map/all_gather | solution.py:460
  306.6 254.2 %all-gather.19.cloned.1.call-start = ((), (), s32[]{:S(2)}) async-start(), calls=%async_computation.14 | async-start | bytes 4718592 | tf_op jit(solution)/shard_map/all_gather | solution.py:547
  307.4 358.1 %reduce-scatter.13.cloned.1.call-start = ((), (), s32[]{:S(2)}) async-start(), calls=%async_computation.17 | async-start | bytes 5242880 | tf_op jit(solution)/shard_map/reduce_scatter | solution.py:464
  573.9 1.3 copy-start.27
  573.9 2.0 copy-start.28
  588.5 164.9 %all-gather.23.cloned.1.call-start = ((), (), s32[]{:S(2)}) async-start(), calls=%async_computation.18 | async-start | bytes 5242880 | tf_op jit(solution)/shard_map/all_gather | solution.py:460
  672.0 214.7 %reduce-scatter.23.cloned.1.call-start = ((), (), s32[]{:S(2)}) async-start(), calls=%async_computation.24 | async-start | bytes 4718592 | tf_op jit(solution)/shard_map/reduce_scatter | solution.py:590
  681.4 207.5 %reduce-scatter.21.cloned.1.call-start = ((), (), s32[]{:S(2)}) async-start(), calls=%async_computation.23 | async-start | bytes 9437184 | tf_op jit(solution)/shard_map/reduce_scatter | solution.py:589
  695.9 240.4 %reduce-scatter.19.cloned.1.call-start = ((), (), s32[]{:S(2)}) async-start(), calls=%async_computation.22 | async-start | bytes 4718592 | tf_op jit(solution)/shard_map/reduce_scatter | solution.py:594
  762.6 252.8 %reduce-scatter.15.cloned.1.call-start = ((), (), s32[]{:S(2)}) async-start(), calls=%async_computation.19 | async-start | bytes 5242880 | tf_op jit(solution)/shard_map/reduce_scatter | solution.py:464
  762.7 8.6 copy-start.11
  803.2 1.1 copy-start.2
  804.2 1.0 copy-start.3
  805.3 1.9 copy-start.6
  807.2 24.4 %copy-start.1 = (f32[1024,256]{1,0:T(8,128)S(1)}, f32[1024,256]{1,0:T(8,128)}, u32[]{:S(2)}) copy-start(f32[1024,256]{1,0:T(8,128)} %copy-done) | copy-start | bytes 3145732
  857.4 1.6 copy-start.26
  857.5 238.5 %reduce-scatter.11.cloned.1.call-start = ((), (), s32[]{:S(2)}) async-start(), calls=%async_computation.15 | async-start | bytes 5242880 | tf_op jit(solution)/shard_map/reduce_scatter | solution.py:464
  867.3 0.7 copy-start.19
  867.3 0.7 copy-start.22
  867.3 317.0 %reduce-scatter.17.cloned.1.call-start = ((), (), s32[]{:S(2)}) async-start(), calls=%async_computation.20 | async-start | bytes 12386304 | tf_op jit(solution)/shard_map/reduce_scatter | solution.py:616
  886.5 128.9 %copy-start.8 = (bf16[256,2048]{1,0:T(8,128)(2,1)S(1)}, bf16[256,2048]{1,0:T(8,128)(2,1)}, u32[]{:S(2)}) copy-start(bf16[256,2048]{1,0:T(8,128)(2,1)} %param.18) | copy-start | bytes 3145732
  886.5 339.5 %all-reduce.3.cloned.1.call-start = ((), (), s32[]{:S(2)}) async-start(), calls=%async_computation.21 | async-start | bytes 1048576 | tf_op jit(solution)/shard_map/psum | solution.py:627
  886.6 209.3 %copy-start.9 = (bf16[256,2048]{1,0:T(8,128)(2,1)S(1)}, bf16[256,2048]{1,0:T(8,128)(2,1)}, u32[]{:S(2)}) copy-start(bf16[256,2048]{1,0:T(8,128)(2,1)} %reduce-scatter.9.cloned.1.call-done) | copy-start | bytes 3145732
  886.6 209.3 %copy-start.12 = (bf16[256,2048]{1,0:T(8,128)(2,1)S(1)}, bf16[256,2048]{1,0:T(8,128)(2,1)}, u32[]{:S(2)}) copy-start(bf16[256,2048]{1,0:T(8,128)(2,1)} %reduce-scatter.13.cloned.1.call-done) | copy-start | bytes 3145732
  1184.4 3.3 copy-start.14
Sparse Core Ops, SparseCore 0:
  9.6 83.4 all-gather.8
  95.6 63.9 all-gather.10
  162.1 37.4 all-gather.12
  227.5 73.9 reduce-scatter.8
  304.0 54.8 all-gather.16
  361.0 80.7 all-gather.14
  443.5 79.2 all-gather.20
  524.8 35.9 all-gather.18
  588.6 76.7 reduce-scatter.12
  672.1 81.2 all-gather.22
  756.8 49.8 reduce-scatter.22
  810.4 71.2 reduce-scatter.20
  885.0 51.2 reduce-scatter.18
  938.6 76.7 reduce-scatter.14
  1017.6 78.2 reduce-scatter.10
  1099.8 84.5 reduce-scatter.16
  1187.8 38.2 all-reduce.2

commit v2 on v1

--- a/solution.py
+++ b/solution.py
@@ -456,6 +456,379 @@
     return jnp.concatenate([cosine, cosine], 1), jnp.concatenate([-sine, sine], 1)
 
 
+MESH = pl.DeviceIdType.MESH
+TILE = 256
+
+
+class Line:
+    def __init__(self, count):
+        self.count = count
+        self.me = lax.axis_index("tensor")
+        self.has_left = self.me > 0
+        self.has_right = self.me < count - 1
+
+    def greet(self):
+        barrier = pltpu.get_barrier_semaphore()
+        for present, shift in ((self.has_left, -1), (self.has_right, 1)):
+
+            @pl.when(present)
+            def _():
+                pl.semaphore_signal(
+                    barrier, inc=1, device_id={"tensor": self.me + shift}, device_id_type=MESH
+                )
+
+        inside = self.has_left & self.has_right
+
+        @pl.when(inside)
+        def _():
+            pl.semaphore_wait(barrier, 2)
+
+        @pl.when(jnp.logical_not(inside))
+        def _():
+            pl.semaphore_wait(barrier, 1)
+
+    def copy(self, source, target, sends, receives, at, side):
+        return pltpu.make_async_remote_copy(
+            src_ref=source,
+            dst_ref=target,
+            send_sem=sends.at[at],
+            recv_sem=receives.at[at],
+            device_id={"tensor": self.me + (1 if side == 0 else -1)},
+            device_id_type=MESH,
+        )
+
+    def place(self, side):
+        return self.me if side == 0 else self.count - 1 - self.me
+
+    def ahead(self, side, distance):
+        return self.me + distance if side == 0 else self.me - distance
+
+    def next_there(self, side):
+        return self.has_right if side == 0 else self.has_left
+
+    def last_there(self, side):
+        return self.has_left if side == 0 else self.has_right
+
+
+class Scatter:
+    def __init__(self, line, parts, rows, span, slots, sends, receives):
+        self.line, self.parts, self.rows, self.span = line, parts, rows, span
+        self.slots, self.sends, self.receives = slots, sends, receives
+
+    def own(self, owner, chunk):
+        return self.parts[pl.ds(pl.multiple_of(owner * self.rows + chunk * self.span, 16), self.span), :]
+
+    def transfer(self, side, chunk, hop):
+        return self.line.copy(
+            self.slots.at[side, chunk, hop - 1],
+            self.slots.at[side, chunk, hop],
+            self.sends,
+            self.receives,
+            (side, chunk, hop - 1),
+            side,
+        )
+
+    def hop(self, chunk, hop):
+        line = self.line
+        for side in (0, 1):
+            place = line.place(side)
+            slot = self.slots.at[side, chunk, hop - 1]
+            owner = line.ahead(side, line.count - hop)
+
+            @pl.when(place == 0)
+            def _():
+                slot[...] = self.own(owner, chunk).astype(slot.dtype)
+
+            if hop > 1:
+
+                @pl.when((place > 0) & (place <= hop - 1))
+                def _():
+                    self.transfer(side, chunk, hop - 1).wait_recv()
+                    slot[...] = (slot[...].astype(FULL) + self.own(owner, chunk)).astype(slot.dtype)
+
+            @pl.when(place <= hop - 1)
+            def _():
+                self.transfer(side, chunk, hop).start()
+
+    def finish(self, chunk, total):
+        line = self.line
+        total[...] = self.own(line.me, chunk)
+        last = line.count - 1
+        for side in (0, 1):
+
+            @pl.when(line.last_there(side))
+            def _():
+                self.transfer(side, chunk, last).wait_recv()
+                total[...] += self.slots[side, chunk, last].astype(FULL)
+
+    def drain(self, chunk):
+        for hop in range(1, self.line.count):
+            for side in (0, 1):
+
+                @pl.when(self.line.place(side) <= hop - 1)
+                def _():
+                    self.transfer(side, chunk, hop).wait_send()
+
+
+class Gather:
+    def __init__(self, line, whole, rows, span, sends, receives):
+        self.line, self.whole, self.rows, self.span = line, whole, rows, span
+        self.sends, self.receives = sends, receives
+
+    def at(self, owner, chunk):
+        return self.whole.at[pl.ds(pl.multiple_of(owner * self.rows + chunk * self.span, 16), self.span), :]
+
+    def transfer(self, side, chunk, hop):
+        piece = self.at(self.line.ahead(1 - side, hop - 1), chunk)
+        return self.line.copy(piece, piece, self.sends, self.receives, (side, chunk, hop - 1), side)
+
+    def arrival(self, side, chunk, hop):
+        piece = self.at(self.line.ahead(1 - side, hop), chunk)
+        return self.line.copy(piece, piece, self.sends, self.receives, (side, chunk, hop - 1), side)
+
+    def send(self, chunk, hop):
+        line = self.line
+        for side in (0, 1):
+
+            @pl.when(line.next_there(side) & (line.place(side) >= hop - 1))
+            def _():
+                self.transfer(side, chunk, hop).start()
+
+    def receive(self, chunk, hop):
+        line = self.line
+        for side in (0, 1):
+
+            @pl.when(line.place(side) >= hop)
+            def _():
+                self.arrival(side, chunk, hop).wait_recv()
+
+    def step(self, chunk, hop):
+        line = self.line
+        for side in (0, 1):
+
+            @pl.when(line.place(side) >= hop)
+            def _():
+                self.arrival(side, chunk, hop).wait_recv()
+
+            if hop < line.count - 1:
+
+                @pl.when(line.next_there(side) & (line.place(side) >= hop))
+                def _():
+                    self.transfer(side, chunk, hop + 1).start()
+
+    def drain(self, chunk):
+        line = self.line
+        for hop in range(1, line.count):
+            for side in (0, 1):
+
+                @pl.when(line.next_there(side) & (line.place(side) >= hop - 1))
+                def _():
+                    self.transfer(side, chunk, hop).wait_send()
+
+
+def project(line, left, right, parts, rows, forward, block):
+    owner = jnp.where(line.me < line.count // 2, line.count - 1 - block, block)
+    at = pl.ds(pl.multiple_of(owner * rows, 16), rows)
+
+    def tile(index, carry):
+        lanes = pl.ds(pl.multiple_of(index * TILE, TILE), TILE)
+        if forward:
+            parts[at, lanes] = mm(left[at, :], right[:, lanes])
+        else:
+            parts[at, lanes] = mm_nt(left[at, :], right[lanes, :])
+        return carry
+
+    lax.fori_loop(0, parts.shape[1] // TILE, tile, 0)
+
+
+def relay(line, scatter, gather, chunks, lag, work, rows_done):
+    last = line.count - 1
+    work(0)
+    turns = lag * (chunks - 1) + last + 1 + (0 if gather is None else last)
+    for turn in range(turns):
+        for chunk in range(chunks):
+            hop = turn - lag * chunk + 1
+            if 1 <= hop <= last:
+                scatter.hop(chunk, hop)
+            elif hop == last + 1:
+                rows_done(chunk)
+                if gather is not None:
+                    gather.send(chunk, 1)
+            elif gather is not None and last + 1 < hop <= 2 * last + 1:
+                gather.step(chunk, hop - last - 1)
+        if turn == 0:
+            lax.fori_loop(1, line.count, lambda block, carry: (work(block), carry)[1], 0)
+    for chunk in range(chunks):
+        scatter.drain(chunk)
+        if gather is not None:
+            gather.drain(chunk)
+
+
+def norm_below(value, above, gain):
+    inverse = lax.rsqrt(jnp.mean(value * value, -1, keepdims=True) + EPSILON)
+    plain = value * inverse
+    scaled = above * gain
+    below = inverse * (scaled - plain * jnp.mean(scaled * plain, -1, keepdims=True))
+    return below, jnp.sum(above * plain, 0, keepdims=True)
+
+
+def mix_kernel(count, chunks, lag, rows, left, right, hidden, gain, out, middle, parts, total, slots, s0, s1, s2, s3):
+    line = Line(count)
+    span = rows // chunks
+    line.greet()
+    scatter = Scatter(line, parts, rows, span, slots, s0, s1)
+    gather = Gather(line, out, rows, span, s2, s3)
+
+    def rows_done(chunk):
+        at = pl.ds(chunk * span, span)
+        scatter.finish(chunk, total)
+        value = total[...] + hidden[at, :].astype(FULL)
+        middle[at, :] = value
+        inverse = lax.rsqrt(jnp.mean(value * value, -1, keepdims=True) + EPSILON)
+        gather.at(line.me, chunk)[...] = (value * inverse * gain[...]).astype(HALF)
+
+    relay(line, scatter, gather, chunks, lag, functools.partial(project, line, left, right, parts, rows, True), rows_done)
+
+
+def ffn_grad_kernel(count, chunks, lag, rows, left, right, middle, cotangent, gain, out, grad_middle, gain_grad, parts, total, slots, s0, s1, s2, s3):
+    line = Line(count)
+    span = rows // chunks
+    line.greet()
+    scatter = Scatter(line, parts, rows, span, slots, s0, s1)
+    gather = Gather(line, out, rows, span, s2, s3)
+    gain_grad[...] = jnp.zeros_like(gain_grad)
+
+    def rows_done(chunk):
+        at = pl.ds(chunk * span, span)
+        scatter.finish(chunk, total)
+        below, part = norm_below(middle[at, :], total[...], gain[...])
+        gain_grad[...] += part
+        result = cotangent[at, :].astype(FULL) + below
+        grad_middle[at, :] = result
+        gather.at(line.me, chunk)[...] = result.astype(HALF)
+
+    relay(line, scatter, gather, chunks, lag, functools.partial(project, line, left, right, parts, rows, False), rows_done)
+
+
+def relay_call(kernel, name, count, chunks, lag, collective, operands, rows, features, extra_out, flops):
+    span = rows // chunks
+    vmem = pl.BlockSpec(memory_space=pltpu.VMEM)
+    hops = count - 1
+    return pl.pallas_call(
+        functools.partial(kernel, count, chunks, lag, rows),
+        in_specs=[vmem] * len(operands),
+        out_specs=[vmem] * (1 + len(extra_out)),
+        out_shape=[jax.ShapeDtypeStruct((count * rows, features), HALF)] + extra_out,
+        scratch_shapes=[
+            pltpu.VMEM((count * rows, features), FULL),
+            pltpu.VMEM((span, features), FULL),
+            pltpu.VMEM((2, chunks, count, span, features), HALF),
+        ]
+        + [pltpu.SemaphoreType.DMA((2, chunks, hops))] * 4,
+        name=name,
+        cost_estimate=pl.CostEstimate(flops=flops, bytes_accessed=20_000_000, transcendentals=0),
+        compiler_params=pltpu.CompilerParams(
+            collective_id=collective, has_side_effects=True, vmem_limit_bytes=56 * 2**20
+        ),
+    )(*operands)
+
+
+def mix_rows(count, chunks, lag, branches, weight_out, hidden, gain):
+    rows, features = hidden.shape
+    return relay_call(
+        mix_kernel, "mix_rows", count, chunks, lag, 1, (branches, weight_out, hidden, gain), rows, features,
+        [jax.ShapeDtypeStruct((rows, features), FULL)], 100_000_000_000,
+    )
+
+
+def ffn_grad_rows(count, chunks, lag, grad_gate, weight_up, middle, cotangent, gain):
+    rows, features = middle.shape
+    return relay_call(
+        ffn_grad_kernel, "ffn_grad_rows", count, chunks, lag, 2, (grad_gate, weight_up, middle, cotangent, gain),
+        rows, features,
+        [jax.ShapeDtypeStruct((rows, features), FULL), jax.ShapeDtypeStruct((1, features), FULL)], 100_000_000_000,
+    )
+
+
+def gather_kernel(count, rows, own, out, own_sem, s0, s1):
+    line = Line(count)
+    keep = pltpu.make_async_copy(own, out.at[pl.ds(pl.multiple_of(line.me * rows, 16), rows), :], own_sem)
+    keep.start()
+    line.greet()
+    keep.wait()
+    gather = Gather(line, out, rows, rows, s0, s1)
+    gather.send(0, 1)
+    for hop in range(1, count):
+        gather.step(0, hop)
+    gather.drain(0)
+
+
+def line_gather(count, collective, own):
+    rows, features = own.shape
+    vmem = pl.BlockSpec(memory_space=pltpu.VMEM)
+    return pl.pallas_call(
+        functools.partial(gather_kernel, count, rows),
+        in_specs=[vmem],
+        out_specs=vmem,
+        out_shape=jax.ShapeDtypeStruct((count * rows, features), own.dtype),
+        scratch_shapes=[pltpu.SemaphoreType.DMA(())] + [pltpu.SemaphoreType.DMA((2, 1, count - 1))] * 2,
+        name="line_gather",
+        cost_estimate=pl.CostEstimate(flops=80_000_000_000, bytes_accessed=20_000_000, transcendentals=0),
+        compiler_params=pltpu.CompilerParams(
+            collective_id=collective, has_side_effects=True, vmem_limit_bytes=48 * 2**20
+        ),
+    )(own)
+
+
+def input_grad_kernel(count, chunks, lag, rows, left, right, hidden, grad_middle, gain, out, gain_grad, parts, total, slots, s0, s1):
+    line = Line(count)
+    span = rows // chunks
+    line.greet()
+    scatter = Scatter(line, parts, rows, span, slots, s0, s1)
+    gain_grad[...] = jnp.zeros_like(gain_grad)
+
+    def rows_done(chunk):
+        at = pl.ds(chunk * span, span)
+        scatter.finish(chunk, total)
+        value = hidden[at, :].astype(FULL)
+        below, part = norm_below(value, total[...], gain[...])
+        gain_grad[...] += part
+        out[at, :] = grad_middle[at, :] + below
+
+    relay(line, scatter, None, chunks, lag, functools.partial(project, line, left, right, parts, rows, False), rows_done)
+
+
+def input_grad_rows(count, chunks, lag, grads, weight_in, hidden, grad_middle, gain):
+    rows, features = hidden.shape
+    span = rows // chunks
+    vmem = pl.BlockSpec(memory_space=pltpu.VMEM)
+    operands = (grads, weight_in, hidden, grad_middle, gain)
+    return pl.pallas_call(
+        functools.partial(input_grad_kernel, count, chunks, lag, rows),
+        in_specs=[vmem] * len(operands),
+        out_specs=[vmem] * 2,
+        out_shape=[
+            jax.ShapeDtypeStruct((rows, features), FULL),
+            jax.ShapeDtypeStruct((1, features), FULL),
+        ],
+        scratch_shapes=[
+            pltpu.VMEM((count * rows, features), FULL),
+            pltpu.VMEM((span, features), FULL),
+            pltpu.VMEM((2, chunks, count, span, features), HALF),
+        ]
+        + [pltpu.SemaphoreType.DMA((2, chunks, count - 1))] * 2,
+        name="input_grad_rows",
+        cost_estimate=pl.CostEstimate(flops=80_000_000_000, bytes_accessed=20_000_000, transcendentals=0),
+        compiler_params=pltpu.CompilerParams(
+            collective_id=3, has_side_effects=True, vmem_limit_bytes=56 * 2**20
+        ),
+    )(*operands)
+
+
+CHUNKS = 4
+LAG = 2
+
+
 def gather_rows(pieces):
     return lax.all_gather(pieces, "tensor", axis=0, tiled=True)
 
@@ -468,12 +841,6 @@
     inverse = lax.rsqrt(jnp.mean(values * values, -1, keepdims=True) + EPSILON)
     plain = values * inverse
     return plain, inverse, plain * gain_vals
-
-
-def norm_backward(grad_above, plain, inverse, gain_vals):
-    grad_plain = grad_above * gain_vals
-    grad_below = inverse * (grad_plain - plain * jnp.mean(grad_plain * plain, -1, keepdims=True))
-    return grad_below, jnp.sum(grad_above * plain, 0)
 
 
 def silu_parts(gate_input):
@@ -510,6 +877,7 @@
     cotangent,
 ):
     tensor_index = lax.axis_index("tensor")
+    count = lax.axis_size("tensor")
     heads = decay_log.shape[0]
     width = mamba_in.shape[2]
     state_size = state_weight.shape[2]
@@ -541,7 +909,7 @@
         1,
     )
     weight_in = lax.all_gather(packed_in, "dp", axis=0, tiled=True)
-    hidden_rows = gather_rows(hidden_in)
+    hidden_rows = line_gather(count, 0, hidden_in)
     weight_out = lax.all_gather(jnp.concatenate([mamba_out, attn_out], 0), "dp", axis=1, tiled=True)
     weight_up = lax.all_gather(gate_up.reshape(block, 2 * units), "dp", axis=0, tiled=True)
     weight_down = lax.all_gather(down_weight, "dp", axis=1, tiled=True)
@@ -566,9 +934,7 @@
     gated_scale = gated_gain.astype(FULL)
     gated_plain = gated_vals * gated_inverse
     branches = jnp.concatenate([(gated_plain * gated_scale).astype(HALF), attended], 1)
-    middle = hidden_in.astype(FULL) + sum_rows(jnp.dot(branches, weight_out))
-    plain_two, inverse_two, scaled_two = norm_forward(middle, gain_two)
-    ffn_rows = gather_rows(scaled_two.astype(HALF))
+    ffn_rows, middle = mix_rows(count, CHUNKS, LAG, branches, weight_out, hidden_in, gain_two[None, :])
     gate_vals = jnp.dot(ffn_rows, weight_up, preferred_element_type=FULL)
     gate_part, up_part = gate_vals[:, :units], gate_vals[:, units:]
     silu_gate, silu_slope = silu_parts(gate_part)
@@ -577,17 +943,16 @@
     grad_gate = jnp.concatenate(
         [grad_act * up_part * silu_slope, grad_act * silu_gate], 1
     ).astype(HALF)
-    grad_ffn_in = sum_rows(dot_nt(grad_gate, weight_up).astype(HALF))
-    grad_middle_norm, ffn_gain_part = norm_backward(grad_ffn_in, plain_two, inverse_two, gain_two)
-    grad_middle = cotangent.astype(FULL) + grad_middle_norm
-    grad_mixed = gather_rows(grad_middle.astype(HALF))
-
+    up_grad = dot_tn(ffn_rows, grad_gate).astype(HALF)
+    down_grad = dot_tn(activated, grad_rows).astype(HALF)
+    grad_gate, up_grad, down_grad = lax.optimization_barrier((grad_gate, up_grad, down_grad))
+    gate_share = lax.psum_scatter(up_grad, "dp", scatter_dimension=0, tiled=True)
+    down_share = lax.psum_scatter(down_grad, "dp", scatter_dimension=1, tiled=True)
+    grad_mixed, grad_middle, ffn_gain_part = ffn_grad_rows(
+        count, CHUNKS, LAG, grad_gate, weight_up, middle, cotangent, gain_two[None, :]
+    )
     ffn_out = sum_rows(jnp.dot(activated, weight_down))
     hidden_out = (middle + ffn_out).astype(HALF)
-    up_grad = dot_tn(ffn_rows, grad_gate).astype(HALF)
-    down_grad = dot_tn(activated, grad_rows).astype(HALF)
-    gate_share = lax.psum_scatter(up_grad, "dp", scatter_dimension=0, tiled=True)
-    down_share = lax.psum_scatter(down_grad, "dp", scatter_dimension=1, tiled=True)
 
     grad_branches = dot_nt(grad_mixed, weight_out)
     out_grad = dot_tn(branches, grad_mixed).astype(HALF)
@@ -611,12 +976,12 @@
     grads = attend_backward(
         col, qheads, packed, attended, lse, grad_branches[:, width:], tables, segments, grads
     )
-    grad_first = sum_rows(dot_nt(grads, weight_in).astype(HALF))
-    in_grad = dot_tn(sequence, grads)
-    in_share = lax.psum_scatter(in_grad.astype(HALF), "dp", scatter_dimension=0, tiled=True)
-    plain_one, inverse_one, _ = norm_forward(hidden_in.astype(FULL), gain_one)
-    grad_hidden_norm, norm_gain_part = norm_backward(grad_first, plain_one, inverse_one, gain_one)
-    hidden_grad = grad_middle + grad_hidden_norm
+    in_grad = dot_tn(sequence, grads).astype(HALF)
+    grads, in_grad = lax.optimization_barrier((grads, in_grad))
+    in_share = lax.psum_scatter(in_grad, "dp", scatter_dimension=0, tiled=True)
+    hidden_grad, norm_gain_part = input_grad_rows(
+        count, 2, 1, grads, weight_in, hidden_in, grad_middle, gain_one[None, :]
+    )
 
     keyval_part = jnp.stack(
         [in_share[:, slice(*col.key)], in_share[:, slice(*col.value)]], 1
@@ -630,7 +995,7 @@
     state_weight_grad = shared[:, : 2 * state_size].reshape(state_weight.shape)
     keyval_weight_grad = shared[:, 2 * state_size :].reshape(keyval_weight.shape)
 
-    gains = lax.psum(jnp.stack([norm_gain_part, ffn_gain_part]), ("dp", "tensor"))
+    gains = lax.psum(jnp.concatenate([norm_gain_part, ffn_gain_part]), ("dp", "tensor"))
     dp_index = lax.axis_index("dp")
     gains = lax.dynamic_slice_in_dim(gains, dp_index * block, block, 1)
     head_sums = lax.psum(

time: 1240 us -> 893 us (0.72)
  waiting for transfers between devices: 835 us -> 74.4 us
  Pallas kernels: 53.6 us -> 529 us
  matrix products: 155 us -> 108 us
    pallas_call x0 -> x4, Pallas kernels: none -> 475 us  [the longest x2 313 us: relay_call(): pl.pallas_call(functools.partial(kernel, count, chunks, lag, rows), in_sp...]
    all_gather x4 -> x1, waiting for transfers between devices: 278 us -> 0.01 us  [gather_rows(): return lax.all_gather(pieces, 'tensor', axis=0, tiled=True)]
    reduce_scatter x4 -> x1, waiting for transfers between devices: 255 us -> 0.01 us  [sum_rows(): lax.psum_scatter(pieces, 'tensor', scatter_dimension=0, tiled=True)]
    all_gather x1, waiting for transfers between devices: 63.4 us -> 0.02 us  [body(): weight_in = lax.all_gather(packed_in, 'dp', axis=0, tiled=True)]
    all_gather x1, waiting for transfers between devices: 51.1 us -> 0.02 us  [body(): lax.all_gather(gate_up.reshape(block, 2 * units), 'dp', axis=0, tiled=True)]
    reduce_scatter x1, waiting for transfers between devices: 83.1 us -> 37.3 us  [body(): in_share = lax.psum_scatter(in_grad, 'dp', scatter_dimension=0, tiled=True)]
    all_gather x1, waiting for transfers between devices: 38 us -> 0.01 us  [body(): weight_down = lax.all_gather(down_weight, 'dp', axis=1, tiled=True)]
    dot_general x4 -> x2, matrix products: 52.2 us -> 21.2 us  [dot_nt(): return jnp.einsum('sb,ab->sa', a, b, preferred_element_type=FULL)]
  transfers between devices with their start and end apart: 17 -> 11, of which waited for: 14 -> 2; matrix products, arithmetic and copies ran while one was open for 14% -> 13% of each run, Pallas kernels for 4% -> 60%
where the time goes in v2:
time: 893 us; the launch traced here: 887 us
  Pallas kernels  529 us (59%)
  matrix products  108 us (12%)
  blocking collectives  87.1 us (10%)
  waiting for transfers between devices  74.4 us (8%)
  local copies, waits for them, and re-layouts  44.1 us (5%)
  other arithmetic  29.2 us (3%)
  between operations  15 us (2%)
    pallas_call x2, Pallas kernels, relay_call(): pl.pallas_call(functools.partial(kernel, count, chunks, lag, rows), in_sp...  313 us
    pallas_call x1, Pallas kernels, input_grad_rows(): pl.pallas_call(functools.partial(input_grad_kernel, count, chunks, lag, r...  88 us
    pallas_call x1, Pallas kernels, line_gather(): pl.pallas_call(functools.partial(gather_kernel, count, rows), in_specs=[v...  74.2 us
    dot_general x4, matrix products, dot_tn(): return jnp.einsum('sa,sb->ab', a, b, preferred_element_type=FULL)  44.1 us
    psum x1, blocking collectives, body(): lax.psum(jnp.concatenate([norm_gain_part, ffn_gain_part]), ('dp', 'tensor'))  38.6 us
    reduce_scatter x1, waiting for transfers between devices, body(): in_share = lax.psum_scatter(in_grad, 'dp', scatter_dimension=0, tiled=True)  37.3 us
    psum x1, waiting for transfers between devices, body(): lax.psum(jnp.concatenate([in_share[:, col.inmap[0]:col.outmap[1]], keyval...  35.2 us
    psum x1, blocking collectives, body(): lax.psum(jnp.sum(grad_mamba * gated_scale * gated_plain, -1), 'tensor')  26.7 us
  transfers between devices with their start and end apart: 11, of which 2 were waited for; matrix products, arithmetic and copies ran while one was open for 13% of the time, Pallas kernels for 60%

profile of v2, /device:TPU:0, one launch (start us, length us, event | category | flops | bytes accessed | tf_op | source)
XLA Modules:
  0.0 887.1 jit_solution(1923379890434488647)
XLA Ops:
  7.3 1.4 broadcast_in_dim.50
  8.7 1.4 copy.54
  10.1 1.4 broadcast_in_dim.51
  11.5 1.5 fusion.12
  13.0 2.8 fusion.10
  17.6 3.0 concatenate.28
  20.7 2.0 pad_maximum_fusion.4
  22.7 1.2 copy.80
  25.5 2.0 fusion.9
  27.5 74.2 %line_gather.1 = bf16[1024,2048]{1,0:T(8,128)(2,1)S(1)} custom-call(bf16[256,2048]{1,0:T(8,128)(2,1)S(1)} %copy-done.12), custom_call_target="tpu_custom_call" | custom-call | flops 80000000000 | bytes 20000000 | tf_op jit(solution)/shard_map/line_gather/pallas_call | solution.py:769
  104.1 2.6 convert_reduce_fusion
  106.7 19.0 %fusion.5.p_ref = f32[1024,2688]{1,0:T(8,128)} fusion(bf16[2048,2688]{1,0:T(8,128)(2,1)} %all-gather.6.cloned.1.call-done.right, bf16[1024,2048]{1,0:T(8,128)(2,1)} %copy-done, f32[2048]{0:T(1024)S(1)} %get-tuple-element.96, f32[1024]{0:T(1024)S(1)} %add_rsqrt_fusion.1), kind=kOutput, calls=%fused_computation.19 | convolution fusion | flops 11282677760 | bytes 26226688 | tf_op jit(solution)/shard_map/dot_general | solution.py:922
  125.7 15.9 %shard_map.305 = (f32[1024,768]{1,0:T(8,128)S(1)}, bf16[8,256,768]{2,1,0:T(8,128)(2,1)}, f32[1024,768]{1,0:T(8,128)}, f32[1024,128]{1,0:T(8,128)S(1)}) custom-call(f32[1024,2688]{1,0:T(8,128)} %fusion.5.p_ref, s32[1024,1]{1,0:T(8,128)S(1)} %copy.57.segc_ref.segb_ref, s32[8,1,128]{2,1,0:T(1,128)S(1)} %bitcast.55, f32[8,128]{1,0:T(8,128)S(1)} %select_maximum_fusion.head_ref), custom_call_target="tpu_custom_call" | custom-call | flops 6000000000 | bytes 30000000 | tf_op jit(solution)/shard_map/pallas_call | solution.py:157
  141.6 1.6 copy-done.13
  143.5 9.7 %psum.35 = f32[1024]{0:T(1024)S(1)} all-reduce(f32[1024]{0:T(1024)S(1)} %slice_reduce_fusion), channel_id=1, replica_groups=mesh['dp'=8,'tensor'=4] {'tensor'}, use_global_device_ids=true, to_apply=%region_1.2 | all-reduce | flops 1024 | bytes 8192 | tf_op jit(solution)/shard_map/psum | solution.py:931
  153.2 5.4 shard_map.306
  161.1 1.6 pad_maximum_fusion.1.left
  162.7 187.8 %mix_rows.1 = (bf16[1024,2048]{1,0:T(8,128)(2,1)}, f32[256,2048]{1,0:T(8,128)}) custom-call(bf16[1024,1024]{1,0:T(8,128)(2,1)} %pad_maximum_fusion.1.left, bf16[1024,2048]{1,0:T(8,128)(2,1)} %all-gather.8.cloned.1.call-done.right, bf16[256,2048]{1,0:T(8,128)(2,1)} %hidden.3, f32[1,2048]{1,0:T(1,128)} %bitcast.66), custom_call_target="tpu_custom_call" | custom-call | flops 99999997952 | bytes 20000000 | tf_op jit(solution)/shard_map/mix_rows/pallas_call | solution.py:717
  350.6 14.4 %fusion.15 = f32[1024,2048]{1,0:T(8,128)} fusion(bf16[1024,2048]{1,0:T(8,128)(2,1)} %get-tuple-element.43, bf16[2048,2048]{1,0:T(8,128)(2,1)} %all-gather.10.cloned.1.call-done.right), kind=kOutput, calls=%fused_computation.67 | convolution fusion | flops 8589934592 | bytes 20971520 | tf_op jit(solution)/shard_map/dot_general | solution.py:938
  365.0 13.2 %multiply_convert_fusion.1 = (bf16[1024,1024]{1,0:T(8,128)(2,1)S(1)}, bf16[1024,1024]{1,0:T(8,128)(2,1)S(1)}, bf16[1024,1024]{1,0:T(8,128)(2,1)}) fusion(f32[1024,2048]{1,0:T(8,128)} %fusion.15, bf16[1024,2048]{1,0:T(8,128)(2,1)} %all-gather.14.cloned.1.call-done, bf16[1024,2048]{1,0:T(8,128)(2,1)} %all-gather.12.cloned.1.call-done), kind=kOutput, calls=%fused_computation.9 | convolution fusion | flops 4310695936 | bytes 23068672 | tf_op jit(solution)/shard_map/sb,ab->sa/dot_general | solution.py:856
  378.2 1.4 copy-done.21
  380.2 12.0 %convolution_convert_fusion.1 = bf16[2048,2048]{1,0:T(8,128)(2,1)} fusion(bf16[1024,2048]{1,0:T(8,128)(2,1)S(1)} %copy-done.42, bf16[1024,1024]{1,0:T(8,128)(2,1)S(1)} %get-tuple-element.98, bf16[1024,1024]{1,0:T(8,128)(2,1)S(1)} %get-tuple-element.97), kind=kOutput, calls=%fused_computation.6 | convolution fusion | flops 8602517504 | bytes 16777216 | tf_op jit(solution)/shard_map/sa,sb->ab/dot_general | solution.py:852
  392.2 5.0 pad_maximum_fusion.left
  397.2 6.1 convolution_convert_fusion.3
  403.5 125.5 %ffn_grad_rows.1 = (bf16[1024,2048]{1,0:T(8,128)(2,1)}, f32[256,2048]{1,0:T(8,128)}, f32[1,2048]{1,0:T(1,128)}) custom-call(bf16[1024,2048]{1,0:T(8,128)(2,1)} %pad_maximum_fusion.left, bf16[2048,2048]{1,0:T(8,128)(2,1)} %all-gather.10.cloned.1.call-done.right, f32[256,2048]{1,0:T(8,128)} %get-tuple-element.42.middle, bf16[256,2048]{1,0:T(8,128)(2,1)} %cotangent.1, ...), custom_call_target="tpu_custom_call" | custom-call | flops 99999997952 | bytes 20000000 | tf_op jit(solution)/shard_map/ffn_grad_rows/pallas_call | solution.py:717
  529.0 8.4 convolution_convert_fusion.2
  537.5 9.4 %fusion.16 = bf16[1024,2048]{1,0:T(8,128)(2,1)} fusion(bf16[1024,1024]{1,0:T(8,128)(2,1)} %get-tuple-element.99, bf16[1024,2048]{1,0:T(8,128)(2,1)} %all-gather.12.cloned.1.call-done), kind=kOutput, calls=%fused_computation.68 | convolution fusion | flops 4294967296 | bytes 10485760 | tf_op jit(solution)/shard_map/dot_general | solution.py:954
  548.8 8.0 fusion.17
  557.0 2.4 multiply_reduce_fusion
  560.4 26.7 %psum.36.prod_ref = f32[1024,1]{1,0:T(8,128)} all-reduce(f32[1024,1]{1,0:T(8,128)} %copy.63), channel_id=1, replica_groups=mesh['dp'=8,'tensor'=4] {'tensor'}, use_global_device_ids=true, to_apply=%region_4.5 | all-reduce | flops 1024 | bytes 8192 | tf_op jit(solution)/shard_map/psum | solution.py:961
  589.2 1.9 copy-done.14
  591.1 24.2 %shard_map.307 = (bf16[1024,2688]{1,0:T(8,128)(2,1)}, f32[1,768]{1,0:T(1,128)S(1)}, f32[1,768]{1,0:T(1,128)S(1)}, f32[8,128]{1,0:T(8,128)S(1)}) custom-call(f32[1024,2688]{1,0:T(8,128)} %fusion.5.p_ref, f32[1024,768]{1,0:T(8,128)S(1)} %copy-done.14, bf16[8,256,768]{2,1,0:T(8,128)(2,1)} %get-tuple-element.48.states_ref, ...), custom_call_target="tpu_custom_call" | custom-call | flops 20000000000 | bytes 40000000 | tf_op jit(solution)/shard_map/pallas_call | solution.py:300
  615.3 7.7 shard_map.308.left
  623.0 17.6 %convolution_convert_fusion = bf16[2048,2688]{1,0:T(8,128)(2,1)} fusion(bf16[1024,2688]{1,0:T(8,128)(2,1)} %shard_map.308.left, bf16[1024,2048]{1,0:T(8,128)(2,1)S(1)} %copy-done.1, f32[2048]{0:T(1024)S(1)} %copy-done.31, f32[1024]{0:T(1024)S(1)} %copy-done.36), kind=kOutput, calls=%fused_computation | convolution fusion | flops 11288182784 | bytes 20721664 | tf_op jit(solution)/shard_map/sa,sb->ab/dot_general | solution.py:852
  641.0 12.1 %psum.39 = f32[804]{0:T(1024)S(1)} all-reduce(f32[804]{0:T(1024)S(1)} %pad_maximum_fusion.8), channel_id=1, replica_groups=mesh['dp'=8,'tensor'=4] {'dp'}, use_global_device_ids=true, to_apply=%region_9.10 | all-reduce | flops 804 | bytes 6432 | tf_op jit(solution)/shard_map/psum | solution.py:1001
  653.8 88.0 %input_grad_rows.1 = (f32[256,2048]{1,0:T(8,128)}, f32[1,2048]{1,0:T(1,128)}) custom-call(bf16[1024,2688]{1,0:T(8,128)(2,1)} %shard_map.308.left, bf16[2048,2688]{1,0:T(8,128)(2,1)} %all-gather.6.cloned.1.call-done.right, bf16[256,2048]{1,0:T(8,128)(2,1)} %hidden.3, f32[256,2048]{1,0:T(8,128)} %get-tuple-element.51.grad_middle, f32[1,2048]{1,0:T(1,128)} %bitcast.65), custom_call_target="tpu_custom_call" | custom-call | flops 80000000000 | bytes 20000000 | tf_op jit(solution)/shard_map/input_grad_rows/pallas_call | solution.py:806
  742.7 38.6 %psum.37 = f32[2,2048]{1,0:T(2,128)S(1)} all-reduce(f32[2,2048]{1,0:T(2,128)S(1)} %pad_maximum_fusion.7), channel_id=1, replica_groups=mesh['dp'=8,'tensor'=4] {'dp','tensor'}, use_global_device_ids=true, to_apply=%region_5.6 | all-reduce | flops 4096 | bytes 32768 | tf_op jit(solution)/shard_map/psum | solution.py:998
  782.5 2.1 convert_element_type.120
  784.6 1.6 slice_convert_fusion.1
  786.3 2.0 slice_convert_fusion
  788.2 2.5 add_convert_fusion
  790.7 4.1 reshape.108
  794.8 37.3 %reduce-scatter.8.cloned.1.call-done = bf16[256,2688]{1,0:T(8,128)(2,1)} async-done(((bf16[2048,2688]{1,0:T(8,128)(2,1)}), bf16[256,2688]{1,0:T(8,128)(2,1)}) %reduce-scatter.8.cloned.1.call-update) | async-done | bytes 1376272 | tf_op jit(solution)/shard_map/reduce_scatter | solution.py:981
  837.1 2.4 copy.69
  840.2 35.2 %all-reduce.3.cloned.1.call-done = bf16[256,1024]{1,0:T(8,128)(2,1)} async-done(((bf16[256,1024]{1,0:T(8,128)(2,1)}), bf16[256,1024]{1,0:T(8,128)(2,1)}) %all-reduce.3.cloned.1.call-update) | async-done | bytes 524304 | tf_op jit(solution)/shard_map/psum | solution.py:992
  875.4 1.1 fusion.11
  876.5 1.1 reshape.104
  878.8 1.3 copy.93
  (156 shorter events, 24.2 us)
Async XLA Ops:
  7.2 8.6 copy-start.25
  7.2 96.9 %all-gather.6.cloned.1.call-start = ((), (), s32[]{:S(2)}) async-start(), calls=%async_computation.5 | async-start | bytes 12386304 | tf_op jit(solution)/shard_map/all_gather | solution.py:911
  17.5 5.2 copy-start.24
  20.6 4.6 copy-start.32
  20.6 4.7 copy-start.8
  20.6 6.9 copy-start.12
  20.6 142.1 %all-gather.8.cloned.1.call-start = ((), (), s32[]{:S(2)}) async-start(), calls=%async_computation.6 | async-start | bytes 4718592 | tf_op jit(solution)/shard_map/all_gather | solution.py:913
  22.7 327.9 %all-gather.10.cloned.1.call-start = ((), (), s32[]{:S(2)}) async-start(), calls=%async_computation.7 | async-start | bytes 9437184 | tf_op jit(solution)/shard_map/all_gather | solution.py:914
  24.0 341.0 %all-gather.14.cloned.1.call-start = ((), (), s32[]{:S(2)}) async-start(), calls=%async_computation.10 | async-start | bytes 5242880 | tf_op jit(solution)/shard_map/all_gather | solution.py:833
  24.6 340.5 %all-gather.12.cloned.1.call-start = ((), (), s32[]{:S(2)}) async-start(), calls=%async_computation.8 | async-start | bytes 4718592 | tf_op jit(solution)/shard_map/all_gather | solution.py:915
  25.2 757.3 %reduce-scatter.14.cloned.1.call-start = ((), (), s32[]{:S(2)}) async-start(), calls=%async_computation.15 | async-start | bytes 4718592 | tf_op jit(solution)/shard_map/reduce_scatter | solution.py:950
  25.2 134.4 %copy-start.28 = (f32[768]{0:T(1024)}, f32[768]{0:T(1024)S(1)}, u32[]{:S(2)}) copy-start(f32[768]{0:T(1024)S(1)} %convert_element_type.99) | copy-start | bytes 9220
  101.7 2.0 copy-start
  102.6 23.1 %copy-start.35 = (f32[1024]{0:T(1024)}, f32[1024]{0:T(1024)S(1)}, u32[]{:S(2)}) copy-start(f32[1024]{0:T(1024)S(1)} %add_rsqrt_fusion.1) | copy-start | bytes 12292
  102.7 23.0 %copy-start.10 = (f32[8,128]{1,0:T(8,128)}, f32[8,128]{1,0:T(8,128)S(1)}, u32[]{:S(2)}) copy-start(f32[8,128]{1,0:T(8,128)S(1)} %select_maximum_fusion.head_ref) | copy-start | bytes 12292
  106.7 19.0 %copy-start.30 = (f32[2048]{0:T(1024)}, f32[2048]{0:T(1024)S(1)}, u32[]{:S(2)}) copy-start(f32[2048]{0:T(1024)S(1)} %get-tuple-element.96) | copy-start | bytes 24580
  141.6 1.6 copy-start.13
  153.2 6.4 copy-start.26
  153.2 6.4 copy-start.15
  158.6 1.0 copy-start.4
  160.0 1.1 copy-start.17
  365.0 15.2 %copy-start.42 = (bf16[1024,2048]{1,0:T(8,128)(2,1)S(1)}, bf16[1024,2048]{1,0:T(8,128)(2,1)}, u32[]{:S(2)}) copy-start(bf16[1024,2048]{1,0:T(8,128)(2,1)} %get-tuple-element.43) | copy-start | bytes 12582916
  378.2 1.4 copy-start.21
  378.2 2.0 copy-start.22
  392.2 5.0 copy-start.40
  392.2 5.0 copy-start.41
  403.4 381.2 %reduce-scatter.10.cloned.1.call-start = ((), (), s32[]{:S(2)}) async-start(), calls=%async_computation.13 | async-start | bytes 4718592 | tf_op jit(solution)/shard_map/reduce_scatter | solution.py:959
  403.4 125.5 %copy-start.3 = (bf16[1024,256]{1,0:T(8,128)(2,1)S(1)}, bf16[1024,256]{1,0:T(8,128)(2,1)}, u32[]{:S(2)}) copy-start(bf16[1024,256]{1,0:T(8,128)(2,1)} %copy-done.2) | copy-start | bytes 1572868
  403.5 125.5 %copy-start.18 = (bf16[1024,768]{1,0:T(8,128)(2,1)S(1)}, bf16[1024,768]{1,0:T(8,128)(2,1)}, u32[]{:S(2)}) copy-start(bf16[1024,768]{1,0:T(8,128)(2,1)} %copy-done.17) | copy-start | bytes 4718596
  537.4 250.8 %reduce-scatter.6.cloned.1.call-start = ((), (), s32[]{:S(2)}) async-start(), calls=%async_computation.9 | async-start | bytes 5242880 | tf_op jit(solution)/shard_map/reduce_scatter | solution.py:837
  546.9 243.8 %reduce-scatter.12.cloned.1.call-start = ((), (), s32[]{:S(2)}) async-start(), calls=%async_computation.14 | async-start | bytes 9437184 | tf_op jit(solution)/shard_map/reduce_scatter | solution.py:949
  547.6 284.4 %reduce-scatter.8.cloned.1.call-start = ((), (), s32[]{:S(2)}) async-start(), calls=%async_computation.11 | async-start | bytes 12386304 | tf_op jit(solution)/shard_map/reduce_scatter | solution.py:981
  548.8 8.2 copy-start.16
  548.8 8.2 copy-start.29
  556.9 30.2 %copy-start.9 = (s32[1024]{0:T(1024)S(1)}, s32[1024]{0:T(1024)}, u32[]{:S(2)}) copy-start(s32[1024]{0:T(1024)} %param.19) | copy-start | bytes 12292
  556.9 30.2 %copy-start.11 = (f32[8,128]{1,0:T(8,128)S(1)}, f32[8,128]{1,0:T(8,128)}, u32[]{:S(2)}) copy-start(f32[8,128]{1,0:T(8,128)} %copy-done.10) | copy-start | bytes 12292
  587.1 1.0 copy-start.6
  588.1 1.0 copy-start.7
  589.2 1.9 copy-start.14
  591.1 24.2 %copy-start.5 = (f32[1024,256]{1,0:T(8,128)S(1)}, f32[1024,256]{1,0:T(8,128)}, u32[]{:S(2)}) copy-start(f32[1024,256]{1,0:T(8,128)} %copy-done.4) | copy-start | bytes 3145732
  615.3 7.7 copy-start.1
  615.3 7.7 copy-start.31
  615.3 7.7 copy-start.36
  640.6 234.7 %all-reduce.3.cloned.1.call-start = ((), (), s32[]{:S(2)}) async-start(), calls=%async_computation.12 | async-start | bytes 1048576 | tf_op jit(solution)/shard_map/psum | solution.py:992
  653.8 88.0 %copy-start.34 = (f32[1,2048]{1,0:T(1,128)S(1)}, f32[1,2048]{1,0:T(1,128)}, u32[]{:S(2)}) copy-start(f32[1,2048]{1,0:T(1,128)} %get-tuple-element.54) | copy-start | bytes 24580
  741.8 46.4 %copy-start.19 = (f32[256,2048]{1,0:T(8,128)S(1)}, f32[256,2048]{1,0:T(8,128)}, u32[]{:S(2)}) copy-start(f32[256,2048]{1,0:T(8,128)} %get-tuple-element.42.middle) | copy-start | bytes 6291460
  832.1 4.8 copy-start.23
  837.1 41.6 %copy-start.20 = (f32[256,2048]{1,0:T(8,128)S(1)}, f32[256,2048]{1,0:T(8,128)}, u32[]{:S(2)}) copy-start(f32[256,2048]{1,0:T(8,128)} %get-tuple-element.150) | copy-start | bytes 6291460
  (6 other events, 5.3 us)
Sparse Core Ops, SparseCore 0:
  20.7 68.1 all-gather.5
  91.4 37.4 all-gather.7
  131.3 54.3 all-gather.9
  187.2 122.4 all-gather.13
  311.4 37.8 all-gather.11
  403.5 49.5 reduce-scatter.13
  537.6 50.6 reduce-scatter.9
  590.6 76.7 reduce-scatter.5
  671.2 72.9 reduce-scatter.11
  747.6 84.4 reduce-scatter.7
  837.1 38.2 all-reduce.2

commit v3 on v2

--- a/solution.py
+++ b/solution.py
@@ -51,6 +51,14 @@
     return jnp.where(iota((size, LANES), 1) < HEAD_DIM, left, right)
 
 
+def as_row(values):
+    return jnp.broadcast_to(values, (LANES, LANES)).T[0:1, :]
+
+
+def as_column(values):
+    return jnp.broadcast_to(values, (LANES, LANES)).T[:, 0:1]
+
+
 def stacked_pair(pair):
     low = iota(pair.shape, 1) < HEAD_DIM
     zero = jnp.zeros_like(pair)
@@ -71,7 +79,7 @@
         self.outmap = (start + state, start + 2 * state)
         start += 2 * state
         self.step = (start, start + LANES)
-        self.total = start + LANES
+        self.total = start + 2 * LANES
 
 
 def stretch_common(col, packed, segc_ref, segr_ref, head_ref, before):
@@ -146,7 +154,7 @@
         gated = (result + skip * drive) * (gate * sigmoid(gate))
         gated_ref[:, lanes] = gated
         square = square + jnp.sum(gated * gated, 1, keepdims=True)
-    square_ref[...] = jnp.broadcast_to(square, square_ref.shape)
+    square_ref[pl.ds(index, 1), :] = as_row(square)
     before[...] = segc_ref[span - 1 : span, :]
 
 
@@ -167,23 +175,24 @@
             pl.BlockSpec((STRETCH, width), lambda i: (i, 0)),
             pl.BlockSpec((1, state_size, width), lambda i: (i, 0, 0)),
             pl.BlockSpec((STRETCH, width), lambda i: (i, 0)),
-            pl.BlockSpec((STRETCH, LANES), lambda i: (i, 0)),
+            pl.BlockSpec((count, LANES), lambda i: (0, 0)),
         ],
         out_shape=[
             jax.ShapeDtypeStruct((length, width), FULL),
             jax.ShapeDtypeStruct((count, state_size, width), HALF),
             jax.ShapeDtypeStruct((length, width), FULL),
-            jax.ShapeDtypeStruct((length, LANES), FULL),
+            jax.ShapeDtypeStruct((count, LANES), FULL),
         ],
         scratch_shapes=[pltpu.VMEM((state_size, width), FULL), pltpu.VMEM((1, 1), jnp.int32)],
-        cost_estimate=pl.CostEstimate(flops=6_000_000_000, bytes_accessed=30_000_000, transcendentals=0),
+        name="scan_forward",
+        cost_estimate=pl.CostEstimate(flops=16_000_000_000, bytes_accessed=30_000_000, transcendentals=0),
         compiler_params=pltpu.CompilerParams(vmem_limit_bytes=48 * 2**20),
     )(packed, segments[:, None], segments.reshape(count, 1, STRETCH), head_params)
 
 
 def scan_backward_kernel(
     col, heads, total_width, p_ref, y_ref, states_ref, gm_ref, inv_ref, prod_ref, gain_ref,
-    segc_ref, segr_ref, segb_ref, head_ref, g_ref, gain_grad_ref, skip_grad_ref, head_grad_ref, future,
+    segc_ref, segr_ref, segb_ref, head_ref, ag_ref, g_ref, gain_grad_ref, skip_grad_ref, head_grad_ref, future,
 ):
     step_index = pl.program_id(0)
     count = pl.num_programs(0)
@@ -212,7 +221,9 @@
     grad_running = jnp.zeros((span, LANES), FULL)
     grad_step = jnp.zeros((span, LANES), FULL)
     grad_last = jnp.zeros((1, LANES), FULL)
-    inverse, product = inv_ref[:, 0:1], prod_ref[:, 0:1] * (1.0 / total_width)
+    chunk = pl.ds(count - 1 - step_index, 1)
+    inverse = as_column(lax.rsqrt(inv_ref[chunk, :] * (1.0 / total_width) + EPSILON))
+    product = as_column(prod_ref[chunk, :] * (1.0 / total_width))
     for pair in range(heads // 2):
         at = pair * LANES
         lanes = slice(at, at + LANES)
@@ -287,12 +298,15 @@
     grad_raw = (grad_step - grad_keep * jnp.exp(head_ref[0:1, :])) * sigmoid(raw)
     grad_raw = jnp.where(lane < heads, grad_raw, 0.0)
     g_ref[:, col.step[0] : col.step[1]] = grad_raw.astype(HALF)
-    g_ref[:, 0 : col.attention] = jnp.zeros((span, col.attention), HALF)
+    g_ref[:, col.step[1] : col.total] = jnp.zeros((span, col.total - col.step[1]), HALF)
+    g_ref[:, 0 : col.attention] = ag_ref[...]
     head_grad_ref[0:1, :] += jnp.sum(keep * grad_keep, 0, keepdims=True)
     head_grad_ref[1:2, :] += jnp.sum(grad_raw, 0, keepdims=True)
 
 
-def scan_backward(col, heads, state_size, packed, y, states, grad_mamba, inverse, product, gain, segments, head_params):
+def scan_backward(
+    col, heads, state_size, packed, y, states, grad_mamba, squares, product, gain, segments, head_params, attention_grads
+):
     length = packed.shape[0]
     width = heads * HEAD_DIM
     count = length // STRETCH
@@ -305,13 +319,14 @@
             pl.BlockSpec((STRETCH, width), back),
             pl.BlockSpec((1, state_size, width), lambda i: (count - 1 - i, 0, 0)),
             pl.BlockSpec((STRETCH, width), back),
-            pl.BlockSpec((STRETCH, 1), back),
-            pl.BlockSpec((STRETCH, 1), back),
+            pl.BlockSpec((count, LANES), lambda i: (0, 0)),
+            pl.BlockSpec((count, LANES), lambda i: (0, 0)),
             pl.BlockSpec((1, width), lambda i: (0, 0)),
             pl.BlockSpec((STRETCH, 1), back),
             pl.BlockSpec((1, 1, STRETCH), lambda i: (count - 1 - i, 0, 0)),
             pl.BlockSpec((STRETCH, 1), lambda i: (jnp.maximum(count - 2 - i, 0), 0)),
             pl.BlockSpec((8, LANES), lambda i: (0, 0)),
+            pl.BlockSpec((STRETCH, col.attention), back),
         ],
         out_specs=[
             pl.BlockSpec((STRETCH, col.total), back),
@@ -326,11 +341,12 @@
             jax.ShapeDtypeStruct((8, LANES), FULL),
         ],
         scratch_shapes=[pltpu.VMEM((state_size, width), FULL)],
-        cost_estimate=pl.CostEstimate(flops=20_000_000_000, bytes_accessed=40_000_000, transcendentals=0),
+        name="scan_backward",
+        cost_estimate=pl.CostEstimate(flops=24_000_000_000, bytes_accessed=40_000_000, transcendentals=0),
         compiler_params=pltpu.CompilerParams(vmem_limit_bytes=48 * 2**20),
     )(
-        packed, y, states, grad_mamba, inverse, product, gain, segments[:, None],
-        segments.reshape(count, 1, STRETCH), segments[:, None], head_params,
+        packed, y, states, grad_mamba, squares, product, gain, segments[:, None],
+        segments.reshape(count, 1, STRETCH), segments[:, None], head_params, attention_grads,
     )
 
 
@@ -338,8 +354,11 @@
     return values * cosine + pltpu.roll(values, ATT_DIM // 2, 1) * sine
 
 
-def attend_forward_kernel(col, heads, p_ref, cos_ref, sin_ref, segc_ref, segr_ref, out_ref, lse_ref):
+def attend_forward_kernel(
+    col, heads, peers, p_ref, cos_ref, sin_ref, segc_ref, segr_ref, own_ref, out_ref, lse_ref, sum_ref, held, sends, receives
+):
     length = p_ref.shape[0]
+    finish = spread(peers, own_ref, held, sends, receives)
     scale = 1.0 / math.sqrt(ATT_DIM)
     keys = turned(p_ref[:, col.key[0] : col.key[1]], cos_ref[...], sin_ref[...]).astype(HALF)
     values = p_ref[:, col.value[0] : col.value[1]].astype(HALF)
@@ -358,13 +377,52 @@
             total = jnp.sum(weights, 1, keepdims=True)
             out_ref[rows, lanes] = (mm(weights.astype(HALF), values[:end]) / total).astype(HALF)
             lse_ref[rows, lanes] = jnp.broadcast_to(highest + jnp.log(total), (ATT_BLOCK, ATT_DIM))
-
-
-def attend_forward(col, heads, packed, tables, segments):
+    finish(sum_ref)
+
+
+def exchange_scratch(peers, shape):
+    return [
+        pltpu.VMEM((peers,) + shape, FULL),
+        pltpu.SemaphoreType.DMA((peers,)),
+        pltpu.SemaphoreType.DMA((peers,)),
+    ]
+
+
+def spread(peers, own_ref, held, sends, receives):
+    me = lax.axis_index("tensor")
+    barrier = pltpu.get_barrier_semaphore()
+    others = [lax.rem(me + distance, peers) for distance in range(1, peers)]
+    for other in others:
+        pl.semaphore_signal(barrier, inc=1, device_id={"tensor": other}, device_id_type=pl.DeviceIdType.MESH)
+    pl.semaphore_wait(barrier, peers - 1)
+
+    def copy(distance):
+        return pltpu.make_async_remote_copy(
+            src_ref=own_ref,
+            dst_ref=held.at[distance],
+            send_sem=sends.at[distance],
+            recv_sem=receives.at[distance],
+            device_id={"tensor": others[distance - 1]},
+            device_id_type=pl.DeviceIdType.MESH,
+        )
+
+    for distance in range(1, peers):
+        copy(distance).start()
+
+    def finish(sum_ref):
+        sum_ref[...] = own_ref[...]
+        for distance in range(1, peers):
+            copy(distance).wait()
+            sum_ref[...] += held[distance]
+
+    return finish
+
+
+def attend_forward(col, heads, peers, packed, tables, segments, own):
     length = packed.shape[0]
     whole = lambda i: (0, 0)
     return pl.pallas_call(
-        functools.partial(attend_forward_kernel, col, heads),
+        functools.partial(attend_forward_kernel, col, heads, peers),
         grid=(1,),
         in_specs=[
             pl.BlockSpec((length, col.attention), whole),
@@ -372,25 +430,33 @@
             pl.BlockSpec((length, ATT_DIM), whole),
             pl.BlockSpec((length, 1), whole),
             pl.BlockSpec((1, length), whole),
+            pl.BlockSpec(own.shape, whole),
         ],
         out_specs=[
             pl.BlockSpec((length, heads * ATT_DIM), whole),
             pl.BlockSpec((length, heads * ATT_DIM), whole),
+            pl.BlockSpec(own.shape, whole),
         ],
         out_shape=[
             jax.ShapeDtypeStruct((length, heads * ATT_DIM), HALF),
             jax.ShapeDtypeStruct((length, heads * ATT_DIM), FULL),
+            jax.ShapeDtypeStruct(own.shape, FULL),
         ],
-        cost_estimate=pl.CostEstimate(flops=2_000_000_000, bytes_accessed=5_000_000, transcendentals=2_000_000),
-        compiler_params=pltpu.CompilerParams(vmem_limit_bytes=48 * 2**20),
-    )(packed, tables[0], tables[1], segments[:, None], segments[None, :])
+        scratch_shapes=exchange_scratch(peers, own.shape),
+        name="attend_forward",
+        cost_estimate=pl.CostEstimate(flops=6_000_000_000, bytes_accessed=5_000_000, transcendentals=2_000_000),
+        compiler_params=pltpu.CompilerParams(
+            vmem_limit_bytes=48 * 2**20, collective_id=4, has_side_effects=True
+        ),
+    )(packed, tables[0], tables[1], segments[:, None], segments[None, :], own)
 
 
 def attend_backward_kernel(
-    col, heads, p_ref, out_ref, lse_ref, go_ref, cos_ref, sin_ref, segc_ref, segr_ref, g_in_ref, g_ref,
-    key_grad, value_grad,
+    col, heads, peers, p_ref, out_ref, lse_ref, go_ref, cos_ref, sin_ref, segc_ref, segr_ref, own_ref, g_ref, sum_ref,
+    key_grad, value_grad, held, sends, receives,
 ):
     length = p_ref.shape[0]
+    finish = spread(peers, own_ref, held, sends, receives)
     scale = 1.0 / math.sqrt(ATT_DIM)
     keys = turned(p_ref[:, col.key[0] : col.key[1]], cos_ref[...], sin_ref[...]).astype(HALF)
     values = p_ref[:, col.value[0] : col.value[1]].astype(HALF)
@@ -416,34 +482,41 @@
             g_ref[rows, lanes] = turned(grad_query, cosine, -sine).astype(HALF)
     g_ref[:, col.key[0] : col.key[1]] = turned(key_grad[...], cos_ref[...], -sin_ref[...]).astype(HALF)
     g_ref[:, col.value[0] : col.value[1]] = value_grad[...].astype(HALF)
-
-
-def attend_backward(col, heads, packed, attended, lse, grad_attended, tables, segments, grads):
+    finish(sum_ref)
+
+
+def attend_backward(col, heads, peers, packed, attended, lse, grad_branches, tables, segments, own):
     length = packed.shape[0]
     width = heads * ATT_DIM
     whole = lambda i: (0, 0)
     return pl.pallas_call(
-        functools.partial(attend_backward_kernel, col, heads),
+        functools.partial(attend_backward_kernel, col, heads, peers),
         grid=(1,),
         in_specs=[
             pl.BlockSpec((length, col.attention), whole),
             pl.BlockSpec((length, width), whole),
             pl.BlockSpec((length, width), whole),
-            pl.BlockSpec((length, width), whole),
+            pl.BlockSpec((length, width), lambda i: (0, grad_branches.shape[1] // width - 1)),
             pl.BlockSpec((length, ATT_DIM), whole),
             pl.BlockSpec((length, ATT_DIM), whole),
             pl.BlockSpec((length, 1), whole),
             pl.BlockSpec((1, length), whole),
-            pl.BlockSpec(memory_space=pl.ANY),
+            pl.BlockSpec(own.shape, whole),
         ],
-        out_specs=pl.BlockSpec((length, col.attention), whole),
-        out_shape=jax.ShapeDtypeStruct(grads.shape, grads.dtype),
-        scratch_shapes=[pltpu.VMEM((length, ATT_DIM), FULL), pltpu.VMEM((length, ATT_DIM), FULL)],
-        input_output_aliases={8: 0},
-        cost_estimate=pl.CostEstimate(flops=5_000_000_000, bytes_accessed=10_000_000, transcendentals=2_000_000),
-        compiler_params=pltpu.CompilerParams(vmem_limit_bytes=48 * 2**20),
+        out_specs=[pl.BlockSpec((length, col.attention), whole), pl.BlockSpec(own.shape, whole)],
+        out_shape=[
+            jax.ShapeDtypeStruct((length, col.attention), HALF),
+            jax.ShapeDtypeStruct(own.shape, FULL),
+        ],
+        scratch_shapes=[pltpu.VMEM((length, ATT_DIM), FULL), pltpu.VMEM((length, ATT_DIM), FULL)]
+        + exchange_scratch(peers, own.shape),
+        name="attend_backward",
+        cost_estimate=pl.CostEstimate(flops=8_000_000_000, bytes_accessed=10_000_000, transcendentals=2_000_000),
+        compiler_params=pltpu.CompilerParams(
+            vmem_limit_bytes=48 * 2**20, collective_id=5, has_side_effects=True
+        ),
     )(
-        packed, attended, lse, grad_attended, tables[0], tables[1], segments[:, None], segments[None, :], grads
+        packed, attended, lse, grad_branches, tables[0], tables[1], segments[:, None], segments[None, :], own
     )
 
 
@@ -456,6 +529,187 @@
     return jnp.concatenate([cosine, cosine], 1), jnp.concatenate([-sine, sine], 1)
 
 
+def weight_grads_kernel(first, left_one, left_two, right_one, right_two, out):
+    index = pl.program_id(0)
+
+    @pl.when(index < first)
+    def _():
+        out[...] = mm_tn(left_one[...], right_one[...]).astype(out.dtype)
+
+    @pl.when(index >= first)
+    def _():
+        out[...] = mm_tn(left_two[...], right_two[...]).astype(out.dtype)
+
+
+def weight_grads(left_one, right_one, left_two, right_two, name):
+    length, features = left_one.shape
+    one, two = right_one.shape[1], right_two.shape[1]
+    tile = max(size for size in (512, 256, 128) if one % size == 0 and two % size == 0)
+    first = one // tile
+    return pl.pallas_call(
+        functools.partial(weight_grads_kernel, first),
+        grid=((one + two) // tile,),
+        in_specs=[
+            pl.BlockSpec((length, features), lambda i: (0, 0)),
+            pl.BlockSpec((length, features), lambda i: (0, 0)),
+            pl.BlockSpec((length, tile), lambda i: (0, jnp.minimum(i, first - 1))),
+            pl.BlockSpec((length, tile), lambda i: (0, jnp.maximum(i - first, 0))),
+        ],
+        out_specs=pl.BlockSpec((features, tile), lambda i: (0, i)),
+        out_shape=jax.ShapeDtypeStruct((features, one + two), HALF),
+        name=name,
+        cost_estimate=pl.CostEstimate(
+            flops=2 * length * features * (one + two), bytes_accessed=40_000_000, transcendentals=0
+        ),
+        compiler_params=pltpu.CompilerParams(vmem_limit_bytes=56 * 2**20),
+    )(left_one, left_two, right_one, right_two)
+
+
+class Plane:
+    def __init__(self, peers, source, whole, sends, receives):
+        self.peers, self.source, self.whole = peers, source, whole
+        self.sends, self.receives = sends, receives
+        self.me = lax.axis_index("dp")
+        self.rows = source.shape[0]
+        self.width = source.shape[1]
+        self.half = self.width // (2 * LANES) * LANES
+        outer = [1 << bit for bit in range(1, peers.bit_length() - 1)]
+        self.orders = [outer, outer[::-1]]
+        self.steps = len(outer)
+
+    def greet(self, barrier):
+        for bit in [1] + self.orders[0]:
+            pl.semaphore_signal(
+                barrier, inc=1, device_id={"dp": self.me ^ bit}, device_id_type=MESH
+            )
+        return 1 + self.steps
+
+    def held(self, side, step):
+        order = self.orders[side]
+        if step == 0:
+            return [0]
+        bit, before = order[step - 1], [0]
+        for earlier in order[: step - 1]:
+            before = before + [offset ^ earlier for offset in before]
+        return [offset ^ bit for offset in before]
+
+    def lanes(self, side):
+        return pl.ds(0, self.half) if side == 0 else pl.ds(self.half, self.width - self.half)
+
+    def block(self, side, offset):
+        at = pl.ds(pl.multiple_of((self.me ^ offset) * self.rows, 16), self.rows)
+        return self.whole.at[at, self.lanes(side)]
+
+    def copy(self, side, bit, offset):
+        source = self.source.at[:, self.lanes(side)] if offset == 0 else self.block(side, offset)
+        at = (side, bit.bit_length() - 1, offset)
+        return pltpu.make_async_remote_copy(
+            src_ref=source,
+            dst_ref=self.block(side, offset),
+            send_sem=self.sends.at[at],
+            recv_sem=self.receives.at[at],
+            device_id={"dp": self.me ^ bit},
+            device_id_type=MESH,
+        )
+
+    def arrival(self, side, bit, offset):
+        at = (side, bit.bit_length() - 1, offset)
+        return pltpu.make_async_remote_copy(
+            src_ref=self.block(side, offset ^ bit),
+            dst_ref=self.block(side, offset ^ bit),
+            send_sem=self.sends.at[at],
+            recv_sem=self.receives.at[at],
+            device_id={"dp": self.me ^ bit},
+            device_id_type=MESH,
+        )
+
+    def sent(self, side, step):
+        blocks = []
+        for earlier in range(step):
+            blocks += self.held(side, earlier)
+        return blocks
+
+    def start(self):
+        for side in (0, 1):
+            if self.steps:
+                self.copy(side, self.orders[side][0], 0).start()
+        for side in (0, 1):
+            self.copy(side, 1, 0).start()
+
+    def advance(self, step):
+        for side in (0, 1):
+            bit = self.orders[side][step - 1]
+            for offset in self.held(side, step):
+                self.arrival(side, bit, offset ^ bit).wait_recv()
+        for side in (0, 1):
+            if step < self.steps:
+                following = self.orders[side][step]
+                for offset in self.sent(side, step + 1):
+                    self.copy(side, following, offset).start()
+        for side in (0, 1):
+            for offset in self.held(side, step):
+                self.copy(side, 1, offset).start()
+
+    def finish(self):
+        for side in (0, 1):
+            for offset in self.sent(side, self.steps + 1):
+                self.arrival(side, 1, offset).wait_recv()
+
+    def drain(self):
+        for side in (0, 1):
+            for offset in self.sent(side, self.steps + 1):
+                self.copy(side, 1, offset).wait_send()
+            for step in range(1, self.steps + 1):
+                for offset in self.sent(side, step):
+                    self.copy(side, self.orders[side][step - 1], offset).wait_send()
+
+
+class Swarm:
+    def __init__(self, peers, count):
+        self.peers, self.count = peers, count
+        self.at_dp, self.at_tensor = lax.axis_index("dp"), lax.axis_index("tensor")
+
+    def greet(self):
+        barrier = pltpu.get_barrier_semaphore()
+        for offset in range(1, self.peers):
+            pl.semaphore_signal(barrier, inc=1, device_id={"dp": self.at_dp ^ offset}, device_id_type=MESH)
+        for distance in range(1, self.count):
+            pl.semaphore_signal(
+                barrier, inc=1, device_id={"tensor": lax.rem(self.at_tensor + distance, self.count)}, device_id_type=MESH
+            )
+        pl.semaphore_wait(barrier, self.peers + self.count - 2)
+
+    def along_dp(self, source_of, held, sends, receives):
+        return [
+            pltpu.make_async_remote_copy(
+                src_ref=source_of(self.at_dp ^ offset),
+                dst_ref=held.at[offset],
+                send_sem=sends.at[offset],
+                recv_sem=receives.at[offset],
+                device_id={"dp": self.at_dp ^ offset},
+                device_id_type=MESH,
+            )
+            for offset in range(1, self.peers)
+        ]
+
+    def along_tensor(self, source, held, sends, receives):
+        return [
+            pltpu.make_async_remote_copy(
+                src_ref=source,
+                dst_ref=held.at[distance],
+                send_sem=sends.at[distance],
+                recv_sem=receives.at[distance],
+                device_id={"tensor": lax.rem(self.at_tensor + distance, self.count)},
+                device_id_type=MESH,
+            )
+            for distance in range(1, self.count)
+        ]
+
+
+def plane_semaphores(peers):
+    return [pltpu.SemaphoreType.DMA((2, max(peers.bit_length() - 1, 1), peers))] * 2
+
+
 MESH = pl.DeviceIdType.MESH
 TILE = 256
 
@@ -467,8 +721,9 @@
         self.has_left = self.me > 0
         self.has_right = self.me < count - 1
 
-    def greet(self):
+    def greet(self, plane=None):
         barrier = pltpu.get_barrier_semaphore()
+        extra = 0 if plane is None else plane.greet(barrier)
         for present, shift in ((self.has_left, -1), (self.has_right, 1)):
 
             @pl.when(present)
@@ -481,11 +736,11 @@
 
         @pl.when(inside)
         def _():
-            pl.semaphore_wait(barrier, 2)
+            pl.semaphore_wait(barrier, 2 + extra)
 
         @pl.when(jnp.logical_not(inside))
         def _():
-            pl.semaphore_wait(barrier, 1)
+            pl.semaphore_wait(barrier, 1 + extra)
 
     def copy(self, source, target, sends, receives, at, side):
         return pltpu.make_async_remote_copy(
@@ -544,7 +799,9 @@
                 @pl.when((place > 0) & (place <= hop - 1))
                 def _():
                     self.transfer(side, chunk, hop - 1).wait_recv()
-                    slot[...] = (slot[...].astype(FULL) + self.own(owner, chunk)).astype(slot.dtype)
+                    slot[...] = (slot[...].astype(FULL) + self.own(owner, chunk).astype(FULL)).astype(
+                        slot.dtype
+                    )
 
             @pl.when(place <= hop - 1)
             def _():
@@ -552,7 +809,7 @@
 
     def finish(self, chunk, total):
         line = self.line
-        total[...] = self.own(line.me, chunk)
+        total[...] = self.own(line.me, chunk).astype(FULL)
         last = line.count - 1
         for side in (0, 1):
 
@@ -626,26 +883,34 @@
                     self.transfer(side, chunk, hop).wait_send()
 
 
-def project(line, left, right, parts, rows, forward, block):
-    owner = jnp.where(line.me < line.count // 2, line.count - 1 - block, block)
-    at = pl.ds(pl.multiple_of(owner * rows, 16), rows)
-
-    def tile(index, carry):
-        lanes = pl.ds(pl.multiple_of(index * TILE, TILE), TILE)
-        if forward:
-            parts[at, lanes] = mm(left[at, :], right[:, lanes])
-        else:
-            parts[at, lanes] = mm_nt(left[at, :], right[lanes, :])
-        return carry
-
-    lax.fori_loop(0, parts.shape[1] // TILE, tile, 0)
-
-
-def relay(line, scatter, gather, chunks, lag, work, rows_done):
+def project(line, left, right, parts, rows, forward):
+    upper = line.me < line.count // 2
+    far = jnp.where(upper, line.count - 1, 0) * rows
+    rest = jnp.where(upper, 0, 1) * rows
+
+    def block(start, size):
+        at = pl.ds(pl.multiple_of(start, 16), size)
+
+        def tile(index, carry):
+            lanes = pl.ds(pl.multiple_of(index * TILE, TILE), TILE)
+            if forward:
+                parts[at, lanes] = mm(left[at, :], right[:, lanes]).astype(parts.dtype)
+            else:
+                parts[at, lanes] = mm_nt(left[at, :], right[lanes, : left.shape[1]]).astype(parts.dtype)
+            return carry
+
+        lax.fori_loop(0, parts.shape[1] // TILE, tile, 0)
+
+    return (lambda: block(far, rows)), (lambda: block(rest, (line.count - 1) * rows))
+
+
+def relay(line, scatter, gather, chunks, lag, rows_done, first=None, second=None, events=None, received=None):
     last = line.count - 1
-    work(0)
+    if first is not None:
+        first()
     turns = lag * (chunks - 1) + last + 1 + (0 if gather is None else last)
     for turn in range(turns):
+        arrived = []
         for chunk in range(chunks):
             hop = turn - lag * chunk + 1
             if 1 <= hop <= last:
@@ -656,8 +921,15 @@
                     gather.send(chunk, 1)
             elif gather is not None and last + 1 < hop <= 2 * last + 1:
                 gather.step(chunk, hop - last - 1)
-        if turn == 0:
-            lax.fori_loop(1, line.count, lambda block, carry: (work(block), carry)[1], 0)
+                if hop == 2 * last + 1:
+                    arrived.append(chunk)
+        if turn == 0 and second is not None:
+            second()
+        if events is not None and turn in events:
+            events[turn]()
+        if received is not None:
+            for chunk in arrived:
+                received(chunk)
     for chunk in range(chunks):
         scatter.drain(chunk)
         if gather is not None:
@@ -672,10 +944,22 @@
     return below, jnp.sum(above * plain, 0, keepdims=True)
 
 
-def mix_kernel(count, chunks, lag, rows, left, right, hidden, gain, out, middle, parts, total, slots, s0, s1, s2, s3):
+def ffn_kernel(
+    count, peers, chunks, lag, rows, units,
+    left, right, hidden, gain, cot_rows, local_weight,
+    out, activated, grad_gate, parts, out_parts, middle,
+    weight, slots, total, part_rows, part_cot, part_gate, part_act, own_sem, s0, s1, s2, s3, p0, p1,
+):
     line = Line(count)
     span = rows // chunks
-    line.greet()
+    features = hidden.shape[1]
+    plane = Plane(peers, local_weight, weight, p0, p1)
+    keep_weight = pltpu.make_async_copy(
+        local_weight, weight.at[pl.ds(pl.multiple_of(plane.me * plane.rows, 16), plane.rows), :], own_sem
+    )
+    keep_weight.start()
+    line.greet(plane)
+    plane.start()
     scatter = Scatter(line, parts, rows, span, slots, s0, s1)
     gather = Gather(line, out, rows, span, s2, s3)
 
@@ -687,10 +971,101 @@
         inverse = lax.rsqrt(jnp.mean(value * value, -1, keepdims=True) + EPSILON)
         gather.at(line.me, chunk)[...] = (value * inverse * gain[...]).astype(HALF)
 
-    relay(line, scatter, gather, chunks, lag, functools.partial(project, line, left, right, parts, rows, True), rows_done)
-
-
-def ffn_grad_kernel(count, chunks, lag, rows, left, right, middle, cotangent, gain, out, grad_middle, gain_grad, parts, total, slots, s0, s1, s2, s3):
+    def received(chunk):
+        if chunk == 0:
+            plane.finish()
+            keep_weight.wait()
+        here = [pl.ds(owner * rows + chunk * span, span) for owner in range(count)]
+        there = [slice(owner * span, (owner + 1) * span) for owner in range(count)]
+        for source, target in zip(here, there):
+            part_rows[target, :] = out[source, :]
+            part_cot[target, :] = cot_rows[source, :]
+
+        def gates(index, carry):
+            lanes = pl.ds(pl.multiple_of(index * TILE, TILE), TILE)
+            upper = pl.ds(pl.multiple_of(units + index * TILE, TILE), TILE)
+            lower = pl.ds(pl.multiple_of(2 * units + index * TILE, TILE), TILE)
+            gate = mm(part_rows[...], weight[:, lanes])
+            up = mm(part_rows[...], weight[:, upper])
+            grad_act = mm(part_cot[...], weight[:, lower])
+            sig = sigmoid(gate)
+            silu = gate * sig
+            act = (silu * up).astype(HALF)
+            grad_one = (grad_act * up * (sig * (1.0 + gate * (1.0 - sig)))).astype(HALF)
+            grad_two = (grad_act * silu).astype(HALF)
+            part_gate[:, lanes] = grad_one
+            part_gate[:, upper] = grad_two
+            part_act[:, lanes] = act
+            for source, target in zip(there, here):
+                activated[target, lanes] = act[source, :]
+                grad_gate[target, lanes] = grad_one[source, :]
+                grad_gate[target, upper] = grad_two[source, :]
+            return carry
+
+        lax.fori_loop(0, units // TILE, gates, 0)
+
+        def back(index, carry):
+            lanes = pl.ds(pl.multiple_of(index * TILE, TILE), TILE)
+            result = mm_nt(part_gate[...], weight[lanes, : 2 * units]).astype(parts.dtype)
+            for source, target in zip(there, here):
+                parts[target, lanes] = result[source, :]
+            result = mm_nt(part_act[...], weight[lanes, 2 * units :]).astype(out_parts.dtype)
+            for source, target in zip(there, here):
+                out_parts[target, lanes] = result[source, :]
+            return carry
+
+        lax.fori_loop(0, features // TILE, back, 0)
+
+    last = count - 1
+    events = {}
+    for step in range(1, plane.steps + 1):
+        events[min(2 + 3 * (step - 1), 2 * last - 1 - (plane.steps - step))] = functools.partial(plane.advance, step)
+    first, second = project(line, left, right, parts, rows, True)
+    relay(line, scatter, gather, chunks, lag, rows_done, first, second, events, received)
+    plane.drain()
+
+
+def ffn_rows_call(count, peers, chunks, lag, branches, weight_out, hidden, gain, cot_rows, local_weight):
+    rows, features = hidden.shape
+    length = count * rows
+    units = local_weight.shape[1] // 3
+    span = rows // chunks
+    vmem = pl.BlockSpec(memory_space=pltpu.VMEM)
+    return pl.pallas_call(
+        functools.partial(ffn_kernel, count, peers, chunks, lag, rows, units),
+        in_specs=[vmem] * 5 + [pl.BlockSpec(memory_space=pl.ANY)],
+        out_specs=[vmem] * 6,
+        out_shape=[
+            jax.ShapeDtypeStruct((length, features), HALF),
+            jax.ShapeDtypeStruct((length, units), HALF),
+            jax.ShapeDtypeStruct((length, 2 * units), HALF),
+            jax.ShapeDtypeStruct((length, features), HALF),
+            jax.ShapeDtypeStruct((length, features), HALF),
+            jax.ShapeDtypeStruct((rows, features), FULL),
+        ],
+        scratch_shapes=[
+            pltpu.VMEM((peers * local_weight.shape[0], 3 * units), HALF),
+            pltpu.VMEM((2, chunks, count, span, features), HALF),
+            pltpu.VMEM((span, features), FULL),
+            pltpu.VMEM((count * span, features), HALF),
+            pltpu.VMEM((count * span, features), HALF),
+            pltpu.VMEM((count * span, 2 * units), HALF),
+            pltpu.VMEM((count * span, units), HALF),
+            pltpu.SemaphoreType.DMA(()),
+        ]
+        + [pltpu.SemaphoreType.DMA((2, chunks, count - 1))] * 4
+        + plane_semaphores(peers),
+        name="ffn_rows",
+        cost_estimate=pl.CostEstimate(flops=150_000_000_000, bytes_accessed=40_000_000, transcendentals=0),
+        compiler_params=pltpu.CompilerParams(
+            collective_id=1, has_side_effects=True, vmem_limit_bytes=61 * 2**20
+        ),
+    )(branches, weight_out, hidden, gain, cot_rows, local_weight)
+
+
+def ffn_grad_kernel(
+    count, chunks, lag, rows, parts, middle, cotangent, gain, out, grad_middle, gain_grad, total, slots, s0, s1, s2, s3
+):
     line = Line(count)
     span = rows // chunks
     line.greet()
@@ -707,116 +1082,203 @@
         grad_middle[at, :] = result
         gather.at(line.me, chunk)[...] = result.astype(HALF)
 
-    relay(line, scatter, gather, chunks, lag, functools.partial(project, line, left, right, parts, rows, False), rows_done)
-
-
-def relay_call(kernel, name, count, chunks, lag, collective, operands, rows, features, extra_out, flops):
+    relay(line, scatter, gather, chunks, lag, rows_done)
+
+
+def ffn_grad_rows(count, chunks, lag, parts, middle, cotangent, gain):
+    rows, features = middle.shape
     span = rows // chunks
     vmem = pl.BlockSpec(memory_space=pltpu.VMEM)
-    hops = count - 1
+    operands = (parts, middle, cotangent, gain)
     return pl.pallas_call(
-        functools.partial(kernel, count, chunks, lag, rows),
+        functools.partial(ffn_grad_kernel, count, chunks, lag, rows),
         in_specs=[vmem] * len(operands),
-        out_specs=[vmem] * (1 + len(extra_out)),
-        out_shape=[jax.ShapeDtypeStruct((count * rows, features), HALF)] + extra_out,
+        out_specs=[vmem] * 3,
+        out_shape=[
+            jax.ShapeDtypeStruct((count * rows, features), HALF),
+            jax.ShapeDtypeStruct((rows, features), FULL),
+            jax.ShapeDtypeStruct((1, features), FULL),
+        ],
         scratch_shapes=[
-            pltpu.VMEM((count * rows, features), FULL),
             pltpu.VMEM((span, features), FULL),
             pltpu.VMEM((2, chunks, count, span, features), HALF),
         ]
-        + [pltpu.SemaphoreType.DMA((2, chunks, hops))] * 4,
-        name=name,
-        cost_estimate=pl.CostEstimate(flops=flops, bytes_accessed=20_000_000, transcendentals=0),
+        + [pltpu.SemaphoreType.DMA((2, chunks, count - 1))] * 4,
+        name="ffn_grad_rows",
+        cost_estimate=pl.CostEstimate(flops=100_000_000_000, bytes_accessed=20_000_000, transcendentals=0),
         compiler_params=pltpu.CompilerParams(
-            collective_id=collective, has_side_effects=True, vmem_limit_bytes=56 * 2**20
+            collective_id=2, has_side_effects=True, vmem_limit_bytes=56 * 2**20
         ),
     )(*operands)
 
 
-def mix_rows(count, chunks, lag, branches, weight_out, hidden, gain):
-    rows, features = hidden.shape
-    return relay_call(
-        mix_kernel, "mix_rows", count, chunks, lag, 1, (branches, weight_out, hidden, gain), rows, features,
-        [jax.ShapeDtypeStruct((rows, features), FULL)], 100_000_000_000,
-    )
-
-
-def ffn_grad_rows(count, chunks, lag, grad_gate, weight_up, middle, cotangent, gain):
-    rows, features = middle.shape
-    return relay_call(
-        ffn_grad_kernel, "ffn_grad_rows", count, chunks, lag, 2, (grad_gate, weight_up, middle, cotangent, gain),
-        rows, features,
-        [jax.ShapeDtypeStruct((rows, features), FULL), jax.ShapeDtypeStruct((1, features), FULL)], 100_000_000_000,
-    )
-
-
-def gather_kernel(count, rows, own, out, own_sem, s0, s1):
+def entry_kernel(
+    count, peers, rows, own, gains, query, keyval, mamba, state, step, kv_lanes,
+    out, weight, all_gains, raw, local, held, own_sems, s0, s1, p0, p1, g0, g1,
+):
     line = Line(count)
-    keep = pltpu.make_async_copy(own, out.at[pl.ds(pl.multiple_of(line.me * rows, 16), rows), :], own_sem)
+    swarm = Swarm(peers, count)
+    plane = Plane(peers, local, weight, p0, p1)
+    block = gains.shape[1]
+    keep = pltpu.make_async_copy(own, raw.at[pl.ds(pl.multiple_of(line.me * rows, 16), rows), :], own_sems.at[0])
     keep.start()
-    line.greet()
+    swarm.greet()
     keep.wait()
-    gather = Gather(line, out, rows, rows, s0, s1)
+    gather = Gather(line, raw, rows, rows, s0, s1)
     gather.send(0, 1)
+    sent = swarm.along_dp(lambda device: gains, held, g0, g1)
+    for copy in sent:
+        copy.start()
+    start = 0
+    shared = pl.ds(pl.multiple_of(kv_lanes(line.me), ATT_DIM), ATT_DIM)
+    for part in (query[...], keyval[:, 0, shared], keyval[:, 1, shared], mamba[:, 0, :], mamba[:, 1, :],
+                 state[:, 0, :], state[:, 1, :], step[...]):
+        local[:, start : start + part.shape[1]] = part
+        start += part.shape[1]
+    keep_weight = pltpu.make_async_copy(
+        local, weight.at[pl.ds(pl.multiple_of(plane.me * plane.rows, 16), plane.rows), :], own_sems.at[1]
+    )
+    keep_weight.start()
+    plane.start()
+    held[0] = gains[...]
+    for copy in sent:
+        copy.wait()
+    for offset in range(peers):
+        lanes = pl.ds(pl.multiple_of((swarm.at_dp ^ offset) * block, block), block)
+        all_gains[:, lanes] = held[offset]
+
+    def normed(owner):
+        at = pl.ds(pl.multiple_of(owner * rows, 16), rows)
+        value = raw[at, :].astype(FULL)
+        inverse = lax.rsqrt(jnp.mean(value * value, -1, keepdims=True) + EPSILON)
+        out[at, :] = (value * inverse * all_gains[0:1, :]).astype(HALF)
+
+    normed(line.me)
     for hop in range(1, count):
         gather.step(0, hop)
+        if hop <= plane.steps:
+            plane.advance(hop)
+        for side in (0, 1):
+
+            @pl.when(line.place(side) >= hop)
+            def _():
+                normed(line.ahead(1 - side, hop))
+
+    for extra in range(count, plane.steps + 1):
+        plane.advance(extra)
+    plane.finish()
     gather.drain(0)
-
-
-def line_gather(count, collective, own):
+    plane.drain()
+    keep_weight.wait()
+
+
+def entry(count, peers, own, gains, query, keyval, mamba, state, step, kv_lanes):
     rows, features = own.shape
-    vmem = pl.BlockSpec(memory_space=pltpu.VMEM)
+    block = query.shape[0]
+    total = query.shape[1] + 2 * ATT_DIM + 2 * mamba.shape[2] + 2 * state.shape[2] + step.shape[1]
+    vmem, anywhere = pl.BlockSpec(memory_space=pltpu.VMEM), pl.BlockSpec(memory_space=pl.ANY)
     return pl.pallas_call(
-        functools.partial(gather_kernel, count, rows),
-        in_specs=[vmem],
-        out_specs=vmem,
-        out_shape=jax.ShapeDtypeStruct((count * rows, features), own.dtype),
-        scratch_shapes=[pltpu.SemaphoreType.DMA(())] + [pltpu.SemaphoreType.DMA((2, 1, count - 1))] * 2,
-        name="line_gather",
+        lambda *refs: entry_kernel(count, peers, rows, *refs[:7], kv_lanes, *refs[7:]),
+        in_specs=[vmem] * 7,
+        out_specs=[vmem, anywhere, vmem],
+        out_shape=[
+            jax.ShapeDtypeStruct((count * rows, features), own.dtype),
+            jax.ShapeDtypeStruct((peers * block, total), HALF),
+            jax.ShapeDtypeStruct((gains.shape[0], peers * block), FULL),
+        ],
+        scratch_shapes=[
+            pltpu.VMEM((count * rows, features), HALF),
+            pltpu.VMEM((block, total), HALF),
+            pltpu.VMEM((peers,) + gains.shape, FULL),
+            pltpu.SemaphoreType.DMA((2,)),
+        ]
+        + [pltpu.SemaphoreType.DMA((2, 1, count - 1))] * 2
+        + plane_semaphores(peers)
+        + [pltpu.SemaphoreType.DMA((peers,))] * 2,
+        name="entry",
         cost_estimate=pl.CostEstimate(flops=80_000_000_000, bytes_accessed=20_000_000, transcendentals=0),
         compiler_params=pltpu.CompilerParams(
-            collective_id=collective, has_side_effects=True, vmem_limit_bytes=48 * 2**20
+            collective_id=0, has_side_effects=True, vmem_limit_bytes=48 * 2**20
         ),
-    )(own)
-
-
-def input_grad_kernel(count, chunks, lag, rows, left, right, hidden, grad_middle, gain, out, gain_grad, parts, total, slots, s0, s1):
+    )(own, gains, query, keyval, mamba, state, step)
+
+
+def input_grad_kernel(
+    count, peers, chunks, lag, rows, left, right, hidden, grad_middle, gain, ffn_gain_grad, head_rows,
+    out, gain_out, head_out,
+    parts, total, slots, gain_rows, held_heads, held_dp, held_tensor, gain_sum, s0, s1, h0, h1, d0, d1, t0, t1,
+):
     line = Line(count)
+    swarm = Swarm(peers, count)
     span = rows // chunks
-    line.greet()
+    block = gain_out.shape[1]
+    swarm.greet()
+    heads_sent = swarm.along_dp(lambda device: head_rows, held_heads, h0, h1)
+    for copy in heads_sent:
+        copy.start()
     scatter = Scatter(line, parts, rows, span, slots, s0, s1)
-    gain_grad[...] = jnp.zeros_like(gain_grad)
+    gain_rows[...] = jnp.zeros_like(gain_rows)
+    gain_rows[1:2, :] = ffn_gain_grad[...]
 
     def rows_done(chunk):
         at = pl.ds(chunk * span, span)
         scatter.finish(chunk, total)
         value = hidden[at, :].astype(FULL)
         below, part = norm_below(value, total[...], gain[...])
-        gain_grad[...] += part
+        gain_rows[0:1, :] += part
         out[at, :] = grad_middle[at, :] + below
 
-    relay(line, scatter, None, chunks, lag, functools.partial(project, line, left, right, parts, rows, False), rows_done)
-
-
-def input_grad_rows(count, chunks, lag, grads, weight_in, hidden, grad_middle, gain):
+    first, second = project(line, left, right, parts, rows, False)
+    relay(line, scatter, None, chunks, lag, rows_done, first, second)
+    own_lanes = lambda device: pl.ds(pl.multiple_of(device * block, block), block)
+    gains_sent = swarm.along_dp(lambda device: gain_rows.at[:, own_lanes(device)], held_dp, d0, d1)
+    for copy in gains_sent:
+        copy.start()
+    head_out[...] = head_rows[...]
+    for offset, copy in enumerate(heads_sent):
+        copy.wait()
+        head_out[...] += held_heads[offset + 1]
+    gain_sum[...] = gain_rows[:, own_lanes(swarm.at_dp)]
+    for offset, copy in enumerate(gains_sent):
+        copy.wait()
+        gain_sum[...] += held_dp[offset + 1]
+    last_sent = swarm.along_tensor(gain_sum, held_tensor, t0, t1)
+    for copy in last_sent:
+        copy.start()
+    gain_out[...] = gain_sum[...]
+    for distance, copy in enumerate(last_sent):
+        copy.wait()
+        gain_out[...] += held_tensor[distance + 1]
+
+
+def input_grad_rows(count, peers, chunks, lag, grads, weight_in, hidden, grad_middle, gain, ffn_gain_grad, head_rows):
     rows, features = hidden.shape
     span = rows // chunks
+    block = features // peers
     vmem = pl.BlockSpec(memory_space=pltpu.VMEM)
-    operands = (grads, weight_in, hidden, grad_middle, gain)
+    operands = (grads, weight_in, hidden, grad_middle, gain, ffn_gain_grad, head_rows)
     return pl.pallas_call(
-        functools.partial(input_grad_kernel, count, chunks, lag, rows),
+        functools.partial(input_grad_kernel, count, peers, chunks, lag, rows),
         in_specs=[vmem] * len(operands),
-        out_specs=[vmem] * 2,
+        out_specs=[vmem] * 3,
         out_shape=[
             jax.ShapeDtypeStruct((rows, features), FULL),
-            jax.ShapeDtypeStruct((1, features), FULL),
+            jax.ShapeDtypeStruct((8, block), FULL),
+            jax.ShapeDtypeStruct(head_rows.shape, FULL),
         ],
         scratch_shapes=[
-            pltpu.VMEM((count * rows, features), FULL),
+            pltpu.VMEM((count * rows, features), HALF),
             pltpu.VMEM((span, features), FULL),
             pltpu.VMEM((2, chunks, count, span, features), HALF),
+            pltpu.VMEM((8, features), FULL),
+            pltpu.VMEM((peers,) + head_rows.shape, FULL),
+            pltpu.VMEM((peers, 8, block), FULL),
+            pltpu.VMEM((count, 8, block), FULL),
+            pltpu.VMEM((8, block), FULL),
         ]
-        + [pltpu.SemaphoreType.DMA((2, chunks, count - 1))] * 2,
+        + [pltpu.SemaphoreType.DMA((2, chunks, count - 1))] * 2
+        + [pltpu.SemaphoreType.DMA((peers,))] * 4
+        + [pltpu.SemaphoreType.DMA((count,))] * 2,
         name="input_grad_rows",
         cost_estimate=pl.CostEstimate(flops=80_000_000_000, bytes_accessed=20_000_000, transcendentals=0),
         compiler_params=pltpu.CompilerParams(
@@ -829,27 +1291,8 @@
 LAG = 2
 
 
-def gather_rows(pieces):
-    return lax.all_gather(pieces, "tensor", axis=0, tiled=True)
-
-
 def sum_rows(pieces):
     return lax.psum_scatter(pieces, "tensor", scatter_dimension=0, tiled=True).astype(FULL)
-
-
-def norm_forward(values, gain_vals):
-    inverse = lax.rsqrt(jnp.mean(values * values, -1, keepdims=True) + EPSILON)
-    plain = values * inverse
-    return plain, inverse, plain * gain_vals
-
-
-def silu_parts(gate_input):
-    sigmoid_vals = jax.nn.sigmoid(gate_input)
-    return gate_input * sigmoid_vals, sigmoid_vals * (1.0 + gate_input * (1.0 - sigmoid_vals))
-
-
-def dot_tn(a, b):
-    return jnp.einsum("sa,sb->ab", a, b, preferred_element_type=FULL)
 
 
 def dot_nt(a, b):
@@ -877,7 +1320,7 @@
     cotangent,
 ):
     tensor_index = lax.axis_index("tensor")
-    count = lax.axis_size("tensor")
+    count, peers = lax.axis_size("tensor"), lax.axis_size("dp")
     heads = decay_log.shape[0]
     width = mamba_in.shape[2]
     state_size = state_weight.shape[2]
@@ -890,34 +1333,25 @@
     kv_head = tensor_index * qheads // group_size
     col = Columns(query_width, width, state_size)
 
-    own_keyval = lax.dynamic_slice_in_dim(keyval_weight, kv_head * ATT_DIM, ATT_DIM, 2)
-    spare = LANES - heads - 2
-    packed_in = jnp.concatenate(
-        [
-            query_weight,
-            own_keyval[:, 0],
-            own_keyval[:, 1],
-            mamba_in[:, 0],
-            mamba_in[:, 1],
-            state_weight[:, 0],
-            state_weight[:, 1],
-            step_weight,
-            jnp.zeros((block, spare), HALF),
-            norm_gain[:, None],
-            ffn_gain[:, None],
-        ],
-        1,
-    )
-    weight_in = lax.all_gather(packed_in, "dp", axis=0, tiled=True)
-    hidden_rows = line_gather(count, 0, hidden_in)
+    gains = jnp.pad(jnp.stack([norm_gain, ffn_gain]).astype(FULL), ((0, 6), (0, 0)))
+    step_padded = jnp.pad(step_weight, ((0, 0), (0, 2 * LANES - heads)))
+    sequence, weight_in, gains = entry(
+        count,
+        peers,
+        hidden_in,
+        gains,
+        query_weight,
+        keyval_weight,
+        mamba_in,
+        state_weight,
+        step_padded,
+        lambda place: (place * qheads // group_size) * ATT_DIM,
+    )
+    gain_one, gain_two = gains[0:1], gains[1:2]
     weight_out = lax.all_gather(jnp.concatenate([mamba_out, attn_out], 0), "dp", axis=1, tiled=True)
-    weight_up = lax.all_gather(gate_up.reshape(block, 2 * units), "dp", axis=0, tiled=True)
-    weight_down = lax.all_gather(down_weight, "dp", axis=1, tiled=True)
-    grad_rows = gather_rows(cotangent)
-
-    gain_one = weight_in[:, col.total - 2].astype(FULL)
-    gain_two = weight_in[:, col.total - 1].astype(FULL)
-    sequence = norm_forward(hidden_rows.astype(FULL), gain_one)[2].astype(HALF)
+    local_ffn = jnp.concatenate([gate_up.reshape(block, 2 * units), down_weight.T], 1)
+    sequence, cotangent_late, weight_out = lax.optimization_barrier((sequence, cotangent, weight_out))
+    cot_rows = lax.all_gather(cotangent_late, "tensor", axis=0, tiled=True)
     length = sequence.shape[0]
     packed = jnp.dot(sequence, weight_in, preferred_element_type=FULL)
     head_params = jnp.pad(
@@ -928,37 +1362,27 @@
     scan_y, states, gated_vals, squares = scan_forward(
         col, heads, state_size, packed, segments, head_params
     )
-    square_sum = lax.psum(squares[:, 0], "tensor")
-    gated_inverse = lax.rsqrt(square_sum / (MAMBA_HEADS * HEAD_DIM) + EPSILON)[:, None]
-    attended, lse = attend_forward(col, qheads, packed, tables, segments)
+    attended, lse, squares = attend_forward(col, qheads, count, packed, tables, segments, squares)
+    gated_inverse = lax.rsqrt(squares / (MAMBA_HEADS * HEAD_DIM) + EPSILON).reshape(length, 1)
     gated_scale = gated_gain.astype(FULL)
     gated_plain = gated_vals * gated_inverse
     branches = jnp.concatenate([(gated_plain * gated_scale).astype(HALF), attended], 1)
-    ffn_rows, middle = mix_rows(count, CHUNKS, LAG, branches, weight_out, hidden_in, gain_two[None, :])
-    gate_vals = jnp.dot(ffn_rows, weight_up, preferred_element_type=FULL)
-    gate_part, up_part = gate_vals[:, :units], gate_vals[:, units:]
-    silu_gate, silu_slope = silu_parts(gate_part)
-    activated = (silu_gate * up_part).astype(HALF)
-    grad_act = dot_nt(grad_rows, weight_down)
-    grad_gate = jnp.concatenate(
-        [grad_act * up_part * silu_slope, grad_act * silu_gate], 1
-    ).astype(HALF)
-    up_grad = dot_tn(ffn_rows, grad_gate).astype(HALF)
-    down_grad = dot_tn(activated, grad_rows).astype(HALF)
-    grad_gate, up_grad, down_grad = lax.optimization_barrier((grad_gate, up_grad, down_grad))
-    gate_share = lax.psum_scatter(up_grad, "dp", scatter_dimension=0, tiled=True)
-    down_share = lax.psum_scatter(down_grad, "dp", scatter_dimension=1, tiled=True)
+    ffn_rows, activated, grad_gate, ffn_parts, out_parts, middle = ffn_rows_call(
+        count, peers, CHUNKS, LAG, branches, weight_out, hidden_in, gain_two, cot_rows, local_ffn
+    )
+    ffn_grad = weight_grads(ffn_rows, grad_gate, cot_rows, activated, "ffn_weight_grads")
+    ffn_parts, ffn_grad = lax.optimization_barrier((ffn_parts, ffn_grad))
+    ffn_share = lax.psum_scatter(ffn_grad, "dp", scatter_dimension=0, tiled=True)
     grad_mixed, grad_middle, ffn_gain_part = ffn_grad_rows(
-        count, CHUNKS, LAG, grad_gate, weight_up, middle, cotangent, gain_two[None, :]
-    )
-    ffn_out = sum_rows(jnp.dot(activated, weight_down))
-    hidden_out = (middle + ffn_out).astype(HALF)
-
+        count, CHUNKS, LAG, ffn_parts, middle, cotangent, gain_two
+    )
+    grad_mixed, ffn_share, out_parts = lax.optimization_barrier((grad_mixed, ffn_share, out_parts))
+    ffn_out = sum_rows(out_parts)
     grad_branches = dot_nt(grad_mixed, weight_out)
-    out_grad = dot_tn(branches, grad_mixed).astype(HALF)
-    out_share = lax.psum_scatter(out_grad, "dp", scatter_dimension=1, tiled=True)
-    grad_mamba = grad_branches[:, :width]
-    product_sum = lax.psum(jnp.sum(grad_mamba * gated_scale * gated_plain, -1), "tensor")[:, None]
+    product_sum = jnp.sum(grad_branches[:, :width] * gated_scale * gated_plain, -1).reshape(-1, LANES)
+    attention_grads, product_sum = attend_backward(
+        col, qheads, count, packed, attended, lse, grad_branches, tables, segments, product_sum
+    )
     grads, gain_part, skip_part, head_part = scan_backward(
         col,
         heads,
@@ -966,22 +1390,33 @@
         packed,
         scan_y,
         states,
-        grad_mamba,
-        gated_inverse,
+        grad_branches,
+        squares,
         product_sum,
         gated_scale[None, :],
         segments,
         head_params,
-    )
-    grads = attend_backward(
-        col, qheads, packed, attended, lse, grad_branches[:, width:], tables, segments, grads
-    )
-    in_grad = dot_tn(sequence, grads).astype(HALF)
-    grads, in_grad = lax.optimization_barrier((grads, in_grad))
+        attention_grads,
+    )
+    in_grad = weight_grads(sequence, grads, grad_mixed, branches, "in_out_weight_grads")
+    grads, in_grad, ffn_out = lax.optimization_barrier((grads, in_grad, ffn_out))
     in_share = lax.psum_scatter(in_grad, "dp", scatter_dimension=0, tiled=True)
-    hidden_grad, norm_gain_part = input_grad_rows(
-        count, 2, 1, grads, weight_in, hidden_in, grad_middle, gain_one[None, :]
-    )
+    head_sums = jnp.concatenate(
+        [
+            gain_part[0],
+            head_part[0, :heads],
+            head_part[1, :heads],
+            skip_part.reshape(heads, HEAD_DIM).sum(1),
+        ]
+    )
+    head_rows = jnp.pad(head_sums, (0, 8 * LANES - head_sums.shape[0])).reshape(8, LANES)
+    hidden_grad, gain_grads, head_rows = input_grad_rows(
+        count, peers, 2, 1, grads, weight_in, hidden_in, grad_middle, gain_one, ffn_gain_part, head_rows
+    )
+    head_sums = head_rows.reshape(-1)
+    hidden_grad, ffn_out, ffn_share = lax.optimization_barrier((hidden_grad, ffn_out, ffn_share))
+    hidden_out = (middle + ffn_out).astype(HALF)
+    out_share = in_share[:, col.total :].T
 
     keyval_part = jnp.stack(
         [in_share[:, slice(*col.key)], in_share[:, slice(*col.value)]], 1
@@ -995,39 +1430,25 @@
     state_weight_grad = shared[:, : 2 * state_size].reshape(state_weight.shape)
     keyval_weight_grad = shared[:, 2 * state_size :].reshape(keyval_weight.shape)
 
-    gains = lax.psum(jnp.concatenate([norm_gain_part, ffn_gain_part]), ("dp", "tensor"))
-    dp_index = lax.axis_index("dp")
-    gains = lax.dynamic_slice_in_dim(gains, dp_index * block, block, 1)
-    head_sums = lax.psum(
-        jnp.concatenate(
-            [
-                head_part[0, :heads],
-                head_part[1, :heads],
-                skip_part.reshape(heads, HEAD_DIM).sum(1),
-                gain_part[0],
-            ]
-        ),
-        "dp",
-    )
     inner_grad = jnp.stack([in_share[:, slice(*col.gate)], in_share[:, slice(*col.drive)]], 1)
     return (
         hidden_out,
         hidden_grad,
-        gains[0],
+        gain_grads[0],
         inner_grad.astype(FULL),
         in_share[:, col.step[0] : col.step[0] + heads].astype(FULL),
         state_weight_grad,
-        head_sums[:heads],
-        head_sums[heads : 2 * heads],
-        head_sums[2 * heads : 3 * heads],
-        head_sums[3 * heads :],
+        head_sums[width : width + heads],
+        head_sums[width + heads : width + 2 * heads],
+        head_sums[width + 2 * heads : width + 3 * heads],
+        head_sums[:width],
         in_share[:, slice(*col.query)].astype(FULL),
         keyval_weight_grad,
         out_share[:width].astype(FULL),
         out_share[width:].astype(FULL),
-        gains[1],
-        gate_share.reshape(gate_up.shape).astype(FULL),
-        down_share.astype(FULL),
+        gain_grads[1],
+        ffn_share[:, : 2 * units].reshape(gate_up.shape).astype(FULL),
+        ffn_share[:, 2 * units :].T.astype(FULL),
     )
 
 

time: 893 us -> 703 us (0.79)
  blocking collectives: 87.1 us -> 0 us
  matrix products: 108 us -> 26.6 us
  local copies, waits for them, and re-layouts: 44.1 us -> 31.1 us
  waiting for transfers between devices: 74.4 us -> 64.6 us
  Pallas kernels: 529 us -> 538 us
    psum x4 -> x0, blocking collectives: 87.1 us -> none  [the longest x1 38.6 us: body(): lax.psum(jnp.concatenate([norm_gain_part, ffn_gain_part]), ('dp', 'tensor'))]
    dot_general x6 -> x0, matrix products: 67.9 us -> none  [the longest x4 44.1 us: dot_tn(): return jnp.einsum('sa,sb->ab', a, b, preferred_element_type=FULL)]
    reduce_scatter x1, waiting for transfers between devices: 37.3 us -> 2.27 us  [body(): in_share = lax.psum_scatter(in_grad, 'dp', scatter_dimension=0, tiled=True)]
    all_gather x4 -> x1, waiting for transfers between devices: 0.05 us -> 30.9 us  [body(): cot_rows = lax.all_gather(cotangent_late, 'tensor', axis=0, tiled=True)]
    dot_general x2 -> x1, matrix products: 21.2 us -> 7.74 us  [dot_nt(): return jnp.einsum('sb,ab->sa', a, b, preferred_element_type=FULL)]
    pallas_call x6 -> x8, Pallas kernels: 489 us -> 496 us  [the longest x1 141 us: ffn_rows_call(): pl.pallas_call(functools.partial(ffn_kernel, count, peers, chunks, lag, r...]
    unnamed x92 -> x78, local copies, waits for them, and re-layouts: 18 us -> 14.2 us
  transfers between devices with their start and end apart: 11 -> 6, of which waited for: 2 -> 4; matrix products, arithmetic and copies ran while one was open for 13% -> 9% of each run, Pallas kernels for 60% -> 54%
where the time goes in v3:
time: 703 us; the launch traced here: 696 us
  Pallas kernels  538 us (77%)
  waiting for transfers between devices  64.6 us (9%)
  local copies, waits for them, and re-layouts  31.1 us (4%)
  matrix products  26.6 us (4%)
  other arithmetic  20.5 us (3%)
  between operations  15.1 us (2%)
    pallas_call x1, Pallas kernels, ffn_rows_call(): pl.pallas_call(functools.partial(ffn_kernel, count, peers, chunks, lag, r...  141 us
    pallas_call x1, Pallas kernels, ffn_grad_rows(): pl.pallas_call(functools.partial(ffn_grad_kernel, count, chunks, lag, row...  115 us
    pallas_call x1, Pallas kernels, input_grad_rows(): pl.pallas_call(functools.partial(input_grad_kernel, count, peers, chunks,...  95.5 us
    pallas_call x1, Pallas kernels, entry(): pl.pallas_call(lambda *refs: entry_kernel(count, peers, rows, *refs[:7],...  81.4 us
    pallas_call x2, Pallas kernels, weight_grads(): pl.pallas_call(functools.partial(weight_grads_kernel, first), grid=((one...  46.8 us
    all_gather x1, waiting for transfers between devices, body(): cot_rows = lax.all_gather(cotangent_late, 'tensor', axis=0, tiled=True)  30.9 us
    psum x1, waiting for transfers between devices, body(): lax.psum(jnp.concatenate([in_share[:, col.inmap[0]:col.outmap[1]], keyval...  28.1 us
    pallas_call x1, Pallas kernels, scan_backward(): pl.pallas_call(functools.partial(scan_backward_kernel, col, heads, MAMBA_...  25.8 us
  transfers between devices with their start and end apart: 6, of which 4 were waited for; matrix products, arithmetic and copies ran while one was open for 9% of the time, Pallas kernels for 54%

profile of v3, /device:TPU:0, one launch (start us, length us, event | category | flops | bytes accessed | tf_op | source)
XLA Modules:
  0.0 696.1 jit_solution(10393151908037446786)
XLA Ops:
  7.3 2.0 pad_maximum_fusion.2
  9.4 0.7 stack.40
  10.7 0.8 copy.46
  11.5 2.9 fusion.4
  15.4 1.2 pad_maximum_fusion.1.local_weight
  17.7 81.4 %entry.1 = (bf16[1024,2048]{1,0:T(8,128)(2,1)}, bf16[2048,2816]{1,0:T(8,128)(2,1)}, f32[8,2048]{1,0:T(8,128)S(1)}) custom-call(bf16[256,2048]{1,0:T(8,128)(2,1)S(1)} %copy-done.7, f32[8,256]{1,0:T(8,128)S(1)} %fusion.8.refs_1_, bf16[256,256]{1,0:T(8,128)(2,1)S(1)} %copy-done.11, bf16[256,2,256]{2,1,0:T(2,128)(2,1)S(1)} %copy-done.9, ...), custom_call_target="tpu_custom_call" | custom-call | flops 80000000000 | bytes 20000000 | tf_op jit(solution)/shard_map/entry/pallas_call | solution.py:1180
  100.1 18.9 %fusion.14.p_ref = f32[1024,2816]{1,0:T(8,128)} fusion(bf16[1024,2048]{1,0:T(8,128)(2,1)} %get-tuple-element.60.left_one, bf16[2048,2816]{1,0:T(8,128)(2,1)} %get-tuple-element.61.right), kind=kOutput, calls=%fused_computation.52 | convolution fusion | flops 11811160064 | bytes 27262976 | tf_op jit(solution)/shard_map/dot_general | solution.py:1356
  119.0 16.3 %scan_forward.1 = (f32[1024,768]{1,0:T(8,128)S(1)}, bf16[8,256,768]{2,1,0:T(8,128)(2,1)}, f32[1024,768]{1,0:T(8,128)}, f32[8,128]{1,0:T(8,128)S(1)}) custom-call(f32[1024,2816]{1,0:T(8,128)} %fusion.14.p_ref, s32[1024,1]{1,0:T(8,128)S(1)} %copy.47.segc_ref.segb_ref, s32[8,1,128]{2,1,0:T(1,128)S(1)} %bitcast.42, f32[8,128]{1,0:T(8,128)S(1)} %select_maximum_fusion.3.head_ref), custom_call_target="tpu_custom_call" | custom-call | flops 16000000000 | bytes 30000000 | tf_op jit(solution)/shard_map/scan_forward/pallas_call | solution.py:165
  135.2 1.7 copy-done.12
  137.0 7.4 %attend_forward.1 = (bf16[1024,256]{1,0:T(8,128)(2,1)S(1)}, f32[1024,256]{1,0:T(8,128)S(1)}, f32[8,128]{1,0:T(8,128)S(1)}) custom-call(f32[1024,2816]{1,0:T(8,128)} %fusion.14.p_ref, f32[1024,128]{1,0:T(8,128)S(1)} %get-tuple-element.153.cos_ref, f32[1024,128]{1,0:T(8,128)S(1)} %get-tuple-element.154.sin_ref, s32[1024,1]{1,0:T(8,128)S(1)} %copy.47.segc_ref.segb_ref, ...), custom_call_target="tpu_custom_call" | custom-call | flops 6000000000 | bytes 5000000 | tf_op jit(solution)/shard_map/attend_forward/pallas_call | solution.py:424
  145.6 1.6 pad_maximum_fusion.left.right_two
  147.2 30.9 %all-gather.5.cloned.1.call-done.cot_rows.left_two = bf16[1024,2048]{1,0:T(8,128)(2,1)} async-done(((bf16[256,2048]{1,0:T(8,128)(2,1)}), bf16[1024,2048]{1,0:T(8,128)(2,1)}) %all-gather.5.cloned.1.call-update) | async-done | bytes 4194320 | tf_op jit(solution)/shard_map/all_gather | solution.py:1354
  178.1 140.7 %ffn_rows.1 = (bf16[1024,2048]{1,0:T(8,128)(2,1)}, bf16[1024,1024]{1,0:T(8,128)(2,1)}, bf16[1024,2048]{1,0:T(8,128)(2,1)}, bf16[1024,2048]{1,0:T(8,128)(2,1)}, b...) custom-call(bf16[1024,1024]{1,0:T(8,128)(2,1)} %pad_maximum_fusion.left.right_two, ...), custom_call_target="tpu_custom_call" | custom-call | flops 149999992832 | bytes 40000000 | tf_op jit(solution)/shard_map/ffn_rows/pallas_call | solution.py:1034
  318.8 20.0 %ffn_weight_grads.1 = bf16[2048,3072]{1,0:T(8,128)(2,1)} custom-call(bf16[1024,2048]{1,0:T(8,128)(2,1)} %get-tuple-element.73.left_one, bf16[1024,2048]{1,0:T(8,128)(2,1)} %all-gather.5.cloned.1.call-done.cot_rows.left_two, bf16[1024,2048]{1,0:T(8,128)(2,1)} %get-tuple-element.74.right_one, bf16[1024,1024]{1,0:T(8,128)(2,1)} %get-tuple-element.75.right_two), custom_call_target="tpu_custom_call" | custom-call | flops 12884901888 | bytes 40000000 | tf_op jit(solution)/shard_map/ffn_weight_grads/pallas_call | solution.py:549
  338.9 115.0 %ffn_grad_rows.1 = (bf16[1024,2048]{1,0:T(8,128)(2,1)}, f32[256,2048]{1,0:T(8,128)}, f32[1,2048]{1,0:T(1,128)}) custom-call(bf16[1024,2048]{1,0:T(8,128)(2,1)} %get-tuple-element.76.parts, f32[256,2048]{1,0:T(8,128)} %get-tuple-element.69.middle, bf16[256,2048]{1,0:T(8,128)(2,1)} %cotangent.1, f32[1,2048]{1,0:T(1,128)} %get-tuple-element.142.gain), custom_call_target="tpu_custom_call" | custom-call | flops 99999997952 | bytes 20000000 | tf_op jit(solution)/shard_map/ffn_grad_rows/pallas_call | solution.py:1093
  454.7 7.7 %fusion.15.go_ref.gm_ref = f32[1024,1024]{1,0:T(8,128)S(1)} fusion(bf16[1024,2048]{1,0:T(8,128)(2,1)} %get-tuple-element.80.left_two, bf16[1024,2048]{1,0:T(8,128)(2,1)} %all-gather.3.cloned.1.call-done.right), kind=kOutput, calls=%fused_computation.53 | convolution fusion | flops 4294967296 | bytes 12582912 | tf_op jit(solution)/shard_map/sb,ab->sa/dot_general | solution.py:1299
  462.5 0.7 fusion.1
  463.2 1.2 copy-done.16
  464.4 8.7 %attend_backward.1 = (bf16[1024,512]{1,0:T(8,128)(2,1)S(1)}, f32[8,128]{1,0:T(8,128)S(1)}) custom-call(f32[1024,2816]{1,0:T(8,128)} %fusion.14.p_ref, bf16[1024,256]{1,0:T(8,128)(2,1)S(1)} %copy-done.3, f32[1024,256]{1,0:T(8,128)S(1)} %get-tuple-element.81.lse_ref, f32[1024,1024]{1,0:T(8,128)} %copy-done.16, f32[1024,128]{1,0:T(8,128)S(1)} %copy-done.1, ...), custom_call_target="tpu_custom_call" | custom-call | flops 8000000000 | bytes 10000000 | tf_op jit(solution)/shard_map/attend_backward/pallas_call | solution.py:492
  473.2 25.8 %scan_backward.1 = (bf16[1024,2816]{1,0:T(8,128)(2,1)}, f32[1,768]{1,0:T(1,128)S(1)}, f32[1,768]{1,0:T(1,128)S(1)}, f32[8,128]{1,0:T(8,128)S(1)}) custom-call(f32[1024,2816]{1,0:T(8,128)} %fusion.14.p_ref, f32[1024,768]{1,0:T(8,128)S(1)} %copy-done.13, bf16[8,256,768]{2,1,0:T(8,128)(2,1)} %get-tuple-element.71.states_ref, f32[1024,1024]{1,0:T(8,128)} %copy-done.16, ...), custom_call_target="tpu_custom_call" | custom-call | flops 24000000000 | bytes 40000000 | tf_op jit(solution)/shard_map/scan_backward/pallas_call | solution.py:314
  499.0 26.8 %in_out_weight_grads.1 = bf16[2048,3840]{1,0:T(8,128)(2,1)} custom-call(bf16[1024,2048]{1,0:T(8,128)(2,1)} %get-tuple-element.60.left_one, bf16[1024,2048]{1,0:T(8,128)(2,1)} %get-tuple-element.80.left_two, bf16[1024,2816]{1,0:T(8,128)(2,1)} %get-tuple-element.86.right_one.left, bf16[1024,1024]{1,0:T(8,128)(2,1)} %pad_maximum_fusion.left.right_two), custom_call_target="tpu_custom_call" | custom-call | flops 16106127360 | bytes 40000000 | tf_op jit(solution)/shard_map/in_out_weight_grads/pallas_call | solution.py:549
  525.8 3.3 reduce-scatter.6.cloned.1.call-done
  529.0 1.5 convert_element_type.53
  530.8 0.7 fusion.9.head_rows
  531.5 95.5 %input_grad_rows.1 = (f32[256,2048]{1,0:T(8,128)}, f32[8,256]{1,0:T(8,128)}, f32[8,128]{1,0:T(8,128)}) custom-call(bf16[1024,2816]{1,0:T(8,128)(2,1)} %get-tuple-element.86.right_one.left, bf16[2048,2816]{1,0:T(8,128)(2,1)} %get-tuple-element.61.right, bf16[256,2048]{1,0:T(8,128)(2,1)} %hidden.3, f32[256,2048]{1,0:T(8,128)} %get-tuple-element.87.grad_middle, ...), custom_call_target="tpu_custom_call" | custom-call | flops 80000000000 | bytes 20000000 | tf_op jit(solution)/shard_map/input_grad_rows/pallas_call | solution.py:1260
  627.0 1.6 slice_convert_fusion
  628.5 4.2 reshape.84
  632.8 1.1 convert_bitcast_fusion
  633.9 1.3 copy.61
  636.4 1.3 fusion.12
  637.8 2.8 add_convert_fusion
  640.6 2.3 reduce-scatter.8.cloned.1.call-done
  642.8 0.9 slice_bitcast_fusion.4
  644.2 1.0 slice.108
  645.1 0.9 pad_maximum_fusion.5
  646.0 1.1 slice_bitcast_fusion
  647.2 1.2 slice_bitcast_fusion.2
  648.3 0.9 slice_convert_fusion.4
  649.3 2.4 copy.57
  651.7 0.7 copy.58
  652.3 1.1 copy.59
  653.5 0.8 copy.60
  654.4 1.6 slice_convert_fusion.3
  656.0 28.1 %all-reduce.6.cloned.1.call-done = bf16[256,1024]{1,0:T(8,128)(2,1)} async-done(((bf16[256,1024]{1,0:T(8,128)(2,1)}), bf16[256,1024]{1,0:T(8,128)(2,1)}) %all-reduce.6.cloned.1.call-update) | async-done | bytes 524304 | tf_op jit(solution)/shard_map/psum | solution.py:1427
  684.1 1.1 fusion.10
  685.2 1.1 reshape.81
  686.3 1.1 reshape.83
  687.5 1.3 copy.69
  (108 shorter events, 7.6 us)
Async XLA Ops:
  7.2 7.3 %copy-start.4 = (s32[1024]{0:T(1024)S(1)}, s32[1024]{0:T(1024)}, u32[]{:S(2)}) copy-start(s32[1024]{0:T(1024)} %param.19) | copy-start | bytes 12292
  7.2 7.5 %copy-start.28 = (bf16[768]{0:T(1024)(128)(2,1)S(1)}, bf16[768]{0:T(1024)(128)(2,1)}, u32[]{:S(2)}) copy-start(bf16[768]{0:T(1024)(128)(2,1)} %param.27) | copy-start | bytes 4612
  7.2 7.5 %copy-start.23 = (bf16[1024,256]{1,0:T(8,128)(2,1)S(1)}, bf16[1024,256]{1,0:T(8,128)(2,1)}, u32[]{:S(2)}) copy-start(bf16[1024,256]{1,0:T(8,128)(2,1)} %param.34) | copy-start | bytes 1572868
  7.2 7.8 %copy-start.22 = (bf16[256,2,1024]{2,1,0:T(2,128)(2,1)S(1)}, bf16[256,2,1024]{2,1,0:T(2,128)(2,1)}, u32[]{:S(2)}) copy-start(bf16[256,2,1024]{2,1,0:T(2,128)(2,1)} %param.33) | copy-start | bytes 3145732
  7.2 92.5 %all-gather.3.cloned.1.call-start = ((), (), s32[]{:S(2)}) async-start(), calls=%async_computation.3 | async-start | bytes 4718592 | tf_op jit(solution)/shard_map/all_gather | solution.py:1351
  9.3 168.8 %all-gather.5.cloned.1.call-start = ((), (), s32[]{:S(2)}) async-start(), calls=%async_computation.4 | async-start | bytes 5242880 | tf_op jit(solution)/shard_map/all_gather | solution.py:1354
  14.7 130.3 %copy-start.24 = (f32[768]{0:T(1024)}, f32[768]{0:T(1024)S(1)}, u32[]{:S(2)}) copy-start(f32[768]{0:T(1024)S(1)} %convert_element_type.51) | copy-start | bytes 9220
  14.9 1.7 copy-start.17
  14.9 1.7 copy-start.18
  15.0 1.7 copy-start.19
  15.3 1.8 copy-start.31
  15.3 1.8 copy-start.32
  15.3 1.8 copy-start.33
  15.3 2.1 copy-start.7
  15.3 2.3 copy-start.8
  15.3 2.3 copy-start.9
  15.3 2.4 copy-start.10
  15.3 2.4 copy-start.11
  17.0 120.0 %copy-start = (f32[1024,128]{1,0:T(8,128)}, f32[1024,128]{1,0:T(8,128)S(1)}, u32[]{:S(2)}) copy-start(f32[1024,128]{1,0:T(8,128)S(1)} %get-tuple-element.153.cos_ref) | copy-start | bytes 1572868
  99.8 354.2 %reduce-scatter.4.cloned.1.call-start = ((), (), s32[]{:S(2)}) async-start(), calls=%async_computation.5 | async-start | bytes 14155776 | tf_op jit(solution)/shard_map/reduce_scatter | solution.py:1375
  135.2 1.7 copy-start.12
  136.9 8.0 %copy-start.14 = (f32[1024,768]{1,0:T(8,128)S(1)}, f32[1024,768]{1,0:T(8,128)}, u32[]{:S(2)}) copy-start(f32[1024,768]{1,0:T(8,128)} %get-tuple-element.62) | copy-start | bytes 9437188
  144.3 1.3 copy-start.2
  144.3 0.6 copy-start.5
  145.0 0.6 copy-start.26
  338.8 190.2 %reduce-scatter.6.cloned.1.call-start = ((), (), s32[]{:S(2)}) async-start(), calls=%async_computation.6 | async-start | bytes 5242880 | tf_op jit(solution)/shard_map/reduce_scatter | solution.py:1295
  453.9 0.7 copy-start.29
  454.0 188.8 %reduce-scatter.8.cloned.1.call-start = ((), (), s32[]{:S(2)}) async-start(), calls=%async_computation.7 | async-start | bytes 17694720 | tf_op jit(solution)/shard_map/reduce_scatter | solution.py:1403
  454.6 7.8 %copy-start.15 = (f32[1024,768]{1,0:T(8,128)S(1)}, f32[1024,768]{1,0:T(8,128)}, u32[]{:S(2)}) copy-start(f32[1024,768]{1,0:T(8,128)} %get-tuple-element.62) | copy-start | bytes 9437188
  454.6 7.8 %copy-start.25 = (f32[768]{0:T(1024)S(1)}, f32[768]{0:T(1024)}, u32[]{:S(2)}) copy-start(f32[768]{0:T(1024)} %copy-done.24) | copy-start | bytes 9220
  454.6 7.8 %copy-start.27 = (f32[1024]{0:T(1024)S(1)}, f32[1024]{0:T(1024)}, u32[]{:S(2)}) copy-start(f32[1024]{0:T(1024)} %copy-done.26) | copy-start | bytes 12292
  462.4 2.0 copy-start.16
  462.4 2.0 copy-start.1
  462.5 2.0 copy-start.3
  464.4 8.8 %copy-start.6 = (f32[8,128]{1,0:T(8,128)S(1)}, f32[8,128]{1,0:T(8,128)}, u32[]{:S(2)}) copy-start(f32[8,128]{1,0:T(8,128)} %copy-done.5) | copy-start | bytes 12292
  464.4 8.8 %copy-start.13 = (f32[1024,768]{1,0:T(8,128)S(1)}, f32[1024,768]{1,0:T(8,128)}, u32[]{:S(2)}) copy-start(f32[1024,768]{1,0:T(8,128)} %copy-done.12) | copy-start | bytes 9437188
  530.5 153.5 %all-reduce.6.cloned.1.call-start = ((), (), s32[]{:S(2)}) async-start(), calls=%async_computation.8 | async-start | bytes 1048576 | tf_op jit(solution)/shard_map/psum | solution.py:1427
  531.5 95.5 %copy-start.21 = (bf16[256,3072]{1,0:T(8,128)(2,1)S(1)}, bf16[256,3072]{1,0:T(8,128)(2,1)}, u32[]{:S(2)}) copy-start(bf16[256,3072]{1,0:T(8,128)(2,1)} %reduce-scatter.4.cloned.1.call-done) | copy-start | bytes 4718596
  628.5 6.7 copy-start.30
  653.5 34.0 %copy-start.20 = (f32[256,2048]{1,0:T(8,128)S(1)}, f32[256,2048]{1,0:T(8,128)}, u32[]{:S(2)}) copy-start(f32[256,2048]{1,0:T(8,128)} %get-tuple-element.173) | copy-start | bytes 6291460
Sparse Core Ops, SparseCore 0:
  10.5 54.9 all-gather.2
  99.9 78.0 all-gather.4
  339.0 91.2 reduce-scatter.3
  454.1 74.8 reduce-scatter.5
  532.8 110.0 reduce-scatter.7
  646.1 37.8 all-reduce.5

commit v4 on v3

--- a/solution.py
+++ b/solution.py
@@ -529,42 +529,6 @@
     return jnp.concatenate([cosine, cosine], 1), jnp.concatenate([-sine, sine], 1)
 
 
-def weight_grads_kernel(first, left_one, left_two, right_one, right_two, out):
-    index = pl.program_id(0)
-
-    @pl.when(index < first)
-    def _():
-        out[...] = mm_tn(left_one[...], right_one[...]).astype(out.dtype)
-
-    @pl.when(index >= first)
-    def _():
-        out[...] = mm_tn(left_two[...], right_two[...]).astype(out.dtype)
-
-
-def weight_grads(left_one, right_one, left_two, right_two, name):
-    length, features = left_one.shape
-    one, two = right_one.shape[1], right_two.shape[1]
-    tile = max(size for size in (512, 256, 128) if one % size == 0 and two % size == 0)
-    first = one // tile
-    return pl.pallas_call(
-        functools.partial(weight_grads_kernel, first),
-        grid=((one + two) // tile,),
-        in_specs=[
-            pl.BlockSpec((length, features), lambda i: (0, 0)),
-            pl.BlockSpec((length, features), lambda i: (0, 0)),
-            pl.BlockSpec((length, tile), lambda i: (0, jnp.minimum(i, first - 1))),
-            pl.BlockSpec((length, tile), lambda i: (0, jnp.maximum(i - first, 0))),
-        ],
-        out_specs=pl.BlockSpec((features, tile), lambda i: (0, i)),
-        out_shape=jax.ShapeDtypeStruct((features, one + two), HALF),
-        name=name,
-        cost_estimate=pl.CostEstimate(
-            flops=2 * length * features * (one + two), bytes_accessed=40_000_000, transcendentals=0
-        ),
-        compiler_params=pltpu.CompilerParams(vmem_limit_bytes=56 * 2**20),
-    )(left_one, left_two, right_one, right_two)
-
-
 class Plane:
     def __init__(self, peers, source, whole, sends, receives):
         self.peers, self.source, self.whole = peers, source, whole
@@ -712,6 +676,7 @@
 
 MESH = pl.DeviceIdType.MESH
 TILE = 256
+WIDE = 512
 
 
 class Line:
@@ -771,52 +736,43 @@
         self.slots, self.sends, self.receives = slots, sends, receives
 
     def own(self, owner, chunk):
-        return self.parts[pl.ds(pl.multiple_of(owner * self.rows + chunk * self.span, 16), self.span), :]
-
-    def transfer(self, side, chunk, hop):
+        return self.parts.at[pl.ds(pl.multiple_of(owner * self.rows + chunk * self.span, 16), self.span), :]
+
+    def transfer(self, side, chunk, hop, source=None):
+        target = self.slots.at[side, chunk, hop - 1]
         return self.line.copy(
-            self.slots.at[side, chunk, hop - 1],
-            self.slots.at[side, chunk, hop],
-            self.sends,
-            self.receives,
-            (side, chunk, hop - 1),
-            side,
+            target if source is None else source, target, self.sends, self.receives, (side, chunk, hop - 1), side
         )
 
     def hop(self, chunk, hop):
         line = self.line
         for side in (0, 1):
             place = line.place(side)
-            slot = self.slots.at[side, chunk, hop - 1]
             owner = line.ahead(side, line.count - hop)
 
             @pl.when(place == 0)
             def _():
-                slot[...] = self.own(owner, chunk).astype(slot.dtype)
+                self.transfer(side, chunk, hop, self.own(owner, chunk)).start()
 
             if hop > 1:
 
                 @pl.when((place > 0) & (place <= hop - 1))
                 def _():
+                    slot = self.slots.at[side, chunk, hop - 2]
                     self.transfer(side, chunk, hop - 1).wait_recv()
-                    slot[...] = (slot[...].astype(FULL) + self.own(owner, chunk).astype(FULL)).astype(
-                        slot.dtype
-                    )
-
-            @pl.when(place <= hop - 1)
-            def _():
-                self.transfer(side, chunk, hop).start()
+                    slot[...] = (slot[...].astype(FULL) + self.own(owner, chunk)[...].astype(FULL)).astype(slot.dtype)
+                    self.transfer(side, chunk, hop, slot).start()
 
     def finish(self, chunk, total):
         line = self.line
-        total[...] = self.own(line.me, chunk).astype(FULL)
+        total[...] = self.own(line.me, chunk)[...].astype(FULL)
         last = line.count - 1
         for side in (0, 1):
 
             @pl.when(line.last_there(side))
             def _():
                 self.transfer(side, chunk, last).wait_recv()
-                total[...] += self.slots[side, chunk, last].astype(FULL)
+                total[...] += self.slots[side, chunk, last - 1].astype(FULL)
 
     def drain(self, chunk):
         for hop in range(1, self.line.count):
@@ -929,9 +885,11 @@
             events[turn]()
         if received is not None:
             for chunk in arrived:
+                scatter.drain(chunk)
                 received(chunk)
     for chunk in range(chunks):
-        scatter.drain(chunk)
+        if received is None:
+            scatter.drain(chunk)
         if gather is not None:
             gather.drain(chunk)
 
@@ -982,9 +940,9 @@
             part_cot[target, :] = cot_rows[source, :]
 
         def gates(index, carry):
-            lanes = pl.ds(pl.multiple_of(index * TILE, TILE), TILE)
-            upper = pl.ds(pl.multiple_of(units + index * TILE, TILE), TILE)
-            lower = pl.ds(pl.multiple_of(2 * units + index * TILE, TILE), TILE)
+            lanes = pl.ds(pl.multiple_of(index * WIDE, WIDE), WIDE)
+            upper = pl.ds(pl.multiple_of(units + index * WIDE, WIDE), WIDE)
+            lower = pl.ds(pl.multiple_of(2 * units + index * WIDE, WIDE), WIDE)
             gate = mm(part_rows[...], weight[:, lanes])
             up = mm(part_rows[...], weight[:, upper])
             grad_act = mm(part_cot[...], weight[:, lower])
@@ -1002,10 +960,10 @@
                 grad_gate[target, upper] = grad_two[source, :]
             return carry
 
-        lax.fori_loop(0, units // TILE, gates, 0)
+        lax.fori_loop(0, units // WIDE, gates, 0)
 
         def back(index, carry):
-            lanes = pl.ds(pl.multiple_of(index * TILE, TILE), TILE)
+            lanes = pl.ds(pl.multiple_of(index * WIDE, WIDE), WIDE)
             result = mm_nt(part_gate[...], weight[lanes, : 2 * units]).astype(parts.dtype)
             for source, target in zip(there, here):
                 parts[target, lanes] = result[source, :]
@@ -1014,7 +972,7 @@
                 out_parts[target, lanes] = result[source, :]
             return carry
 
-        lax.fori_loop(0, features // TILE, back, 0)
+        lax.fori_loop(0, features // WIDE, back, 0)
 
     last = count - 1
     events = {}
@@ -1045,7 +1003,7 @@
         ],
         scratch_shapes=[
             pltpu.VMEM((peers * local_weight.shape[0], 3 * units), HALF),
-            pltpu.VMEM((2, chunks, count, span, features), HALF),
+            pltpu.VMEM((2, chunks, count - 1, span, features), HALF),
             pltpu.VMEM((span, features), FULL),
             pltpu.VMEM((count * span, features), HALF),
             pltpu.VMEM((count * span, features), HALF),
@@ -1061,55 +1019,6 @@
             collective_id=1, has_side_effects=True, vmem_limit_bytes=61 * 2**20
         ),
     )(branches, weight_out, hidden, gain, cot_rows, local_weight)
-
-
-def ffn_grad_kernel(
-    count, chunks, lag, rows, parts, middle, cotangent, gain, out, grad_middle, gain_grad, total, slots, s0, s1, s2, s3
-):
-    line = Line(count)
-    span = rows // chunks
-    line.greet()
-    scatter = Scatter(line, parts, rows, span, slots, s0, s1)
-    gather = Gather(line, out, rows, span, s2, s3)
-    gain_grad[...] = jnp.zeros_like(gain_grad)
-
-    def rows_done(chunk):
-        at = pl.ds(chunk * span, span)
-        scatter.finish(chunk, total)
-        below, part = norm_below(middle[at, :], total[...], gain[...])
-        gain_grad[...] += part
-        result = cotangent[at, :].astype(FULL) + below
-        grad_middle[at, :] = result
-        gather.at(line.me, chunk)[...] = result.astype(HALF)
-
-    relay(line, scatter, gather, chunks, lag, rows_done)
-
-
-def ffn_grad_rows(count, chunks, lag, parts, middle, cotangent, gain):
-    rows, features = middle.shape
-    span = rows // chunks
-    vmem = pl.BlockSpec(memory_space=pltpu.VMEM)
-    operands = (parts, middle, cotangent, gain)
-    return pl.pallas_call(
-        functools.partial(ffn_grad_kernel, count, chunks, lag, rows),
-        in_specs=[vmem] * len(operands),
-        out_specs=[vmem] * 3,
-        out_shape=[
-            jax.ShapeDtypeStruct((count * rows, features), HALF),
-            jax.ShapeDtypeStruct((rows, features), FULL),
-            jax.ShapeDtypeStruct((1, features), FULL),
-        ],
-        scratch_shapes=[
-            pltpu.VMEM((span, features), FULL),
-            pltpu.VMEM((2, chunks, count, span, features), HALF),
-        ]
-        + [pltpu.SemaphoreType.DMA((2, chunks, count - 1))] * 4,
-        name="ffn_grad_rows",
-        cost_estimate=pl.CostEstimate(flops=100_000_000_000, bytes_accessed=20_000_000, transcendentals=0),
-        compiler_params=pltpu.CompilerParams(
-            collective_id=2, has_side_effects=True, vmem_limit_bytes=56 * 2**20
-        ),
-    )(*operands)
 
 
 def entry_kernel(
@@ -1203,15 +1112,149 @@
     )(own, gains, query, keyval, mamba, state, step)
 
 
-def input_grad_kernel(
-    count, peers, chunks, lag, rows, left, right, hidden, grad_middle, gain, ffn_gain_grad, head_rows,
-    out, gain_out, head_out,
-    parts, total, slots, gain_rows, held_heads, held_dp, held_tensor, gain_sum, s0, s1, h0, h1, d0, d1, t0, t1,
+class Fold:
+    def __init__(self, peers, chunks, product, parts, held, store, sends, receives, early=()):
+        self.me, self.early = lax.axis_index("dp"), list(early)
+        self.peers, self.chunks = peers, chunks
+        self.product, self.parts, self.held, self.store = product, parts, held, store
+        self.sends, self.receives = sends, receives
+        outer = [1 << bit for bit in range(1, peers.bit_length() - 1)]
+        self.orders = [[1] + outer, [1] + outer[::-1]]
+        self.stages = len(outer) + 2
+        self.turns = chunks + 2 * (self.stages - 1)
+
+    def greet(self, barrier):
+        for bit in self.orders[0]:
+            pl.semaphore_signal(
+                barrier, inc=1, device_id={"dp": self.me ^ bit}, device_id_type=MESH
+            )
+        return len(self.orders[0])
+
+    def column(self, chunk):
+        result = chunk
+        table = self.early + [at for at in range(self.chunks) if at not in self.early]
+        for place, at in enumerate(table):
+            if place != at:
+                result = jnp.where(chunk == place, at, result)
+        return result
+
+    def kept(self, order, step):
+        mask = sum(order[:step])
+        return [offset for offset in range(self.peers) if not offset & mask]
+
+    def copies(self, parity, chunk, step):
+        order = self.orders[parity]
+        bit = order[step]
+        mine, next_kept = self.kept(order, step), self.kept(order, step + 1)
+        result = []
+        for offset in mine:
+            if offset & bit:
+                if step == 0:
+                    source = self.parts.at[lax.rem(chunk, 3), self.me ^ offset]
+                else:
+                    source = self.held[step - 1].at[chunk, mine.index(offset)]
+                place = next_kept.index(offset ^ bit)
+                result.append(
+                    pltpu.make_async_remote_copy(
+                        src_ref=source,
+                        dst_ref=self.held[step].at[chunk, place],
+                        send_sem=self.sends[step].at[chunk, place],
+                        recv_sem=self.receives[step].at[chunk, place],
+                        device_id={"dp": self.me ^ bit},
+                        device_id_type=MESH,
+                    )
+                )
+        return result
+
+    def stage(self, number, parity, chunk):
+        order = self.orders[parity]
+        if number == 0:
+            self.product(self.column(chunk), self.parts.at[lax.rem(chunk, 3)])
+        else:
+            step = number - 1
+            copies = self.copies(parity, chunk, step)
+            for copy in copies:
+                copy.wait_recv()
+            mine, left = self.kept(order, step), self.kept(order, step + 1)
+            for place, offset in enumerate(left):
+                if step == 0:
+                    own = self.parts[lax.rem(chunk, 3), self.me ^ offset]
+                else:
+                    own = self.held[step - 1][chunk, mine.index(offset)]
+                value = own.astype(FULL) + self.held[step][chunk, place].astype(FULL)
+                if number == self.stages - 1:
+                    column = self.column(chunk)
+                    for at in range(self.chunks):
+
+                        @pl.when(column == at)
+                        def _():
+                            self.store(at, value)
+
+                else:
+                    self.held[step][chunk, place] = value.astype(HALF)
+            if step == 0:
+                for copy in copies:
+                    copy.wait_send()
+        if number < self.stages - 1:
+            for copy in self.copies(parity, chunk, number):
+                copy.start()
+
+    def run(self, first, last):
+        def pair(index, carry):
+            for odd in (0, 1):
+                turn = 2 * index + odd
+                for number in reversed(range(self.stages)):
+                    chunk = turn - 2 * number
+
+                    @pl.when((chunk >= 0) & (chunk < self.chunks))
+                    def _():
+                        self.stage(number, odd, chunk)
+
+            return carry
+
+        lax.fori_loop(first // 2, last // 2, pair, 0)
+
+    def drain(self):
+        def pair(index, carry):
+            for odd in (0, 1):
+                chunk = 2 * index + odd
+
+                @pl.when(chunk < self.chunks)
+                def _():
+                    for step in range(1, self.stages - 1):
+                        for copy in self.copies(odd, chunk, step):
+                            copy.wait_send()
+
+            return carry
+
+        lax.fori_loop(0, (self.chunks + 1) // 2, pair, 0)
+
+
+def fold_scratch(peers, chunks, rows, width):
+    steps = peers.bit_length() - 1
+    sizes = [peers >> (step + 1) for step in range(steps)]
+    return (
+        [pltpu.VMEM((3, peers, rows, width), HALF)]
+        + [pltpu.VMEM((chunks, size, rows, width), HALF) for size in sizes]
+        + [pltpu.SemaphoreType.DMA((chunks, size)) for size in sizes] * 2
+    )
+
+
+def final_kernel(
+    count, peers, chunks, rows, kv_owner, col, heads, width,
+    left, weight_in, hidden, grad_middle, gain, ffn_gain_grad, head_rows, sequence, grad_mixed, branches,
+    out, gain_out, head_out, query_out, inner_out, step_out, state_out, keyval_out, mamba_out, attn_out,
+    parts, total, slots, gain_rows, held_heads, held_dp, held_tensor, gain_sum, tiles, gathered, fold_parts, *rest,
 ):
+    steps = peers.bit_length() - 1
+    held, fold_sends, fold_receives = rest[:steps], rest[steps : 2 * steps], rest[2 * steps : 3 * steps]
+    s0, s1, h0, h1, d0, d1, t0, t1, tile_sems, a0, a1 = rest[3 * steps :]
     line = Line(count)
     swarm = Swarm(peers, count)
     span = rows // chunks
     block = gain_out.shape[1]
+    first_chunks = left.shape[1] // width
+    fold_chunks = first_chunks + branches.shape[1] // width
     swarm.greet()
     heads_sent = swarm.along_dp(lambda device: head_rows, held_heads, h0, h1)
     for copy in heads_sent:
@@ -1228,61 +1271,287 @@
         gain_rows[0:1, :] += part
         out[at, :] = grad_middle[at, :] + below
 
-    first, second = project(line, left, right, parts, rows, False)
-    relay(line, scatter, None, chunks, lag, rows_done, first, second)
-    own_lanes = lambda device: pl.ds(pl.multiple_of(device * block, block), block)
-    gains_sent = swarm.along_dp(lambda device: gain_rows.at[:, own_lanes(device)], held_dp, d0, d1)
-    for copy in gains_sent:
-        copy.start()
+    upper = line.me < line.count // 2
+    pieces = parts.shape[1] // TILE
+
+    def fetch(index):
+        slot = index % 2
+        return pltpu.make_async_copy(
+            weight_in.at[index * TILE : (index + 1) * TILE, :], tiles.at[slot], tile_sems.at[slot]
+        )
+
+    def project_tile(start, size, index, following):
+        at = pl.ds(pl.multiple_of(start, 16), size)
+        if following is not None:
+            fetch(following).start()
+        fetch(index).wait()
+        parts[at, index * TILE : (index + 1) * TILE] = mm_nt(left[at, :], tiles[index % 2]).astype(parts.dtype)
+
+    def product(column, target):
+        def fill(grad_left, grad_right, index):
+            lanes = pl.ds(pl.multiple_of(index * width, width), width)
+            target[...] = mm_tn(grad_left[...], grad_right[:, lanes]).astype(HALF).reshape(target.shape)
+
+        @pl.when(column < first_chunks)
+        def _():
+            fill(sequence, left, column)
+
+        @pl.when(column >= first_chunks)
+        def _():
+            fill(grad_mixed, branches, column - first_chunks)
+
+    shared = (col.key, col.value, col.inmap, col.outmap)
+    own_rows = pl.ds(pl.multiple_of(line.me * block, block), block)
+
+    def store(at, value):
+        for piece in range(0, width, LANES):
+            begin = at * width + piece
+            part = value[:, piece : piece + LANES]
+            place = 0
+            for start, end in shared:
+                if start <= begin < end:
+                    gathered[own_rows, place + begin - start : place + begin - start + LANES] = part.astype(HALF)
+                place += end - start
+            if begin < col.query[1]:
+                query_out[:, begin : begin + LANES] = part
+            for index, (start, end) in enumerate((col.gate, col.drive)):
+                if start <= begin < end:
+                    inner_out[:, index, begin - start : begin - start + LANES] = part
+            if begin == col.step[0]:
+                step_out[...] = part[:, :heads]
+            if begin >= col.total:
+                turned_part = part.T
+                begin -= col.total
+                if begin < mamba_out.shape[0]:
+                    mamba_out[begin : begin + LANES, :] = turned_part
+                else:
+                    begin -= mamba_out.shape[0]
+                    attn_out[begin : begin + LANES, :] = turned_part
+
+    early = sorted({at for begin, end in shared for at in range(begin // width, (end - 1) // width + 1)})
+    fold = Fold(peers, fold_chunks, product, fold_parts, held, store, fold_sends, fold_receives, early)
+    gather = Gather(line, gathered, block, block, a0, a1)
+    gains = []
+
+    def send_gains():
+        gains.extend(
+            swarm.along_dp(
+                lambda device: gain_rows.at[:, pl.ds(pl.multiple_of(device * block, block), block)], held_dp, d0, d1
+            )
+        )
+        for copy in gains:
+            copy.start()
+
+    far, others = jnp.where(upper, count - 1, 0) * rows, jnp.where(upper, 0, 1) * rows
+    fetch(0).start()
+    for index in range(pieces):
+        project_tile(far, rows, index, (index + 1) % pieces)
+    for chunk in range(chunks):
+        scatter.hop(chunk, 1)
+
+    def project_others(first, last):
+        for index in range(first, last):
+            project_tile(others, (count - 1) * rows, index, index + 1 if index + 1 < pieces else None)
+
+    turns = fold.turns + fold.turns % 2
+    early_done = len(early) + 2 * (fold.stages - 1)
+    early_done += early_done % 2
+    half = pieces // 2
+    line_steps = [functools.partial(project_others, 0, half), functools.partial(project_others, half, pieces)]
+    line_steps += [functools.partial(scatter.hop, chunk, hop) for hop in range(2, count) for chunk in range(chunks)]
+    line_steps += [functools.partial(rows_done, chunk) for chunk in range(chunks)] + [send_gains]
+    early_steps = [lambda: gather.send(0, 1)] + [functools.partial(gather.step, 0, hop) for hop in range(1, count)]
+    for done in range(2, turns + 2, 2):
+        fold.run(done - 2, done)
+        if line_steps:
+            line_steps.pop(0)()
+        if done >= early_done and early_steps and (done - early_done) % 4 == 0:
+            early_steps.pop(0)()
+    for step in line_steps + early_steps:
+        step()
     head_out[...] = head_rows[...]
     for offset, copy in enumerate(heads_sent):
         copy.wait()
         head_out[...] += held_heads[offset + 1]
-    gain_sum[...] = gain_rows[:, own_lanes(swarm.at_dp)]
-    for offset, copy in enumerate(gains_sent):
+    gain_sum[...] = gain_rows[:, pl.ds(pl.multiple_of(swarm.at_dp * block, block), block)]
+    for offset, copy in enumerate(gains):
         copy.wait()
         gain_sum[...] += held_dp[offset + 1]
     last_sent = swarm.along_tensor(gain_sum, held_tensor, t0, t1)
     for copy in last_sent:
         copy.start()
+    pair = 2 * ATT_DIM
+    state = (gathered.shape[1] - pair) // 2
+    for part in range(2):
+        lanes = slice(pair + part * state, pair + (part + 1) * state)
+        whole = gathered[0:block, lanes].astype(FULL)
+        for owner in range(1, count):
+            whole = whole + gathered[owner * block : (owner + 1) * block, lanes].astype(FULL)
+        state_out[:, part, :] = whole
+    for head in range(KV_HEADS):
+        for part in range(2):
+            lanes = slice(part * ATT_DIM, (part + 1) * ATT_DIM)
+            value = jnp.zeros((block, ATT_DIM), FULL)
+            for owner in range(count):
+                if kv_owner(owner) == head:
+                    value = value + gathered[owner * block : (owner + 1) * block, lanes].astype(FULL)
+            keyval_out[:, part, head * ATT_DIM : (head + 1) * ATT_DIM] = value
     gain_out[...] = gain_sum[...]
     for distance, copy in enumerate(last_sent):
         copy.wait()
         gain_out[...] += held_tensor[distance + 1]
-
-
-def input_grad_rows(count, peers, chunks, lag, grads, weight_in, hidden, grad_middle, gain, ffn_gain_grad, head_rows):
+    for chunk in range(chunks):
+        scatter.drain(chunk)
+    gather.drain(0)
+    fold.drain()
+
+
+def final_rows(
+    count, peers, chunks, kv_owner, col, heads, width, grads, weight_in, hidden, grad_middle, gain, ffn_gain_grad,
+    head_rows, sequence, grad_mixed, branches,
+):
     rows, features = hidden.shape
     span = rows // chunks
     block = features // peers
+    one, two = grads.shape[1], branches.shape[1]
+    tile = 256 if one % 256 == 0 and two % 256 == 0 else 128
+    fold_chunks = (one + two) // tile
     vmem = pl.BlockSpec(memory_space=pltpu.VMEM)
-    operands = (grads, weight_in, hidden, grad_middle, gain, ffn_gain_grad, head_rows)
+    state = col.inmap[1] - col.inmap[0]
+    operands = (
+        grads, weight_in, hidden, grad_middle, gain, ffn_gain_grad, head_rows, sequence, grad_mixed, branches
+    )
+    outputs = [
+        (rows, features),
+        (8, block),
+        head_rows.shape,
+        (block, col.query[1]),
+        (block, 2, width),
+        (block, heads),
+        (block, 2, state),
+        (block, 2, KV_HEADS * ATT_DIM),
+        (width, block),
+        (two - width, block),
+    ]
     return pl.pallas_call(
-        functools.partial(input_grad_kernel, count, peers, chunks, lag, rows),
-        in_specs=[vmem] * len(operands),
-        out_specs=[vmem] * 3,
-        out_shape=[
-            jax.ShapeDtypeStruct((rows, features), FULL),
-            jax.ShapeDtypeStruct((8, block), FULL),
-            jax.ShapeDtypeStruct(head_rows.shape, FULL),
-        ],
+        functools.partial(final_kernel, count, peers, chunks, rows, kv_owner, col, heads, tile),
+        in_specs=[vmem, pl.BlockSpec(memory_space=pl.ANY)] + [vmem] * (len(operands) - 2),
+        out_specs=[vmem] * len(outputs),
+        out_shape=[jax.ShapeDtypeStruct(shape, FULL) for shape in outputs],
         scratch_shapes=[
             pltpu.VMEM((count * rows, features), HALF),
             pltpu.VMEM((span, features), FULL),
-            pltpu.VMEM((2, chunks, count, span, features), HALF),
+            pltpu.VMEM((2, chunks, count - 1, span, features), HALF),
             pltpu.VMEM((8, features), FULL),
             pltpu.VMEM((peers,) + head_rows.shape, FULL),
             pltpu.VMEM((peers, 8, block), FULL),
             pltpu.VMEM((count, 8, block), FULL),
             pltpu.VMEM((8, block), FULL),
+            pltpu.VMEM((2, TILE, one), HALF),
+            pltpu.VMEM((count * block, 2 * (ATT_DIM + state)), HALF),
         ]
+        + fold_scratch(peers, fold_chunks, block, tile)
         + [pltpu.SemaphoreType.DMA((2, chunks, count - 1))] * 2
         + [pltpu.SemaphoreType.DMA((peers,))] * 4
-        + [pltpu.SemaphoreType.DMA((count,))] * 2,
-        name="input_grad_rows",
+        + [pltpu.SemaphoreType.DMA((count,))] * 2
+        + [pltpu.SemaphoreType.DMA((2,))]
+        + [pltpu.SemaphoreType.DMA((2, 1, count - 1))] * 2,
+        name="final_rows",
         cost_estimate=pl.CostEstimate(flops=80_000_000_000, bytes_accessed=20_000_000, transcendentals=0),
         compiler_params=pltpu.CompilerParams(
-            collective_id=3, has_side_effects=True, vmem_limit_bytes=56 * 2**20
+            collective_id=3, has_side_effects=True, vmem_limit_bytes=62 * 2**20
+        ),
+    )(*operands)
+
+
+def ffn_grad_kernel(
+    count, peers, chunks, lag, rows, width,
+    parts, middle, cotangent, gain, ffn_rows, grad_gate, cot_rows, activated,
+    out, grad_middle, gain_grad, up_out, down_out,
+    total, slots, fold_parts, *rest,
+):
+    steps = peers.bit_length() - 1
+    held, fold_sends, fold_receives = rest[:steps], rest[steps : 2 * steps], rest[2 * steps : 3 * steps]
+    s0, s1, s2, s3 = rest[3 * steps :]
+    line = Line(count)
+    span = rows // chunks
+    units = activated.shape[1]
+    first_chunks = 2 * units // width
+
+    def product(column, target):
+        def fill(grad_left, grad_right, index):
+            lanes = pl.ds(pl.multiple_of(index * width, width), width)
+            target[...] = mm_tn(grad_left[...], grad_right[:, lanes]).astype(HALF).reshape(target.shape)
+
+        @pl.when(column < first_chunks)
+        def _():
+            fill(ffn_rows, grad_gate, column)
+
+        @pl.when(column >= first_chunks)
+        def _():
+            fill(cot_rows, activated, column - first_chunks)
+
+    def store(at, value):
+        begin = at * width
+        if begin < 2 * units:
+            up_out[:, begin // units, begin % units : begin % units + width] = value
+        else:
+            down_out[begin - 2 * units : begin - 2 * units + width, :] = value.T
+
+    fold = Fold(peers, 3 * units // width, product, fold_parts, held, store, fold_sends, fold_receives)
+    line.greet(fold)
+    scatter = Scatter(line, parts, rows, span, slots, s0, s1)
+    gather = Gather(line, out, rows, span, s2, s3)
+    gain_grad[...] = jnp.zeros_like(gain_grad)
+
+    def rows_done(chunk):
+        at = pl.ds(chunk * span, span)
+        scatter.finish(chunk, total)
+        below, part = norm_below(middle[at, :], total[...], gain[...])
+        gain_grad[...] += part
+        result = cotangent[at, :].astype(FULL) + below
+        grad_middle[at, :] = result
+        gather.at(line.me, chunk)[...] = result.astype(HALF)
+
+    turns = lag * (chunks - 1) + 2 * (count - 1) + 1
+    pairs = (fold.turns + 1) // 2
+    ends = [min(pairs, -(-pairs * (turn + 1) // (turns - 2))) for turn in range(turns)]
+    events = {
+        turn: functools.partial(fold.run, 2 * (ends[turn - 1] if turn else 0), 2 * ends[turn]) for turn in range(turns)
+    }
+    relay(line, scatter, gather, chunks, lag, rows_done, events=events)
+    fold.drain()
+
+
+def ffn_grad_rows(count, peers, chunks, lag, parts, middle, cotangent, gain, ffn_rows, grad_gate, cot_rows, activated):
+    rows, features = middle.shape
+    span = rows // chunks
+    block = features // peers
+    units = activated.shape[1]
+    width = 256
+    vmem = pl.BlockSpec(memory_space=pltpu.VMEM)
+    operands = (parts, middle, cotangent, gain, ffn_rows, grad_gate, cot_rows, activated)
+    return pl.pallas_call(
+        functools.partial(ffn_grad_kernel, count, peers, chunks, lag, rows, width),
+        in_specs=[vmem] * len(operands),
+        out_specs=[vmem] * 5,
+        out_shape=[
+            jax.ShapeDtypeStruct((count * rows, features), HALF),
+            jax.ShapeDtypeStruct((rows, features), FULL),
+            jax.ShapeDtypeStruct((1, features), FULL),
+            jax.ShapeDtypeStruct((block, 2, units), FULL),
+            jax.ShapeDtypeStruct((units, block), FULL),
+        ],
+        scratch_shapes=[
+            pltpu.VMEM((span, features), FULL),
+            pltpu.VMEM((2, chunks, count - 1, span, features), HALF),
+        ]
+        + fold_scratch(peers, 3 * units // width, block, width)
+        + [pltpu.SemaphoreType.DMA((2, chunks, count - 1))] * 4,
+        name="ffn_grad_rows",
+        cost_estimate=pl.CostEstimate(flops=100_000_000_000, bytes_accessed=20_000_000, transcendentals=0),
+        compiler_params=pltpu.CompilerParams(
+            collective_id=2, has_side_effects=True, vmem_limit_bytes=62 * 2**20
         ),
     )(*operands)
 
@@ -1370,13 +1639,10 @@
     ffn_rows, activated, grad_gate, ffn_parts, out_parts, middle = ffn_rows_call(
         count, peers, CHUNKS, LAG, branches, weight_out, hidden_in, gain_two, cot_rows, local_ffn
     )
-    ffn_grad = weight_grads(ffn_rows, grad_gate, cot_rows, activated, "ffn_weight_grads")
-    ffn_parts, ffn_grad = lax.optimization_barrier((ffn_parts, ffn_grad))
-    ffn_share = lax.psum_scatter(ffn_grad, "dp", scatter_dimension=0, tiled=True)
-    grad_mixed, grad_middle, ffn_gain_part = ffn_grad_rows(
-        count, CHUNKS, LAG, ffn_parts, middle, cotangent, gain_two
-    )
-    grad_mixed, ffn_share, out_parts = lax.optimization_barrier((grad_mixed, ffn_share, out_parts))
+    grad_mixed, grad_middle, ffn_gain_part, gate_up_grad, down_weight_grad = ffn_grad_rows(
+        count, peers, CHUNKS, LAG, ffn_parts, middle, cotangent, gain_two, ffn_rows, grad_gate, cot_rows, activated
+    )
+    grad_mixed, out_parts = lax.optimization_barrier((grad_mixed, out_parts))
     ffn_out = sum_rows(out_parts)
     grad_branches = dot_nt(grad_mixed, weight_out)
     product_sum = jnp.sum(grad_branches[:, :width] * gated_scale * gated_plain, -1).reshape(-1, LANES)
@@ -1398,9 +1664,6 @@
         head_params,
         attention_grads,
     )
-    in_grad = weight_grads(sequence, grads, grad_mixed, branches, "in_out_weight_grads")
-    grads, in_grad, ffn_out = lax.optimization_barrier((grads, in_grad, ffn_out))
-    in_share = lax.psum_scatter(in_grad, "dp", scatter_dimension=0, tiled=True)
     head_sums = jnp.concatenate(
         [
             gain_part[0],
@@ -1410,45 +1673,56 @@
         ]
     )
     head_rows = jnp.pad(head_sums, (0, 8 * LANES - head_sums.shape[0])).reshape(8, LANES)
-    hidden_grad, gain_grads, head_rows = input_grad_rows(
-        count, peers, 2, 1, grads, weight_in, hidden_in, grad_middle, gain_one, ffn_gain_part, head_rows
+    (
+        hidden_grad,
+        gain_grads,
+        head_rows,
+        query_grad,
+        inner_grad,
+        step_grad,
+        state_grad,
+        keyval_grad,
+        mamba_out_grad,
+        attn_out_grad,
+    ) = final_rows(
+        count,
+        peers,
+        2,
+        lambda place: place * qheads // group_size,
+        col,
+        heads,
+        width,
+        grads,
+        weight_in,
+        hidden_in,
+        grad_middle,
+        gain_one,
+        ffn_gain_part,
+        head_rows,
+        sequence,
+        grad_mixed,
+        branches,
     )
     head_sums = head_rows.reshape(-1)
-    hidden_grad, ffn_out, ffn_share = lax.optimization_barrier((hidden_grad, ffn_out, ffn_share))
     hidden_out = (middle + ffn_out).astype(HALF)
-    out_share = in_share[:, col.total :].T
-
-    keyval_part = jnp.stack(
-        [in_share[:, slice(*col.key)], in_share[:, slice(*col.value)]], 1
-    )
-    keyval_grad = lax.dynamic_update_slice_in_dim(
-        jnp.zeros(keyval_weight.shape, HALF), keyval_part, kv_head * ATT_DIM, 2
-    ).reshape(block, -1)
-    shared = lax.psum(
-        jnp.concatenate([in_share[:, col.inmap[0] : col.outmap[1]], keyval_grad], 1), "tensor"
-    ).astype(FULL)
-    state_weight_grad = shared[:, : 2 * state_size].reshape(state_weight.shape)
-    keyval_weight_grad = shared[:, 2 * state_size :].reshape(keyval_weight.shape)
-
-    inner_grad = jnp.stack([in_share[:, slice(*col.gate)], in_share[:, slice(*col.drive)]], 1)
     return (
         hidden_out,
         hidden_grad,
         gain_grads[0],
-        inner_grad.astype(FULL),
-        in_share[:, col.step[0] : col.step[0] + heads].astype(FULL),
-        state_weight_grad,
+        inner_grad,
+        step_grad,
+        state_grad,
         head_sums[width : width + heads],
         head_sums[width + heads : width + 2 * heads],
         head_sums[width + 2 * heads : width + 3 * heads],
         head_sums[:width],
-        in_share[:, slice(*col.query)].astype(FULL),
-        keyval_weight_grad,
-        out_share[:width].astype(FULL),
-        out_share[width:].astype(FULL),
+        query_grad,
+        keyval_grad,
+        mamba_out_grad,
+        attn_out_grad,
         gain_grads[1],
-        ffn_share[:, : 2 * units].reshape(gate_up.shape).astype(FULL),
-        ffn_share[:, 2 * units :].T.astype(FULL),
+        gate_up_grad,
+        down_weight_grad,
     )
 
 

time: 703 us -> 663 us (0.943)
  waiting for transfers between devices: 64.6 us -> 31.1 us
    psum x1 -> x0, waiting for transfers between devices: 28.1 us -> none  [body(): lax.psum(jnp.concatenate([in_share[:, col.inmap[0]:col.outmap[1]], keyval...]
    unnamed x78 -> x95, local copies, waits for them, and re-layouts: 14.2 us -> 20.4 us
    pallas_call x4 -> x2, Pallas kernels: 257 us -> 262 us  [the longest x1 137 us: final_rows(): pl.pallas_call(functools.partial(final_kernel, count, peers, chunks, rows...]
  transfers between devices with their start and end apart: 6 -> 3, of which waited for: 4 -> 1; matrix products, arithmetic and copies ran while one was open for 9% -> 6% of each run, Pallas kernels for 54% -> 42%
where the time goes in v4:
time: 663 us; the launch traced here: 656 us
  Pallas kernels  539 us (81%)
  waiting for transfers between devices  31.1 us (5%)
  local copies, waits for them, and re-layouts  28 us (4%)
  matrix products  26.5 us (4%)
  other arithmetic  16.4 us (2%)
  between operations  14.6 us (2%)
    pallas_call x1, Pallas kernels, ffn_rows_call(): pl.pallas_call(functools.partial(ffn_kernel, count, peers, chunks, lag, r...  138 us
    pallas_call x1, Pallas kernels, final_rows(): pl.pallas_call(functools.partial(final_kernel, count, peers, chunks, rows...  137 us
    pallas_call x1, Pallas kernels, ffn_grad_rows(): pl.pallas_call(functools.partial(ffn_grad_kernel, count, peers, chunks, l...  124 us
    pallas_call x1, Pallas kernels, entry(): pl.pallas_call(lambda *refs: entry_kernel(count, peers, rows, *refs[:7],...  81.4 us
    all_gather x1, waiting for transfers between devices, body(): cot_rows = lax.all_gather(cotangent_late, 'tensor', axis=0, tiled=True)  31.1 us
    pallas_call x1, Pallas kernels, scan_backward(): pl.pallas_call(functools.partial(scan_backward_kernel, col, heads, MAMBA_...  26.1 us
    unnamed x95, local copies, waits for them, and re-layouts  20.4 us
    dot_general x1, matrix products, body(): packed = jnp.dot(sequence, weight_in, preferred_element_type=FULL)  18.8 us
  transfers between devices with their start and end apart: 3, of which 1 were waited for; matrix products, arithmetic and copies ran while one was open for 6% of the time, Pallas kernels for 42%

profile of v4, /device:TPU:0, one launch (start us, length us, event | category | flops | bytes accessed | tf_op | source)
XLA Modules:
  0.0 655.7 jit_solution(16848111275396861800)
XLA Ops:
  7.2 2.0 pad_maximum_fusion.2
  9.3 0.7 convert_element_type.21
  10.0 0.7 broadcast_in_dim.8.gain_ref
  10.7 0.8 copy.41
  11.5 0.7 stack.21
  12.2 0.7 stack.22
  12.8 0.9 copy.42.segc_ref.segb_ref
  13.8 2.8 fusion.4
  16.6 0.3 copy.53
  16.9 2.0 copy.44
  19.0 2.5 pad_maximum_fusion.1.local_weight
  21.5 1.8 pad_maximum_fusion.3
  23.4 81.4 %entry.1 = (bf16[1024,2048]{1,0:T(8,128)(2,1)}, bf16[2048,2816]{1,0:T(8,128)(2,1)}, f32[8,2048]{1,0:T(8,128)S(1)}) custom-call(bf16[256,2048]{1,0:T(8,128)(2,1)S(1)} %copy-done.14, f32[8,256]{1,0:T(8,128)S(1)} %fusion.8.refs_1_, bf16[256,256]{1,0:T(8,128)(2,1)S(1)} %copy-done.18, bf16[256,2,256]{2,1,0:T(2,128)(2,1)S(1)} %copy-done.16, ...), custom_call_target="tpu_custom_call" | custom-call | flops 80000000000 | bytes 20000000 | tf_op jit(solution)/shard_map/entry/pallas_call | solution.py:1089
  104.9 0.6 fusion.10
  105.8 18.8 %fusion.13.p_ref = f32[1024,2816]{1,0:T(8,128)} fusion(bf16[1024,2048]{1,0:T(8,128)(2,1)} %get-tuple-element.60.sequence, bf16[2048,2816]{1,0:T(8,128)(2,1)} %get-tuple-element.61.weight_in), kind=kOutput, calls=%fused_computation.36 | convolution fusion | flops 11811160064 | bytes 27262976 | tf_op jit(solution)/shard_map/dot_general | solution.py:1625
  124.6 16.3 %scan_forward.1 = (f32[1024,768]{1,0:T(8,128)S(1)}, bf16[8,256,768]{2,1,0:T(8,128)(2,1)}, f32[1024,768]{1,0:T(8,128)}, f32[8,128]{1,0:T(8,128)S(1)}) custom-call(f32[1024,2816]{1,0:T(8,128)} %fusion.13.p_ref, s32[1024,1]{1,0:T(8,128)S(1)} %copy.42.segc_ref.segb_ref, s32[8,1,128]{2,1,0:T(1,128)S(1)} %bitcast.28, f32[8,128]{1,0:T(8,128)S(1)} %select_maximum_fusion.3.head_ref), custom_call_target="tpu_custom_call" | custom-call | flops 16000000000 | bytes 30000000 | tf_op jit(solution)/shard_map/scan_forward/pallas_call | solution.py:165
  140.8 1.6 copy-done.19
  142.5 7.4 %attend_forward.1 = (bf16[1024,256]{1,0:T(8,128)(2,1)S(1)}, f32[1024,256]{1,0:T(8,128)S(1)}, f32[8,128]{1,0:T(8,128)S(1)}) custom-call(f32[1024,2816]{1,0:T(8,128)} %fusion.13.p_ref, f32[1024,128]{1,0:T(8,128)S(1)} %get-tuple-element.147.cos_ref, f32[1024,128]{1,0:T(8,128)S(1)} %get-tuple-element.148.sin_ref, s32[1024,1]{1,0:T(8,128)S(1)} %copy.42.segc_ref.segb_ref, ...), custom_call_target="tpu_custom_call" | custom-call | flops 6000000000 | bytes 5000000 | tf_op jit(solution)/shard_map/attend_forward/pallas_call | solution.py:424
  149.9 0.6 copy-done.12
  150.5 0.3 multiply_convert_fusion
  150.9 0.3 copy-done.36
  151.1 1.6 pad_maximum_fusion.left.branches
  152.7 31.1 %all-gather.5.cloned.1.call-done.cot_rows = bf16[1024,2048]{1,0:T(8,128)(2,1)} async-done(((bf16[256,2048]{1,0:T(8,128)(2,1)}), bf16[1024,2048]{1,0:T(8,128)(2,1)}) %all-gather.5.cloned.1.call-update) | async-done | bytes 4194320 | tf_op jit(solution)/shard_map/all_gather | solution.py:1623
  183.8 137.8 %ffn_rows.1 = (bf16[1024,2048]{1,0:T(8,128)(2,1)}, bf16[1024,1024]{1,0:T(8,128)(2,1)}, bf16[1024,2048]{1,0:T(8,128)(2,1)}, bf16[1024,2048]{1,0:T(8,128)(2,1)}, b...) custom-call(bf16[1024,1024]{1,0:T(8,128)(2,1)} %pad_maximum_fusion.left.branches, ...), custom_call_target="tpu_custom_call" | custom-call | flops 149999992832 | bytes 40000000 | tf_op jit(solution)/shard_map/ffn_rows/pallas_call | solution.py:992
  321.6 124.1 %ffn_grad_rows.1 = (bf16[1024,2048]{1,0:T(8,128)(2,1)}, f32[256,2048]{1,0:T(8,128)}, f32[1,2048]{1,0:T(1,128)}, f32[256,2,1024]{2,1,0:T(2,128)}, f32[1024,256]{1,0:T(8,128)}) custom-call(bf16[1024,2048]{1,0:T(8,128)(2,1)} %get-tuple-element.70.parts, f32[256,2048]{1,0:T(8,128)} %get-tuple-element.69.middle, bf16[256,2048]{1,0:T(8,128)(2,1)} %cotangent.1, ...), custom_call_target="tpu_custom_call" | custom-call | flops 99999997952 | bytes 20000000 | tf_op jit(solution)/shard_map/ffn_grad_rows/pallas_call | solution.py:1534
  445.8 7.7 %fusion.14.go_ref.gm_ref = f32[1024,1024]{1,0:T(8,128)S(1)} fusion(bf16[1024,2048]{1,0:T(8,128)(2,1)} %get-tuple-element.79.grad_mixed, bf16[1024,2048]{1,0:T(8,128)(2,1)} %all-gather.3.cloned.1.call-done.right), kind=kOutput, calls=%fused_computation.37 | convolution fusion | flops 4294967296 | bytes 12582912 | tf_op jit(solution)/shard_map/sb,ab->sa/dot_general | solution.py:1568
  453.5 1.9 copy-done.23
  455.5 0.7 fusion.1
  456.2 1.0 copy-done.1
  457.7 8.2 %attend_backward.1 = (bf16[1024,512]{1,0:T(8,128)(2,1)S(1)}, f32[8,128]{1,0:T(8,128)S(1)}) custom-call(f32[1024,2816]{1,0:T(8,128)} %fusion.13.p_ref, bf16[1024,256]{1,0:T(8,128)(2,1)S(1)} %copy-done.7, f32[1024,256]{1,0:T(8,128)S(1)} %get-tuple-element.80.lse_ref, f32[1024,1024]{1,0:T(8,128)} %copy-done.23, f32[1024,128]{1,0:T(8,128)S(1)} %copy-done.1, ...), custom_call_target="tpu_custom_call" | custom-call | flops 8000000000 | bytes 10000000 | tf_op jit(solution)/shard_map/attend_backward/pallas_call | solution.py:492
  465.9 26.1 %scan_backward.1 = (bf16[1024,2816]{1,0:T(8,128)(2,1)}, f32[1,768]{1,0:T(1,128)S(1)}, f32[1,768]{1,0:T(1,128)S(1)}, f32[8,128]{1,0:T(8,128)S(1)}) custom-call(f32[1024,2816]{1,0:T(8,128)} %fusion.13.p_ref, f32[1024,768]{1,0:T(8,128)S(1)} %copy-done.20, bf16[8,256,768]{2,1,0:T(8,128)(2,1)} %get-tuple-element.78.states_ref, f32[1024,1024]{1,0:T(8,128)} %copy-done.23, ...), custom_call_target="tpu_custom_call" | custom-call | flops 24000000000 | bytes 40000000 | tf_op jit(solution)/shard_map/scan_backward/pallas_call | solution.py:314
  492.3 0.7 fusion.9.head_rows
  492.9 137.4 %final_rows.1 = (f32[256,2048]{1,0:T(8,128)}, f32[8,256]{1,0:T(8,128)}, f32[8,128]{1,0:T(8,128)}, f32[256,256]{1,0:T(8,128)}, f32[256,2,768]{2,1,0:T(2,128)}, /*...) custom-call(bf16[1024,2816]{1,0:T(8,128)(2,1)} %get-tuple-element.83, ...), custom_call_target="tpu_custom_call" | custom-call | flops 80000000000 | bytes 20000000 | tf_op jit(solution)/shard_map/final_rows/pallas_call | solution.py:1436
  630.4 1.7 copy.51
  632.1 1.4 fusion.12
  633.5 1.3 slice_bitcast_fusion
  634.8 1.3 fusion.11
  636.1 3.1 add_convert_fusion
  639.2 1.3 copy.63
  640.5 0.8 copy-done.26
  641.4 1.1 copy.64
  642.5 0.8 copy.65
  643.3 0.7 copy.66
  644.0 0.8 copy.67
  644.8 0.9 copy.68
  645.7 0.7 copy.69
  646.4 1.3 copy.70
  647.7 1.0 copy.71
  (94 shorter events, 1.3 us)
Async XLA Ops:
  7.2 9.4 %copy-start.27 = (bf16[256,2,1024]{2,1,0:T(2,128)(2,1)S(1)}, bf16[256,2,1024]{2,1,0:T(2,128)(2,1)}, u32[]{:S(2)}) copy-start(bf16[256,2,1024]{2,1,0:T(2,128)(2,1)} %param.33) | copy-start | bytes 3145732
  7.2 98.3 %all-gather.3.cloned.1.call-start = ((), (), s32[]{:S(2)}) async-start(), calls=%async_computation.1 | async-start | bytes 4718592 | tf_op jit(solution)/shard_map/all_gather | solution.py:1620
  9.2 174.6 %all-gather.5.cloned.1.call-start = ((), (), s32[]{:S(2)}) async-start(), calls=%async_computation.2 | async-start | bytes 5242880 | tf_op jit(solution)/shard_map/all_gather | solution.py:1623
  10.0 140.5 %copy-start.34 = (f32[768]{0:T(1024)}, f32[768]{0:T(1024)S(1)}, u32[]{:S(2)}) copy-start(f32[768]{0:T(1024)S(1)} %convert_element_type.21) | copy-start | bytes 9220
  13.7 128.7 %copy-start.4 = (s32[1024,1]{1,0:T(8,128)}, s32[1024,1]{1,0:T(8,128)S(1)}, u32[]{:S(2)}) copy-start(s32[1024,1]{1,0:T(8,128)S(1)} %copy.42.segc_ref.segb_ref) | copy-start | bytes 12292
  16.6 4.9 copy-start.38
  16.6 4.9 copy-start.39
  16.6 4.9 copy-start.40
  18.9 4.4 copy-start.14
  18.9 4.4 copy-start.15
  18.9 4.4 copy-start.16
  18.9 4.4 copy-start.17
  18.9 4.4 copy-start.18
  21.5 103.0 %copy-start.10 = (f32[8,128]{1,0:T(8,128)}, f32[8,128]{1,0:T(8,128)S(1)}, u32[]{:S(2)}) copy-start(f32[8,128]{1,0:T(8,128)S(1)} %select_maximum_fusion.3.head_ref) | copy-start | bytes 12292
  23.4 119.1 %copy-start = (f32[1024,128]{1,0:T(8,128)}, f32[1024,128]{1,0:T(8,128)S(1)}, u32[]{:S(2)}) copy-start(f32[1024,128]{1,0:T(8,128)S(1)} %get-tuple-element.147.cos_ref) | copy-start | bytes 1572868
  23.4 119.1 %copy-start.2 = (f32[1024,128]{1,0:T(8,128)}, f32[1024,128]{1,0:T(8,128)S(1)}, u32[]{:S(2)}) copy-start(f32[1024,128]{1,0:T(8,128)S(1)} %get-tuple-element.148.sin_ref) | copy-start | bytes 1572868
  105.5 530.6 %reduce-scatter.2.cloned.1.call-start = ((), (), s32[]{:S(2)}) async-start(), calls=%async_computation.3 | async-start | bytes 5242880 | tf_op jit(solution)/shard_map/reduce_scatter | solution.py:1564
  105.8 18.8 %copy-start.8 = (s32[1024]{0:T(1024)S(1)}, s32[1024]{0:T(1024)}, u32[]{:S(2)}) copy-start(s32[1024]{0:T(1024)} %param.19) | copy-start | bytes 12292
  140.8 1.6 copy-start.19
  142.5 8.1 %copy-start.21 = (f32[1024,768]{1,0:T(8,128)S(1)}, f32[1024,768]{1,0:T(8,128)}, u32[]{:S(2)}) copy-start(f32[1024,768]{1,0:T(8,128)} %get-tuple-element.62) | copy-start | bytes 9437188
  149.9 1.3 copy-start.6
  149.9 0.6 copy-start.12
  150.5 0.6 copy-start.36
  445.7 9.7 %copy-start.22 = (f32[1024,768]{1,0:T(8,128)S(1)}, f32[1024,768]{1,0:T(8,128)}, u32[]{:S(2)}) copy-start(f32[1024,768]{1,0:T(8,128)} %get-tuple-element.62) | copy-start | bytes 9437188
  445.8 9.7 %copy-start.35 = (f32[768]{0:T(1024)S(1)}, f32[768]{0:T(1024)}, u32[]{:S(2)}) copy-start(f32[768]{0:T(1024)} %copy-done.34) | copy-start | bytes 9220
  445.8 9.7 %copy-start.37 = (f32[1024]{0:T(1024)S(1)}, f32[1024]{0:T(1024)}, u32[]{:S(2)}) copy-start(f32[1024]{0:T(1024)} %copy-done.36) | copy-start | bytes 12292
  453.5 1.9 copy-start.23
  456.2 1.0 copy-start.1
  456.2 1.2 copy-start.3
  456.2 1.3 copy-start.5
  456.2 1.5 copy-start.7
  456.2 1.5 copy-start.9
  457.7 8.2 %copy-start.11 = (f32[8,128]{1,0:T(8,128)S(1)}, f32[8,128]{1,0:T(8,128)}, u32[]{:S(2)}) copy-start(f32[8,128]{1,0:T(8,128)} %copy-done.10) | copy-start | bytes 12292
  457.7 8.2 %copy-start.13 = (f32[8,128]{1,0:T(8,128)S(1)}, f32[8,128]{1,0:T(8,128)}, u32[]{:S(2)}) copy-start(f32[8,128]{1,0:T(8,128)} %copy-done.12) | copy-start | bytes 12292
  457.7 8.2 %copy-start.20 = (f32[1024,768]{1,0:T(8,128)S(1)}, f32[1024,768]{1,0:T(8,128)}, u32[]{:S(2)}) copy-start(f32[1024,768]{1,0:T(8,128)} %copy-done.19) | copy-start | bytes 9437188
  630.4 8.9 %copy-start.25 = (f32[256,2048]{1,0:T(8,128)S(1)}, f32[256,2048]{1,0:T(8,128)}, u32[]{:S(2)}) copy-start(f32[256,2048]{1,0:T(8,128)} %get-tuple-element.167) | copy-start | bytes 6291460
  639.2 2.2 copy-start.26
  639.2 3.3 copy-start.31
  641.4 2.0 copy-start.33
  641.4 2.7 copy-start.30
  641.4 3.5 copy-start.29
  641.4 4.3 copy-start.32
  642.5 3.9 copy-start.24
  644.8 2.9 copy-start.28
Sparse Core Ops, SparseCore 0:
  10.5 52.2 all-gather.2
  105.6 78.1 all-gather.4
  456.4 89.7 reduce-scatter.1

commit v5 on v4

--- a/solution.py
+++ b/solution.py
@@ -520,9 +520,8 @@
     )
 
 
-def rope_tables(length):
+def rope_tables(positions):
     half = ATT_DIM // 2
-    positions = jnp.arange(length, dtype=FULL)
     frequency = ROPE_BASE ** (-jnp.arange(half, dtype=FULL) / half)
     angles = positions[:, None] * frequency[None, :]
     cosine, sine = jnp.cos(angles), jnp.sin(angles)
@@ -676,7 +675,7 @@
 
 MESH = pl.DeviceIdType.MESH
 TILE = 256
-WIDE = 512
+WIDE = 1024
 
 
 class Line:
@@ -929,6 +928,8 @@
         inverse = lax.rsqrt(jnp.mean(value * value, -1, keepdims=True) + EPSILON)
         gather.at(line.me, chunk)[...] = (value * inverse * gain[...]).astype(HALF)
 
+    wide = min(WIDE, units)
+
     def received(chunk):
         if chunk == 0:
             plane.finish()
@@ -940,9 +941,9 @@
             part_cot[target, :] = cot_rows[source, :]
 
         def gates(index, carry):
-            lanes = pl.ds(pl.multiple_of(index * WIDE, WIDE), WIDE)
-            upper = pl.ds(pl.multiple_of(units + index * WIDE, WIDE), WIDE)
-            lower = pl.ds(pl.multiple_of(2 * units + index * WIDE, WIDE), WIDE)
+            lanes = pl.ds(pl.multiple_of(index * wide, wide), wide)
+            upper = pl.ds(pl.multiple_of(units + index * wide, wide), wide)
+            lower = pl.ds(pl.multiple_of(2 * units + index * wide, wide), wide)
             gate = mm(part_rows[...], weight[:, lanes])
             up = mm(part_rows[...], weight[:, upper])
             grad_act = mm(part_cot[...], weight[:, lower])
@@ -960,10 +961,10 @@
                 grad_gate[target, upper] = grad_two[source, :]
             return carry
 
-        lax.fori_loop(0, units // WIDE, gates, 0)
+        lax.fori_loop(0, units // wide, gates, 0)
 
         def back(index, carry):
-            lanes = pl.ds(pl.multiple_of(index * WIDE, WIDE), WIDE)
+            lanes = pl.ds(pl.multiple_of(index * wide, wide), wide)
             result = mm_nt(part_gate[...], weight[lanes, : 2 * units]).astype(parts.dtype)
             for source, target in zip(there, here):
                 parts[target, lanes] = result[source, :]
@@ -972,7 +973,7 @@
                 out_parts[target, lanes] = result[source, :]
             return carry
 
-        lax.fori_loop(0, features // WIDE, back, 0)
+        lax.fori_loop(0, features // wide, back, 0)
 
     last = count - 1
     events = {}
@@ -1131,103 +1132,61 @@
         return len(self.orders[0])
 
     def column(self, chunk):
-        result = chunk
-        table = self.early + [at for at in range(self.chunks) if at not in self.early]
-        for place, at in enumerate(table):
-            if place != at:
-                result = jnp.where(chunk == place, at, result)
-        return result
-
-    def kept(self, order, step):
-        mask = sum(order[:step])
-        return [offset for offset in range(self.peers) if not offset & mask]
-
-    def copies(self, parity, chunk, step):
-        order = self.orders[parity]
-        bit = order[step]
-        mine, next_kept = self.kept(order, step), self.kept(order, step + 1)
-        result = []
-        for offset in mine:
-            if offset & bit:
-                if step == 0:
-                    source = self.parts.at[lax.rem(chunk, 3), self.me ^ offset]
-                else:
-                    source = self.held[step - 1].at[chunk, mine.index(offset)]
-                place = next_kept.index(offset ^ bit)
-                result.append(
-                    pltpu.make_async_remote_copy(
-                        src_ref=source,
-                        dst_ref=self.held[step].at[chunk, place],
-                        send_sem=self.sends[step].at[chunk, place],
-                        recv_sem=self.receives[step].at[chunk, place],
-                        device_id={"dp": self.me ^ bit},
-                        device_id_type=MESH,
-                    )
-                )
-        return result
+        return (self.early + [at for at in range(self.chunks) if at not in self.early])[chunk]
+
+    def place(self, parity, owner):
+        offset = self.me ^ owner
+        return sum(
+            lax.rem(offset // bit, 2) * (self.peers >> (step + 1)) for step, bit in enumerate(self.orders[parity])
+        )
+
+    def level(self, chunk, step, upper):
+        size = self.peers >> (step + 1)
+        at = pl.ds(size if upper else 0, size)
+        if step == 0:
+            return self.parts.at[chunk % 3, at]
+        return self.held[step - 1].at[chunk, at]
+
+    def copy(self, parity, chunk, step):
+        return pltpu.make_async_remote_copy(
+            src_ref=self.level(chunk, step, True),
+            dst_ref=self.held[step].at[chunk],
+            send_sem=self.sends[step].at[chunk],
+            recv_sem=self.receives[step].at[chunk],
+            device_id={"dp": self.me ^ self.orders[parity][step]},
+            device_id_type=MESH,
+        )
 
     def stage(self, number, parity, chunk):
-        order = self.orders[parity]
         if number == 0:
-            self.product(self.column(chunk), self.parts.at[lax.rem(chunk, 3)])
+            self.product(
+                self.column(chunk), self.parts.at[chunk % 3], functools.partial(self.place, parity)
+            )
         else:
             step = number - 1
-            copies = self.copies(parity, chunk, step)
-            for copy in copies:
-                copy.wait_recv()
-            mine, left = self.kept(order, step), self.kept(order, step + 1)
-            for place, offset in enumerate(left):
-                if step == 0:
-                    own = self.parts[lax.rem(chunk, 3), self.me ^ offset]
-                else:
-                    own = self.held[step - 1][chunk, mine.index(offset)]
-                value = own.astype(FULL) + self.held[step][chunk, place].astype(FULL)
-                if number == self.stages - 1:
-                    column = self.column(chunk)
-                    for at in range(self.chunks):
-
-                        @pl.when(column == at)
-                        def _():
-                            self.store(at, value)
-
-                else:
-                    self.held[step][chunk, place] = value.astype(HALF)
+            copy = self.copy(parity, chunk, step)
+            copy.wait_recv()
+            value = self.level(chunk, step, False)[...].astype(FULL) + self.held[step][chunk].astype(FULL)
+            if number == self.stages - 1:
+                self.store(self.column(chunk), value[0])
+            else:
+                self.held[step][chunk] = value.astype(HALF)
             if step == 0:
-                for copy in copies:
-                    copy.wait_send()
+                copy.wait_send()
         if number < self.stages - 1:
-            for copy in self.copies(parity, chunk, number):
-                copy.start()
+            self.copy(parity, chunk, number).start()
 
     def run(self, first, last):
-        def pair(index, carry):
-            for odd in (0, 1):
-                turn = 2 * index + odd
-                for number in reversed(range(self.stages)):
-                    chunk = turn - 2 * number
-
-                    @pl.when((chunk >= 0) & (chunk < self.chunks))
-                    def _():
-                        self.stage(number, odd, chunk)
-
-            return carry
-
-        lax.fori_loop(first // 2, last // 2, pair, 0)
+        for turn in range(first, min(last, self.turns)):
+            for number in reversed(range(self.stages)):
+                chunk = turn - 2 * number
+                if 0 <= chunk < self.chunks:
+                    self.stage(number, chunk % 2, chunk)
 
     def drain(self):
-        def pair(index, carry):
-            for odd in (0, 1):
-                chunk = 2 * index + odd
-
-                @pl.when(chunk < self.chunks)
-                def _():
-                    for step in range(1, self.stages - 1):
-                        for copy in self.copies(odd, chunk, step):
-                            copy.wait_send()
-
-            return carry
-
-        lax.fori_loop(0, (self.chunks + 1) // 2, pair, 0)
+        for chunk in range(self.chunks):
+            for step in range(1, self.stages - 1):
+                self.copy(chunk % 2, chunk, step).wait_send()
 
 
 def fold_scratch(peers, chunks, rows, width):
@@ -1236,7 +1195,7 @@
     return (
         [pltpu.VMEM((3, peers, rows, width), HALF)]
         + [pltpu.VMEM((chunks, size, rows, width), HALF) for size in sizes]
-        + [pltpu.SemaphoreType.DMA((chunks, size)) for size in sizes] * 2
+        + [pltpu.SemaphoreType.DMA((chunks,)) for _ in sizes] * 2
     )
 
 
@@ -1287,17 +1246,17 @@
         fetch(index).wait()
         parts[at, index * TILE : (index + 1) * TILE] = mm_nt(left[at, :], tiles[index % 2]).astype(parts.dtype)
 
-    def product(column, target):
+    def product(column, target, place):
         def fill(grad_left, grad_right, index):
-            lanes = pl.ds(pl.multiple_of(index * width, width), width)
-            target[...] = mm_tn(grad_left[...], grad_right[:, lanes]).astype(HALF).reshape(target.shape)
-
-        @pl.when(column < first_chunks)
-        def _():
+            lanes = slice(index * width, (index + 1) * width)
+            result = mm_tn(grad_left[...], grad_right[:, lanes]).astype(HALF)
+            size = target.shape[1]
+            for owner in range(target.shape[0]):
+                target[place(owner)] = result[owner * size : (owner + 1) * size, :]
+
+        if column < first_chunks:
             fill(sequence, left, column)
-
-        @pl.when(column >= first_chunks)
-        def _():
+        else:
             fill(grad_mixed, branches, column - first_chunks)
 
     shared = (col.key, col.value, col.inmap, col.outmap)
@@ -1353,17 +1312,15 @@
         for index in range(first, last):
             project_tile(others, (count - 1) * rows, index, index + 1 if index + 1 < pieces else None)
 
-    turns = fold.turns + fold.turns % 2
     early_done = len(early) + 2 * (fold.stages - 1)
-    early_done += early_done % 2
     half = pieces // 2
     line_steps = [functools.partial(project_others, 0, half), functools.partial(project_others, half, pieces)]
     line_steps += [functools.partial(scatter.hop, chunk, hop) for hop in range(2, count) for chunk in range(chunks)]
     line_steps += [functools.partial(rows_done, chunk) for chunk in range(chunks)] + [send_gains]
     early_steps = [lambda: gather.send(0, 1)] + [functools.partial(gather.step, 0, hop) for hop in range(1, count)]
-    for done in range(2, turns + 2, 2):
-        fold.run(done - 2, done)
-        if line_steps:
+    for done in range(1, fold.turns + 1):
+        fold.run(done - 1, done)
+        if line_steps and done % 2 == 0:
             line_steps.pop(0)()
         if done >= early_done and early_steps and (done - early_done) % 4 == 0:
             early_steps.pop(0)()
@@ -1478,17 +1435,17 @@
     units = activated.shape[1]
     first_chunks = 2 * units // width
 
-    def product(column, target):
+    def product(column, target, place):
         def fill(grad_left, grad_right, index):
-            lanes = pl.ds(pl.multiple_of(index * width, width), width)
-            target[...] = mm_tn(grad_left[...], grad_right[:, lanes]).astype(HALF).reshape(target.shape)
-
-        @pl.when(column < first_chunks)
-        def _():
+            lanes = slice(index * width, (index + 1) * width)
+            result = mm_tn(grad_left[...], grad_right[:, lanes]).astype(HALF)
+            size = target.shape[1]
+            for owner in range(target.shape[0]):
+                target[place(owner)] = result[owner * size : (owner + 1) * size, :]
+
+        if column < first_chunks:
             fill(ffn_rows, grad_gate, column)
-
-        @pl.when(column >= first_chunks)
-        def _():
+        else:
             fill(cot_rows, activated, column - first_chunks)
 
     def store(at, value):
@@ -1514,10 +1471,9 @@
         gather.at(line.me, chunk)[...] = result.astype(HALF)
 
     turns = lag * (chunks - 1) + 2 * (count - 1) + 1
-    pairs = (fold.turns + 1) // 2
-    ends = [min(pairs, -(-pairs * (turn + 1) // (turns - 2))) for turn in range(turns)]
+    ends = [min(fold.turns, -(-fold.turns * (turn + 1) // (turns - 2))) for turn in range(turns)]
     events = {
-        turn: functools.partial(fold.run, 2 * (ends[turn - 1] if turn else 0), 2 * ends[turn]) for turn in range(turns)
+        turn: functools.partial(fold.run, ends[turn - 1] if turn else 0, ends[turn]) for turn in range(turns)
     }
     relay(line, scatter, gather, chunks, lag, rows_done, events=events)
     fold.drain()
@@ -1618,15 +1574,17 @@
     )
     gain_one, gain_two = gains[0:1], gains[1:2]
     weight_out = lax.all_gather(jnp.concatenate([mamba_out, attn_out], 0), "dp", axis=1, tiled=True)
-    local_ffn = jnp.concatenate([gate_up.reshape(block, 2 * units), down_weight.T], 1)
-    sequence, cotangent_late, weight_out = lax.optimization_barrier((sequence, cotangent, weight_out))
+    sequence, cotangent_late, weight_out, gate_late, down_late, positions = lax.optimization_barrier(
+        (sequence, cotangent, weight_out, gate_up, down_weight, jnp.arange(sequence.shape[0], dtype=FULL))
+    )
     cot_rows = lax.all_gather(cotangent_late, "tensor", axis=0, tiled=True)
+    local_ffn = jnp.concatenate([gate_late.reshape(block, 2 * units), down_late.T], 1)
     length = sequence.shape[0]
     packed = jnp.dot(sequence, weight_in, preferred_element_type=FULL)
     head_params = jnp.pad(
         jnp.stack([decay_log, step_bias, skip_gain]), ((0, 5), (0, LANES - heads))
     )
-    tables = rope_tables(length)
+    tables = rope_tables(positions)
 
     scan_y, states, gated_vals, squares = scan_forward(
         col, heads, state_size, packed, segments, head_params

time: 663 us -> 656 us (0.989)
    unnamed x95 -> x94, local copies, waits for them, and re-layouts: 20.4 us -> 23.4 us
  transfers between devices with their start and end apart: 3 -> 3, of which waited for: 1 -> 1; matrix products, arithmetic and copies ran while one was open for 6% -> 6% of each run, Pallas kernels for 42% -> 43%
where the time goes in v5:
time: 656 us; the launch traced here: 649 us
  Pallas kernels  535 us (82%)
  local copies, waits for them, and re-layouts  32 us (5%)
  waiting for transfers between devices  27.3 us (4%)
  matrix products  26.1 us (4%)
  between operations  14.4 us (2%)
  other arithmetic  13.5 us (2%)
    pallas_call x1, Pallas kernels, final_rows(): pl.pallas_call(functools.partial(final_kernel, count, peers, chunks, rows...  137 us
    pallas_call x1, Pallas kernels, ffn_rows_call(): pl.pallas_call(functools.partial(ffn_kernel, count, peers, chunks, lag, r...  136 us
    pallas_call x1, Pallas kernels, ffn_grad_rows(): pl.pallas_call(functools.partial(ffn_grad_kernel, count, peers, chunks, l...  123 us
    pallas_call x1, Pallas kernels, entry(): pl.pallas_call(lambda *refs: entry_kernel(count, peers, rows, *refs[:7],...  81.4 us
    all_gather x1, waiting for transfers between devices, body(): cot_rows = lax.all_gather(cotangent_late, 'tensor', axis=0, tiled=True)  27.3 us
    pallas_call x1, Pallas kernels, scan_backward(): pl.pallas_call(functools.partial(scan_backward_kernel, col, heads, MAMBA_...  26.1 us
    unnamed x94, local copies, waits for them, and re-layouts  23.4 us
    dot_general x1, matrix products, body(): packed = jnp.dot(sequence, weight_in, preferred_element_type=FULL)  18.4 us
  transfers between devices with their start and end apart: 3, of which 1 were waited for; matrix products, arithmetic and copies ran while one was open for 6% of the time, Pallas kernels for 43%

profile of v5, /device:TPU:0, one launch (start us, length us, event | category | flops | bytes accessed | tf_op | source)
XLA Modules:
  0.0 649.0 jit_solution(5285443172388164751)
XLA Ops:
  7.2 1.9 pad_maximum_fusion.2
  9.2 0.7 convert_element_type.21
  9.9 0.7 broadcast_in_dim.8.gain_ref
  10.6 0.8 copy.41
  11.4 0.7 stack.21
  12.1 0.7 stack.22
  12.7 0.9 copy.42.segc_ref.segb_ref
  13.7 0.8 select_maximum_fusion.3.head_ref
  14.5 1.2 copy-done.14
  15.7 1.1 copy-done.15
  16.9 0.9 copy-done.16
  17.8 0.9 copy-done.17
  18.8 0.9 copy-done.18
  19.7 81.4 %entry.1 = (bf16[1024,2048]{1,0:T(8,128)(2,1)}, bf16[2048,2816]{1,0:T(8,128)(2,1)}, f32[8,2048]{1,0:T(8,128)S(1)}) custom-call(bf16[256,2048]{1,0:T(8,128)(2,1)S(1)} %copy-done.14, f32[8,256]{1,0:T(8,128)S(1)} %fusion.6.refs_1_, bf16[256,256]{1,0:T(8,128)(2,1)S(1)} %copy-done.18, bf16[256,2,256]{2,1,0:T(2,128)(2,1)S(1)} %copy-done.16, ...), custom_call_target="tpu_custom_call" | custom-call | flops 80000000000 | bytes 20000000 | tf_op jit(solution)/shard_map/entry/pallas_call | solution.py:1090
  102.1 1.0 copy.44
  103.3 1.9 fusion.2
  105.6 18.4 %fusion.11.p_ref = f32[1024,2816]{1,0:T(8,128)} fusion(bf16[1024,2048]{1,0:T(8,128)(2,1)S(1)} %copy-done.40, bf16[2048,2816]{1,0:T(8,128)(2,1)} %get-tuple-element.64.weight_in), kind=kOutput, calls=%fused_computation.35 | convolution fusion | flops 11811160064 | bytes 27262976 | tf_op jit(solution)/shard_map/dot_general | solution.py:1583
  124.0 16.3 %scan_forward.1 = (f32[1024,768]{1,0:T(8,128)S(1)}, bf16[8,256,768]{2,1,0:T(8,128)(2,1)}, f32[1024,768]{1,0:T(8,128)}, f32[8,128]{1,0:T(8,128)S(1)}) custom-call(f32[1024,2816]{1,0:T(8,128)} %fusion.11.p_ref, s32[1024,1]{1,0:T(8,128)S(1)} %copy.42.segc_ref.segb_ref, s32[8,1,128]{2,1,0:T(1,128)S(1)} %bitcast.28, f32[8,128]{1,0:T(8,128)S(1)} %select_maximum_fusion.3.head_ref), custom_call_target="tpu_custom_call" | custom-call | flops 16000000000 | bytes 30000000 | tf_op jit(solution)/shard_map/scan_forward/pallas_call | solution.py:165
  140.3 1.7 copy-done.19
  142.0 8.1 %attend_forward.1 = (bf16[1024,256]{1,0:T(8,128)(2,1)S(1)}, f32[1024,256]{1,0:T(8,128)S(1)}, f32[8,128]{1,0:T(8,128)S(1)}) custom-call(f32[1024,2816]{1,0:T(8,128)} %fusion.11.p_ref, f32[1024,128]{1,0:T(8,128)S(1)} %get-tuple-element.153.cos_ref, f32[1024,128]{1,0:T(8,128)S(1)} %get-tuple-element.154.sin_ref, s32[1024,1]{1,0:T(8,128)S(1)} %copy.42.segc_ref.segb_ref, ...), custom_call_target="tpu_custom_call" | custom-call | flops 6000000000 | bytes 5000000 | tf_op jit(solution)/shard_map/attend_forward/pallas_call | solution.py:424
  151.2 1.6 pad_maximum_fusion.left.branches
  152.8 1.3 pad_maximum_fusion.1.local_weight
  154.1 27.3 %all-gather.5.cloned.1.call-done.cot_rows = bf16[1024,2048]{1,0:T(8,128)(2,1)} async-done(((bf16[256,2048]{1,0:T(8,128)(2,1)}), bf16[1024,2048]{1,0:T(8,128)(2,1)}) %all-gather.5.cloned.1.call-update) | async-done | bytes 4194320 | tf_op jit(solution)/shard_map/all_gather | solution.py:1580
  181.3 135.7 %ffn_rows.1 = (bf16[1024,2048]{1,0:T(8,128)(2,1)}, bf16[1024,1024]{1,0:T(8,128)(2,1)}, bf16[1024,2048]{1,0:T(8,128)(2,1)}, bf16[1024,2048]{1,0:T(8,128)(2,1)}, b...) custom-call(bf16[1024,1024]{1,0:T(8,128)(2,1)} %pad_maximum_fusion.left.branches, ...), custom_call_target="tpu_custom_call" | custom-call | flops 149999992832 | bytes 40000000 | tf_op jit(solution)/shard_map/ffn_rows/pallas_call | solution.py:993
  317.0 123.0 %ffn_grad_rows.1 = (bf16[1024,2048]{1,0:T(8,128)(2,1)}, f32[256,2048]{1,0:T(8,128)}, f32[1,2048]{1,0:T(1,128)}, f32[256,2,1024]{2,1,0:T(2,128)}, f32[1024,256]{1,0:T(8,128)}) custom-call(bf16[1024,2048]{1,0:T(8,128)(2,1)} %get-tuple-element.76.parts, f32[256,2048]{1,0:T(8,128)} %get-tuple-element.75.middle, bf16[256,2048]{1,0:T(8,128)(2,1)} %cotangent.1, ...), custom_call_target="tpu_custom_call" | custom-call | flops 99999997952 | bytes 20000000 | tf_op jit(solution)/shard_map/ffn_grad_rows/pallas_call | solution.py:1490
  440.1 7.7 %fusion.12.go_ref.gm_ref = f32[1024,1024]{1,0:T(8,128)S(1)} fusion(bf16[1024,2048]{1,0:T(8,128)(2,1)} %get-tuple-element.85.grad_mixed, bf16[1024,2048]{1,0:T(8,128)(2,1)} %all-gather.3.cloned.1.call-done.right), kind=kOutput, calls=%fused_computation.36 | convolution fusion | flops 4294967296 | bytes 12582912 | tf_op jit(solution)/shard_map/sb,ab->sa/dot_general | solution.py:1524
  447.8 1.9 copy-done.23
  449.8 0.7 fusion.1
  450.5 1.0 copy-done.1
  452.0 8.3 %attend_backward.1 = (bf16[1024,512]{1,0:T(8,128)(2,1)S(1)}, f32[8,128]{1,0:T(8,128)S(1)}) custom-call(f32[1024,2816]{1,0:T(8,128)} %fusion.11.p_ref, bf16[1024,256]{1,0:T(8,128)(2,1)S(1)} %copy-done.7, f32[1024,256]{1,0:T(8,128)S(1)} %get-tuple-element.86.lse_ref, f32[1024,1024]{1,0:T(8,128)} %copy-done.23, f32[1024,128]{1,0:T(8,128)S(1)} %copy-done.1, ...), custom_call_target="tpu_custom_call" | custom-call | flops 8000000000 | bytes 10000000 | tf_op jit(solution)/shard_map/attend_backward/pallas_call | solution.py:492
  460.3 26.1 %scan_backward.1 = (bf16[1024,2816]{1,0:T(8,128)(2,1)}, f32[1,768]{1,0:T(1,128)S(1)}, f32[1,768]{1,0:T(1,128)S(1)}, f32[8,128]{1,0:T(8,128)S(1)}) custom-call(f32[1024,2816]{1,0:T(8,128)} %fusion.11.p_ref, f32[1024,768]{1,0:T(8,128)S(1)} %copy-done.20, bf16[8,256,768]{2,1,0:T(8,128)(2,1)} %get-tuple-element.84.states_ref, f32[1024,1024]{1,0:T(8,128)} %copy-done.23, ...), custom_call_target="tpu_custom_call" | custom-call | flops 24000000000 | bytes 40000000 | tf_op jit(solution)/shard_map/scan_backward/pallas_call | solution.py:314
  486.6 0.7 fusion.7.head_rows
  487.3 136.5 %final_rows.1 = (f32[256,2048]{1,0:T(8,128)}, f32[8,256]{1,0:T(8,128)}, f32[8,128]{1,0:T(8,128)}, f32[256,256]{1,0:T(8,128)}, f32[256,2,768]{2,1,0:T(2,128)}, /*...) custom-call(bf16[1024,2816]{1,0:T(8,128)(2,1)} %get-tuple-element.89, ...), custom_call_target="tpu_custom_call" | custom-call | flops 80000000000 | bytes 20000000 | tf_op jit(solution)/shard_map/final_rows/pallas_call | solution.py:1393
  623.8 1.7 copy.51
  625.6 1.4 fusion.10
  626.9 1.3 slice_bitcast_fusion
  628.2 1.3 fusion.9
  629.5 3.1 add_convert_fusion
  632.7 1.3 copy.63
  634.0 0.8 copy-done.27
  634.8 1.1 copy.64
  636.0 0.8 copy.65
  636.8 0.7 copy.66
  637.5 0.8 copy.67
  638.3 0.9 copy.68
  639.2 0.7 copy.69
  639.9 1.3 copy.70
  641.2 1.0 copy.71
  (95 shorter events, 3.5 us)
Async XLA Ops:
  7.2 94.6 %all-gather.3.cloned.1.call-start = ((), (), s32[]{:S(2)}) async-start(), calls=%async_computation.1 | async-start | bytes 4718592 | tf_op jit(solution)/shard_map/all_gather | solution.py:1576
  9.2 172.2 %all-gather.5.cloned.1.call-start = ((), (), s32[]{:S(2)}) async-start(), calls=%async_computation.2 | async-start | bytes 5242880 | tf_op jit(solution)/shard_map/all_gather | solution.py:1580
  9.9 140.3 %copy-start.36 = (f32[768]{0:T(1024)}, f32[768]{0:T(1024)S(1)}, u32[]{:S(2)}) copy-start(f32[768]{0:T(1024)S(1)} %convert_element_type.21) | copy-start | bytes 9220
  13.7 128.4 %copy-start.4 = (s32[1024,1]{1,0:T(8,128)}, s32[1024,1]{1,0:T(8,128)S(1)}, u32[]{:S(2)}) copy-start(s32[1024,1]{1,0:T(8,128)S(1)} %copy.42.segc_ref.segb_ref) | copy-start | bytes 12292
  14.5 1.2 copy-start.14
  15.7 1.1 copy-start.15
  16.9 0.9 copy-start.16
  17.8 0.9 copy-start.17
  18.8 0.9 copy-start.18
  19.7 104.3 %copy-start.10 = (f32[8,128]{1,0:T(8,128)}, f32[8,128]{1,0:T(8,128)S(1)}, u32[]{:S(2)}) copy-start(f32[8,128]{1,0:T(8,128)S(1)} %select_maximum_fusion.3.head_ref) | copy-start | bytes 12292
  19.7 82.1 %copy-start.28 = (bf16[256,2,1024]{2,1,0:T(2,128)(2,1)S(1)}, bf16[256,2,1024]{2,1,0:T(2,128)(2,1)}, u32[]{:S(2)}) copy-start(bf16[256,2,1024]{2,1,0:T(2,128)(2,1)} %param.33) | copy-start | bytes 3145732
  19.7 82.3 %copy-start.31 = (bf16[1024,256]{1,0:T(8,128)(2,1)S(1)}, bf16[1024,256]{1,0:T(8,128)(2,1)}, u32[]{:S(2)}) copy-start(bf16[1024,256]{1,0:T(8,128)(2,1)} %param.34) | copy-start | bytes 1572868
  103.1 526.5 %reduce-scatter.2.cloned.1.call-start = ((), (), s32[]{:S(2)}) async-start(), calls=%async_computation.3 | async-start | bytes 5242880 | tf_op jit(solution)/shard_map/reduce_scatter | solution.py:1520
  103.3 2.3 copy-start.40
  105.6 36.5 %copy-start = (f32[1024,128]{1,0:T(8,128)}, f32[1024,128]{1,0:T(8,128)S(1)}, u32[]{:S(2)}) copy-start(f32[1024,128]{1,0:T(8,128)S(1)} %get-tuple-element.153.cos_ref) | copy-start | bytes 1572868
  105.6 36.4 %copy-start.2 = (f32[1024,128]{1,0:T(8,128)}, f32[1024,128]{1,0:T(8,128)S(1)}, u32[]{:S(2)}) copy-start(f32[1024,128]{1,0:T(8,128)S(1)} %get-tuple-element.154.sin_ref) | copy-start | bytes 1572868
  105.6 18.4 %copy-start.8 = (s32[1024]{0:T(1024)S(1)}, s32[1024]{0:T(1024)}, u32[]{:S(2)}) copy-start(s32[1024]{0:T(1024)} %param.19) | copy-start | bytes 12292
  140.3 1.7 copy-start.19
  142.0 8.8 %copy-start.21 = (f32[1024,768]{1,0:T(8,128)S(1)}, f32[1024,768]{1,0:T(8,128)}, u32[]{:S(2)}) copy-start(f32[1024,768]{1,0:T(8,128)} %get-tuple-element.65) | copy-start | bytes 9437188
  150.1 2.7 copy-start.6
  150.1 2.7 copy-start.12
  150.1 0.7 copy-start.38
  151.2 1.6 copy-start.26
  440.0 9.7 %copy-start.22 = (f32[1024,768]{1,0:T(8,128)S(1)}, f32[1024,768]{1,0:T(8,128)}, u32[]{:S(2)}) copy-start(f32[1024,768]{1,0:T(8,128)} %get-tuple-element.65) | copy-start | bytes 9437188
  440.0 9.7 %copy-start.37 = (f32[768]{0:T(1024)S(1)}, f32[768]{0:T(1024)}, u32[]{:S(2)}) copy-start(f32[768]{0:T(1024)} %copy-done.36) | copy-start | bytes 9220
  440.1 9.7 %copy-start.39 = (f32[1024]{0:T(1024)S(1)}, f32[1024]{0:T(1024)}, u32[]{:S(2)}) copy-start(f32[1024]{0:T(1024)} %copy-done.38) | copy-start | bytes 12292
  447.8 1.9 copy-start.23
  450.5 1.0 copy-start.1
  450.5 1.2 copy-start.3
  450.5 1.3 copy-start.5
  450.5 1.5 copy-start.7
  450.5 1.5 copy-start.9
  452.0 8.3 %copy-start.11 = (f32[8,128]{1,0:T(8,128)S(1)}, f32[8,128]{1,0:T(8,128)}, u32[]{:S(2)}) copy-start(f32[8,128]{1,0:T(8,128)} %copy-done.10) | copy-start | bytes 12292
  452.0 8.3 %copy-start.13 = (f32[8,128]{1,0:T(8,128)S(1)}, f32[8,128]{1,0:T(8,128)}, u32[]{:S(2)}) copy-start(f32[8,128]{1,0:T(8,128)} %copy-done.12) | copy-start | bytes 12292
  452.0 8.3 %copy-start.20 = (f32[1024,768]{1,0:T(8,128)S(1)}, f32[1024,768]{1,0:T(8,128)}, u32[]{:S(2)}) copy-start(f32[1024,768]{1,0:T(8,128)} %copy-done.19) | copy-start | bytes 9437188
  623.8 8.9 %copy-start.25 = (f32[256,2048]{1,0:T(8,128)S(1)}, f32[256,2048]{1,0:T(8,128)}, u32[]{:S(2)}) copy-start(f32[256,2048]{1,0:T(8,128)} %get-tuple-element.173) | copy-start | bytes 6291460
  632.7 2.2 copy-start.27
  632.7 3.3 copy-start.33
  634.8 2.0 copy-start.35
  634.8 2.7 copy-start.32
  634.8 3.5 copy-start.30
  634.8 4.3 copy-start.34
  636.0 3.9 copy-start.24
  638.3 2.9 copy-start.29
Sparse Core Ops, SparseCore 0:
  10.5 53.7 all-gather.2
  103.2 78.0 all-gather.4
  450.7 90.2 reduce-scatter.1
